TPU v7x, 32 devices: a whole 2x2x4 slice. The times are simulated.
32 devices in a mesh: seq: 8 (over z, x), tensor: 4 (over y, core).
Axes of the slice: x: 2, y: 2, z: 4, core: 2. Of those that a mesh axis runs over, the one named last changes fastest.
Arguments:
- queries: bfloat16 [512, 2048], P('seq', 'tensor'), may hold values from -5 to 5
- draft_keys: bfloat16 [512, 2048], P('seq', 'tensor'), may hold values from -5 to 5
- draft_values: bfloat16 [512, 2048], P('seq', 'tensor'), may hold values from -6 to 6
- key_cache: bfloat16 [96, 128, 2048], P('seq', None, 'tensor'), may hold values from -6 to 6
- value_cache: bfloat16 [96, 128, 2048], P('seq', None, 'tensor'), may hold values from -6 to 6
- page_request: int32 [96], P('seq'), may hold values from 0 to 7, as said below
- page_slot: int32 [96], P('seq'), may hold values from 0 to 88, as said below
- cache_len: int32 [8], replicated, may hold values from 1 to 11384, as said below
- tree_mask: int32 [8, 64, 64], P('seq'), may hold values from 0 to 1, as said below
- accepted: int32 [8, 8], P('seq'), may hold values from 0 to 28, as said below
- hidden_in: bfloat16 [512, 2048], P('seq'), may hold values from -0.75 to 0.75
- out_proj: bfloat16 [2048, 2048], P('tensor'), may hold values from -0.125 to 0.125
- norm_gain: float32 [2048], replicated, may hold values from 0.5 to 1.5
- gate_proj: bfloat16 [64, 2048, 1024], P('seq', None, 'tensor'), may hold values from -0.125 to 0.125
- up_proj: bfloat16 [64, 2048, 1024], P('seq', None, 'tensor'), may hold values from -0.125 to 0.125
- down_proj: bfloat16 [64, 1024, 2048], P('seq', 'tensor'), may hold values from -0.1875 to 0.1875
- expert_ids: int32 [512, 8], P('seq'), may hold values from 0 to 63, all different within a row; in each aligned block of 64 rows (0 to 63, 64 to 127, ...) at most 16 rows name the same one
- route_weight: float32 [512, 8], P('seq'), may hold values from 0.02 to 0.5
Outputs:
- mixed_out: bfloat16 [512, 2048], P('seq', 'tensor')
- log_sum_exp: float32 [512, 16], P('seq', 'tensor')
- key_cache_out: bfloat16 [96, 128, 2048], P('seq', None, 'tensor')
- value_cache_out: bfloat16 [96, 128, 2048], P('seq', None, 'tensor')
Inputs may be any that keep to these rules, and one draw needn't show every extreme that they name: `page_request`: every request holds one or more pages and at most 128; together they hold all 96 pages, and one request holds min(128, 89). `page_slot`: the pages of one request carry the numbers 0, 1, 2 and so on, each once. A request's pages hold cache_len + 8 positions or more, and its last page holds at least one of its first cache_len positions. `tree_mask`: row i marks node i and its ancestors in a tree rooted at node 0; each node's parent stands one to four nodes before it. `accepted`: the 8 nodes nearest the root on a path from node 0, in order from the root. `expert_ids`: at most 16 of the 64 rows of one request name the same expert.
All inputs are finite; a program needn't handle non-finite values.
Results may differ from a plain program's by a relative error of at most 0.024.
Values may be sent and summed in bfloat16 or wider, within the bound.
No kernel may reach another device: no remote copies, remote signals or barrier semaphores. Data moves between devices by JAX's collectives and lax.ppermute only.
A program may use at most 128 MiB of HBM per device.

v0:
```python
import math

import jax
import jax.numpy as jnp
from jax import lax
from jax.sharding import PartitionSpec as P

HD = 128
EXPERTS = 64
CAP = 16


MASKED = -1e30
HIGHEST = lax.Precision.HIGHEST


def expert_block(slot_rows, gate_proj, up_proj, down_proj):
    gate_value = jnp.einsum(
        "gecd,edf->gecf", slot_rows, gate_proj, preferred_element_type=jnp.float32
    )
    up_value = jnp.einsum("gecd,edf->gecf", slot_rows, up_proj, preferred_element_type=jnp.float32)
    active = (jax.nn.silu(gate_value) * up_value).astype(jnp.bfloat16)
    return jnp.einsum(
        "gecf,efd->gecd", active, down_proj, preferred_element_type=jnp.float32
    ).astype(jnp.bfloat16)


def on_device(
    queries,
    draft_keys,
    draft_values,
    key_cache,
    value_cache,
    page_request,
    page_slot,
    cache_len,
    tree_mask,
    accepted,
    hidden_in,
    out_proj,
    norm_gain,
    gate_proj,
    up_proj,
    down_proj,
    expert_ids,
    route_weight,
):
    draft_len, head_width = queries.shape
    page_count, page_len, _ = key_cache.shape
    head_count = head_width // HD
    scaling = 1.0 / math.sqrt(HD)
    accept_rows = jnp.concatenate([draft_keys[accepted[0]], draft_values[accepted[0]]], axis=1)
    every_query, every_accept = (
        lax.all_gather(queries[None], "seq", axis=0, tiled=True),
        lax.all_gather(accept_rows[None], "seq", axis=0, tiled=True),
    )
    request_count = every_query.shape[0]
    request_ids = jnp.arange(request_count, dtype=jnp.int32)
    owner_mask = page_request[:, None] == request_ids[None, :]
    owner_weight = owner_mask.astype(jnp.bfloat16)
    page_queries = jnp.einsum(
        "pr,rqc->pqc", owner_weight, every_query, preferred_element_type=jnp.float32
    ).astype(jnp.bfloat16)
    page_length = jnp.sum(jnp.where(owner_mask, cache_len[None, :], 0), axis=1)
    position = page_slot[:, None] * page_len + jnp.arange(page_len, dtype=jnp.int32)[None, :]
    live_key = position < page_length[:, None]
    far_scores = (
        jnp.einsum(
            "pqhd,pkhd->phqk",
            page_queries.reshape(page_count, draft_len, head_count, HD),
            key_cache.reshape(page_count, page_len, head_count, HD),
            preferred_element_type=jnp.float32,
        )
        * scaling
    )
    far_scores = jnp.where(live_key[:, None, None, :], far_scores, MASKED)
    page_max = jnp.max(far_scores, axis=3)
    far_weights = jnp.exp(far_scores - page_max[:, :, :, None])
    page_sum = jnp.sum(far_weights, axis=3)
    page_out = jnp.einsum(
        "phqk,pkhd->phqd",
        far_weights.astype(jnp.bfloat16),
        value_cache.reshape(page_count, page_len, head_count, HD),
        preferred_element_type=jnp.float32,
    )
    member_mask = owner_mask.T[:, :, None, None]
    dest_max = jnp.max(jnp.where(member_mask, page_max[None], MASKED), axis=1)
    factor = jnp.where(
        member_mask, jnp.exp(jnp.minimum(page_max[None] - dest_max[:, None], 0.0)), 0.0
    )
    dest_sum = jnp.einsum("rphq,phq->rhq", factor, page_sum, precision=HIGHEST)
    dest_out = jnp.einsum("rphq,phqd->rhqd", factor, page_out, precision=HIGHEST)
    got_out, got_max, got_sum = (
        lax.all_to_all(
            dest_out.astype(jnp.bfloat16), "seq", split_axis=0, concat_axis=0, tiled=True
        ).astype(dest_out.dtype),
        lax.all_to_all(
            dest_max.astype(jnp.bfloat16), "seq", split_axis=0, concat_axis=0, tiled=True
        ).astype(dest_max.dtype),
        lax.all_to_all(
            dest_sum.astype(jnp.bfloat16), "seq", split_axis=0, concat_axis=0, tiled=True
        ).astype(dest_sum.dtype),
    )
    own_queries = queries.reshape(draft_len, head_count, HD)
    near_scores = (
        jnp.einsum(
            "qhd,khd->hqk",
            own_queries,
            draft_keys.reshape(draft_len, head_count, HD),
            preferred_element_type=jnp.float32,
        )
        * scaling
    )
    near_scores = jnp.where((tree_mask[0] > 0)[None], near_scores, MASKED)
    near_max = jnp.max(near_scores, axis=2)
    near_weights = jnp.exp(near_scores - near_max[:, :, None])
    near_sum = jnp.sum(near_weights, axis=2)
    near_out = jnp.einsum(
        "hqk,khd->hqd",
        near_weights.astype(jnp.bfloat16),
        draft_values.reshape(draft_len, head_count, HD),
        preferred_element_type=jnp.float32,
    )
    row_max = jnp.maximum(near_max, jnp.max(got_max, axis=0))
    near_scale = jnp.exp(near_max - row_max)
    far_scale = jnp.exp(got_max - row_max[None])
    total_sum = near_sum * near_scale + jnp.sum(got_sum * far_scale, axis=0)
    summed = near_out * near_scale[:, :, None] + jnp.sum(got_out * far_scale[:, :, :, None], axis=0)
    attended = (
        (summed / total_sum[:, :, None])
        .transpose(1, 0, 2)
        .reshape(draft_len, head_width)
        .astype(jnp.bfloat16)
    )
    log_sum_exp = (row_max + jnp.log(total_sum)).T
    partial_proj = jnp.dot(attended, out_proj, preferred_element_type=jnp.float32)
    projected = lax.psum(partial_proj.astype(jnp.bfloat16), "tensor").astype(jnp.float32)
    mixed = hidden_in.astype(jnp.float32) + projected
    normed = (
        mixed * lax.rsqrt(jnp.mean(mixed * mixed, axis=1, keepdims=True) + 1e-06) * norm_gain
    ).astype(jnp.bfloat16)
    pick_count = expert_ids.shape[1]
    local_experts = gate_proj.shape[0]
    group_count = EXPERTS // local_experts
    slots_total = EXPERTS * CAP
    flat_ids = expert_ids.reshape(-1)
    hits = (flat_ids[:, None] == jnp.arange(EXPERTS, dtype=jnp.int32)[None, :]).astype(jnp.int32)
    rank = jnp.sum((jnp.cumsum(hits, axis=0) - hits) * hits, axis=1)
    slot_of = (flat_ids * CAP + rank).reshape(draft_len, pick_count)
    slot_ids = jnp.arange(slots_total, dtype=jnp.int32)
    dispatch_map = jnp.any(slot_ids[:, None, None] == slot_of[None], axis=2).astype(jnp.bfloat16)
    send_rows = (
        jnp.dot(dispatch_map, normed, preferred_element_type=jnp.float32)
        .astype(jnp.bfloat16)
        .reshape(group_count, local_experts, CAP, normed.shape[1])
    )
    combine = jnp.sum(
        jnp.where(slot_of[:, :, None] == slot_ids[None, None, :], route_weight[:, :, None], 0.0),
        axis=1,
    )
    column_width = mixed.shape[1] // lax.axis_size("tensor")
    column_start = lax.axis_index("tensor") * column_width
    result = expert_block(
        lax.all_to_all(send_rows, "seq", split_axis=0, concat_axis=0, tiled=True),
        gate_proj,
        up_proj,
        down_proj,
    )
    back_rows = lax.all_to_all(result, "seq", split_axis=0, concat_axis=0, tiled=True)
    flat_rows = back_rows.reshape(slots_total, back_rows.shape[3])
    combine_high = combine.astype(jnp.bfloat16)
    combine_low = (combine - combine_high.astype(jnp.float32)).astype(jnp.bfloat16)
    weighted = jnp.dot(combine_high, flat_rows, preferred_element_type=jnp.float32) + jnp.dot(
        combine_low, flat_rows, preferred_element_type=jnp.float32
    )
    moe_part = lax.psum_scatter(
        weighted.astype(jnp.bfloat16), "tensor", scatter_dimension=1, tiled=True
    ).astype(jnp.float32)
    mixed_out = (lax.dynamic_slice_in_dim(mixed, column_start, column_width, 1) + moe_part).astype(
        jnp.bfloat16
    )
    accept_count = every_accept.shape[1]
    page_accept = jnp.einsum(
        "pr,rac->pac", owner_weight, every_accept, preferred_element_type=jnp.float32
    ).astype(jnp.bfloat16)
    offset = position - page_length[:, None]
    placement = offset[:, :, None] == jnp.arange(accept_count, dtype=jnp.int32)[None, None, :]
    written = jnp.einsum(
        "pia,pac->pic",
        placement.astype(jnp.bfloat16),
        page_accept,
        preferred_element_type=jnp.float32,
    ).astype(jnp.bfloat16)
    touched = jnp.any(placement, axis=2)[:, :, None]
    key_cache_out = jnp.where(touched, written[:, :, :head_width], key_cache)
    value_cache_out = jnp.where(touched, written[:, :, head_width:], value_cache)
    return (mixed_out, log_sum_exp, key_cache_out, value_cache_out)


def solution(mesh):
    return jax.shard_map(
        on_device,
        mesh=mesh,
        in_specs=(
            P("seq", "tensor"),
            P("seq", "tensor"),
            P("seq", "tensor"),
            P("seq", None, "tensor"),
            P("seq", None, "tensor"),
            P("seq"),
            P("seq"),
            P(),
            P("seq", None, None),
            P("seq", None),
            P("seq", None),
            P("tensor", None),
            P(),
            P("seq", None, "tensor"),
            P("seq", None, "tensor"),
            P("seq", "tensor", None),
            P("seq", None),
            P("seq", None),
        ),
        out_specs=(
            P("seq", "tensor"),
            P("seq", "tensor"),
            P("seq", None, "tensor"),
            P("seq", None, "tensor"),
        ),
        check_vma=False,
    )
```

profile of v0, /device:TPU:0, one launch (start us, length us, event | category | flops | bytes accessed | tf_op | source)
XLA Modules:
  0.0 393.0 jit_solution(8291172530403849364)
XLA Ops:
  7.2 0.8 broadcast_multiply_fusion
  8.0 0.7 iota_compare_fusion.7
  8.6 0.8 select_reduce_fusion.2
  9.4 33.2 %all-gather = bf16[512,512]{1,0:T(8,128)(2,1)S(1)} all-gather(bf16[64,512]{1,0:T(8,128)(2,1)} %param.18), channel_id=2, replica_groups=mesh['seq'=8,'tensor'=4] {'seq'}, dimensions={0}, use_global_device_ids=true | all-gather | bytes 589824 | tf_op jit(solution)/shard_map/all_gather | solution.py:54
  42.6 1.2 convolution_convert_fusion.3
  43.8 1.3 reshape.247
  45.1 4.0 %fusion.103 = (f32[12,4,64]{2,1,0:T(4,128)S(1)}, f32[12,4,64,128]{3,2,1,0:T(8,128)}) fusion(bf16[12,64,4,128]{3,2,0,1:T(4,128)(2,1)} %reshape.247, pred[12,128]{1,0:T(8,128)(4,1)S(1)} %fusion.90, bf16[12,128,512]{2,1,0:T(8,128)(2,1)} %param.21), kind=kOutput, calls=%fused_computation.125 | convolution fusion | flops 101839872 | bytes 3945984 | tf_op jit(solution)/shard_map/pqhd,pkhd->phqk/dot_general | solution.py:68
  49.2 2.3 fusion.22
  51.7 0.3 select_reduce_fusion.1
  52.0 0.7 multiply_reduce_fusion
  52.8 0.7 reshape.251
  53.5 5.7 %all-to-all-start.2 = ((bf16[8,2,128]{2,1,0:T(2,128)(2,1)}), bf16[8,2,128]{2,1,0:T(2,128)(2,1)S(1)}, u32[]{:S(2)}, u32[]{:S(2)}) async-start(bf16[8,2,128]{2,1,0:T(2,128)(2,1)} %reshape.251), calls=%async_computation.2 | async-start | bytes 8192 | tf_op jit(solution)/shard_map/all_to_all | solution.py:100
  59.5 2.5 fusion.14
  62.0 3.2 fusion.47
  65.2 1.2 reduce-window.6
  66.4 0.2 slice_reduce_fusion
  66.9 0.7 reshape.249
  67.8 6.0 %all-to-all-start = ((bf16[8,2,128]{2,1,0:T(2,128)(2,1)}), bf16[8,2,128]{2,1,0:T(2,128)(2,1)S(1)}, u32[]{:S(2)}, u32[]{:S(2)}) async-start(bf16[8,2,128]{2,1,0:T(2,128)(2,1)} %reshape.249), calls=%async_computation | async-start | bytes 8192 | tf_op jit(solution)/shard_map/all_to_all | solution.py:97
  73.9 0.9 copy.170
  74.9 5.4 %all-to-all-done = bf16[8,2,128]{2,1,0:T(2,128)(2,1)S(1)} async-done(((bf16[8,2,128]{2,1,0:T(2,128)(2,1)}), bf16[8,2,128]{2,1,0:T(2,128)(2,1)S(1)}, u32[]{:S(2)}, u32[]{:S(2)}) %all-to-all-start) | async-done | bytes 4128 | tf_op jit(solution)/shard_map/all_to_all | solution.py:97
  80.3 3.5 all-to-all-start.1
  83.8 0.2 fusion.104
  84.3 0.6 fusion.95
  84.9 9.1 %all-to-all-done.1 = bf16[8,4,64,128]{3,2,1,0:T(8,128)(2,1)S(1)} async-done(((bf16[8,4,64,128]{3,2,1,0:T(8,128)(2,1)}), bf16[8,4,64,128]{3,2,1,0:T(8,128)(2,1)S(1)}, u32[]{:S(2)}, u32[]{:S(2)}) %all-to-all-start.1) | async-done | bytes 524320 | tf_op jit(solution)/shard_map/all_to_all | solution.py:94
  94.0 0.3 multiply_reduce_fusion.1
  94.3 0.2 fusion.55
  94.6 1.2 convolution_convert_fusion.1
  95.8 0.7 fusion.13
  96.5 30.5 %all-reduce.2.cloned.1.call-done = bf16[64,2048]{1,0:T(8,128)(2,1)} async-done(((bf16[64,2048]{1,0:T(8,128)(2,1)}), bf16[64,2048]{1,0:T(8,128)(2,1)}) %all-reduce.2.cloned.1.call-update) | async-done | bytes 262160 | tf_op jit(solution)/shard_map/psum | solution.py:137
  127.0 1.1 convert_add_fusion
  128.2 2.4 convolution_convert_fusion
  130.6 97.6 %all_to_all.25 = bf16[8,8,16,2048]{3,2,1,0:T(8,128)(2,1)S(1)} all-to-all(bf16[8,8,16,2048]{3,2,1,0:T(8,128)(2,1)S(1)} %bitcast.166), channel_id=1, replica_groups=mesh['seq'=8,'tensor'=4] {'seq'}, dimensions={0} | all-to-all | bytes 8388608 | tf_op jit(solution)/shard_map/all_to_all | solution.py:164
  228.3 1.3 fusion.24
  229.5 5.0 %fusion.39 = bf16[8,8,16,256]{3,2,0,1:T(8,128)(2,1)S(1)} fusion(bf16[8,2048,256]{2,1,0:T(8,128)(2,1)} %param.32, bf16[8,8,16,2048]{3,2,1,0:T(8,128)(2,1)S(1)} %all_to_all.25, f32[8,8,16,256]{3,2,0,1:T(8,128)S(1)} %fusion.24), kind=kOutput, calls=%fused_computation.38 | convolution fusion | flops 1075314688 | bytes 14155776 | tf_op jit(solution)/shard_map/gecd,edf->gecf/dot_general | solution.py:21
  234.6 1.3 convert_bitcast_fusion
  235.8 2.5 copy.181
  238.3 4.7 %all-to-all-start.4 = ((bf16[8,8,16,2048]{3,2,1,0:T(8,128)(2,1)}), bf16[8,8,16,2048]{3,2,1,0:T(8,128)(2,1)}, u32[]{:S(2)}, u32[]{:S(2)}) async-start(bf16[8,8,16,2048]{3,2,1,0:T(8,128)(2,1)} %copy.181), calls=%async_computation.4 | async-start | bytes 8388608 | tf_op jit(solution)/shard_map/all_to_all | solution.py:169
  243.1 0.6 gather_fusion
  243.7 0.6 gather_fusion.1
  244.3 110.9 %all-gather.1 = bf16[64,1024]{1,0:T(8,128)(2,1)S(1)} all-gather(bf16[8,1024]{1,0:T(8,128)(2,1)S(1)} %pad_maximum_fusion), channel_id=3, replica_groups=mesh['seq'=8,'tensor'=4] {'seq'}, dimensions={0}, use_global_device_ids=true | all-gather | bytes 147456 | tf_op jit(solution)/shard_map/all_gather | solution.py:55
  355.2 0.7 select_reduce_fusion
  356.0 0.3 convolution_convert_fusion.4
  356.3 2.8 convolution_convert_fusion.2
  359.1 3.0 fusion.84
  362.1 3.7 fusion.10
  365.9 4.3 %slice_select_fusion = (bf16[12,128,512]{2,1,0:T(8,128)(2,1)}, bf16[12,128,512]{2,1,0:T(8,128)(2,1)}) fusion(bf16[12,128,512]{2,1,0:T(8,128)(2,1)} %param.22, bf16[12,128,1024]{2,1,0:T(8,128)(2,1)} %convolution_convert_fusion.2, pred[12,128]{1,0:T(8,128)(4,1)S(1)} %fusion.87, bf16[12,128,512]{2,1,0:T(8,128)(2,1)} %param.21), kind=kLoop, calls=%fused_computation.28 | loop fusion | flops 1572864 | bytes 9438720 | tf_op jit(solution)/shard_map/jit(_where)/select_n | solution.py:196
  370.2 14.5 %reduce-scatter.2.cloned.1.call-done = bf16[64,512]{1,0:T(8,128)(2,1)} async-done(((bf16[64,2048]{1,0:T(8,128)(2,1)}), bf16[64,512]{1,0:T(8,128)(2,1)}) %reduce-scatter.2.cloned.1.call-update) | async-done | bytes 65552 | tf_op jit(solution)/shard_map/reduce_scatter | solution.py:176
  384.7 1.5 add_convert_fusion
  (72 shorter events, 1.9 us)
Async XLA Ops:
  7.2 87.4 %copy-start = (bf16[512,2048]{1,0:T(8,128)(2,1)S(1)}, bf16[512,2048]{1,0:T(8,128)(2,1)}, u32[]{:S(2)}) copy-start(bf16[512,2048]{1,0:T(8,128)(2,1)} %param.29) | copy-start | bytes 6291460
  49.1 10.0 %copy-start.7 = (s32[64,8]{0,1:T(8,128)S(1)}, s32[64,8]{0,1:T(8,128)}, u32[]{:S(2)}) copy-start(s32[64,8]{0,1:T(8,128)} %param.34) | copy-start | bytes 6148
  49.1 10.3 %copy-start.6 = (s32[1,64,64]{2,1,0:T(8,128)S(1)}, s32[1,64,64]{2,1,0:T(8,128)}, u32[]{:S(2)}) copy-start(s32[1,64,64]{2,1,0:T(8,128)} %param.26) | copy-start | bytes 49156
  53.5 14.3 %all-to-all-start.2 = ((bf16[8,2,128]{2,1,0:T(2,128)(2,1)}), bf16[8,2,128]{2,1,0:T(2,128)(2,1)S(1)}, u32[]{:S(2)}, u32[]{:S(2)}) async-start(bf16[8,2,128]{2,1,0:T(2,128)(2,1)} %reshape.251), calls=%async_computation.2 | async-start | bytes 8192 | tf_op jit(solution)/shard_map/all_to_all | solution.py:100
  65.2 18.6 %copy-start.3 = (bf16[64,512]{1,0:T(8,128)(2,1)S(1)}, bf16[64,512]{1,0:T(8,128)(2,1)}, u32[]{:S(2)}) copy-start(bf16[64,512]{1,0:T(8,128)(2,1)} %param.18) | copy-start | bytes 196612
  65.2 18.6 %copy-start.4 = (bf16[64,512]{1,0:T(8,128)(2,1)S(1)}, bf16[64,512]{1,0:T(8,128)(2,1)}, u32[]{:S(2)}) copy-start(bf16[64,512]{1,0:T(8,128)(2,1)} %param.19) | copy-start | bytes 196612
  65.2 29.1 %copy-start.5 = (bf16[64,512]{1,0:T(8,128)(2,1)S(1)}, bf16[64,512]{1,0:T(8,128)(2,1)}, u32[]{:S(2)}) copy-start(bf16[64,512]{1,0:T(8,128)(2,1)} %param.20) | copy-start | bytes 196612
  67.8 12.5 %all-to-all-start = ((bf16[8,2,128]{2,1,0:T(2,128)(2,1)}), bf16[8,2,128]{2,1,0:T(2,128)(2,1)S(1)}, u32[]{:S(2)}, u32[]{:S(2)}) async-start(bf16[8,2,128]{2,1,0:T(2,128)(2,1)} %reshape.249), calls=%async_computation | async-start | bytes 8192 | tf_op jit(solution)/shard_map/all_to_all | solution.py:97
  80.3 13.7 %all-to-all-start.1 = ((bf16[8,4,64,128]{3,2,1,0:T(8,128)(2,1)}), bf16[8,4,64,128]{3,2,1,0:T(8,128)(2,1)S(1)}, u32[]{:S(2)}, u32[]{:S(2)}) async-start(bf16[8,4,64,128]{3,2,1,0:T(8,128)(2,1)} %copy.170), calls=%async_computation.1 | async-start | bytes 1048576 | tf_op jit(solution)/shard_map/all_to_all | solution.py:94
  83.8 43.3 %all-reduce.2.cloned.1.call-start = ((), (), s32[]{:S(2)}) async-start(), calls=%async_computation.6 | async-start | bytes 524288 | tf_op jit(solution)/shard_map/psum | solution.py:137
  84.3 42.8 %copy-start.2 = (bf16[64,2048]{1,0:T(8,128)(2,1)S(1)}, bf16[64,2048]{1,0:T(8,128)(2,1)}, u32[]{:S(2)}) copy-start(bf16[64,2048]{1,0:T(8,128)(2,1)} %param.28) | copy-start | bytes 786436
  94.3 33.9 %copy-start.8 = (f32[2048]{0:T(1024)S(1)}, f32[2048]{0:T(1024)}, u32[]{:S(2)}) copy-start(f32[2048]{0:T(1024)} %param.30) | copy-start | bytes 24580
  128.2 100.1 %slice-start.2 = ((s8[8388608]{0:T(1024)(128)(4,1)}), s8[4194304]{0:T(1024)(128)(4,1)S(1)}, s32[]{:S(2)}) async-start(s8[8388608]{0:T(1024)(128)(4,1)} %bitcast.173), calls=%async_computation.10 | async-start | bytes 8388608
  130.6 97.6 %slice-start.3 = ((s8[8388608]{0:T(1024)(128)(4,1)}), s8[4194304]{0:T(1024)(128)(4,1)S(1)}, s32[]{:S(2)}) async-start(s8[8388608]{0:T(1024)(128)(4,1)} %bitcast.173), calls=%async_computation.11 | async-start | bytes 8388608
  228.3 6.3 %slice-start = ((s8[8388608]{0:T(1024)(128)(4,1)}), s8[4194304]{0:T(1024)(128)(4,1)S(1)}, s32[]{:S(2)}) async-start(s8[8388608]{0:T(1024)(128)(4,1)} %bitcast.167), calls=%async_computation.8 | async-start | bytes 8388608
  229.5 5.0 %slice-start.1 = ((s8[8388608]{0:T(1024)(128)(4,1)}), s8[4194304]{0:T(1024)(128)(4,1)S(1)}, s32[]{:S(2)}) async-start(s8[8388608]{0:T(1024)(128)(4,1)} %bitcast.167), calls=%async_computation.9 | async-start | bytes 8388608
  238.3 4.7 %copy-start.11 = (s32[1,8]{1,0:T(1,128)S(1)}, s32[1,8]{1,0:T(1,128)}, u32[]{:S(2)}) copy-start(s32[1,8]{1,0:T(1,128)} %param.27) | copy-start | bytes 100
  238.3 5.9 %copy-start.9 = (f32[64,8]{0,1:T(8,128)S(1)}, f32[64,8]{0,1:T(8,128)}, u32[]{:S(2)}) copy-start(f32[64,8]{0,1:T(8,128)} %param.35) | copy-start | bytes 6148
  238.3 117.7 %copy-start.10 = (s32[12]{0:T(128)S(1)}, s32[12]{0:T(128)}, u32[]{:S(2)}) copy-start(s32[12]{0:T(128)} %param.23) | copy-start | bytes 148
  238.3 120.8 %all-to-all-start.4 = ((bf16[8,8,16,2048]{3,2,1,0:T(8,128)(2,1)}), bf16[8,8,16,2048]{3,2,1,0:T(8,128)(2,1)}, u32[]{:S(2)}, u32[]{:S(2)}) async-start(bf16[8,8,16,2048]{3,2,1,0:T(8,128)(2,1)} %copy.181), calls=%async_computation.4 | async-start | bytes 8388608 | tf_op jit(solution)/shard_map/all_to_all | solution.py:169
  243.0 141.7 %reduce-scatter.2.cloned.1.call-start = ((), (), s32[]{:S(2)}) async-start(), calls=%async_computation.7 | async-start | bytes 327680 | tf_op jit(solution)/shard_map/reduce_scatter | solution.py:176
  365.9 20.3 %copy-start.1 = (bf16[512,2048]{1,0:T(8,128)(2,1)S(1)}, bf16[512,2048]{1,0:T(8,128)(2,1)}, u32[]{:S(2)}) copy-start(bf16[512,2048]{1,0:T(8,128)(2,1)} %param.29) | copy-start | bytes 6291460
Sparse Core Ops, SparseCore 0:
  95.9 31.0 all-reduce.1
  366.0 18.6 reduce-scatter.1
where the time goes:
time: 394 us; the launch traced here: 393 us
  blocking collectives  242 us (61%)
  waiting for transfers between devices  59.5 us (15%)
  matrix products  32.2 us (8%)
  starting transfers between devices  19.9 us (5%)
  other arithmetic  16.5 us (4%)
  between operations  14.4 us (4%)
  local copies, waits for them, and re-layouts  8.74 us (2%)
    all_gather x1, blocking collectives, on_device(): lax.all_gather(accept_rows[None], 'seq', axis=0, tiled=True)  111 us
    all_to_all x1, blocking collectives, on_device(): lax.all_to_all(send_rows, 'seq', split_axis=0, concat_axis=0, tiled=True)  97.6 us
    all_gather x1, blocking collectives, on_device(): lax.all_gather(queries[None], 'seq', axis=0, tiled=True)  33.2 us
    psum x1, waiting for transfers between devices, on_device(): lax.psum(partial_proj.astype(jnp.bfloat16), 'tensor').astype(jnp.float32)  30.5 us
    reduce_scatter x1, waiting for transfers between devices, on_device(): lax.psum_scatter(weighted.astype(jnp.bfloat16), 'tensor', scatter_dimensi...  14.5 us
    all_to_all x1, waiting for transfers between devices, on_device(): lax.all_to_all(dest_out.astype(jnp.bfloat16), 'seq', split_axis=0, concat...  9.08 us
  transfers between devices with their start and end apart: 6, of which 4 were waited for; matrix products, arithmetic and copies ran while one was open for 5% of the time, Pallas kernels for 0%

commit v1 on v0

v1 whole, which is shorter than its diff:
```python
import functools
import math

import jax
import jax.numpy as jnp
from jax import lax
from jax.experimental import pallas as pl
from jax.experimental.pallas import tpu as pltpu
from jax.sharding import PartitionSpec as P

HD = 128
CAP = 16
MASKED = -1e30
F32 = jnp.float32
BF16 = jnp.bfloat16
I32 = jnp.int32
STAT = 128
VMEM_LIMIT = 56 * 1024 * 1024


def vmem():
    return pl.BlockSpec(memory_space=pltpu.VMEM)


def smem():
    return pl.BlockSpec(memory_space=pltpu.SMEM)


def shape(dims, dtype):
    return jax.ShapeDtypeStruct(dims, dtype)


def params():
    return pltpu.CompilerParams(vmem_limit_bytes=VMEM_LIMIT)


def cost(flops, moved):
    return pl.CostEstimate(flops=flops, bytes_accessed=moved, transcendentals=0)


def each(count, body):
    if count <= 16:
        for i in range(count):
            body(i)
    else:

        @pl.loop(0, count)
        def _(i):
            body(i)


def dot(a, b):
    return jnp.dot(a, b, preferred_element_type=F32)


def dot_t(a, b):
    return lax.dot_general(a, b, (((1,), (1,)), ((), ())), preferred_element_type=F32)


def aligned(index, size):
    return index * size if isinstance(index, int) else pl.multiple_of(index * size, size)


def three_parts(value):
    high = value.astype(BF16).astype(F32)
    rest = value - high
    middle = rest.astype(BF16).astype(F32)
    return high, middle, rest - middle


def near_kernel(q_ref, k_ref, v_ref, mask_ref, acc_ref, ids_ref, rw_ref, out_ref, lse_ref, pack_ref):
    draft, width = q_ref.shape
    scaling = 1.0 / math.sqrt(HD)
    seen = mask_ref[0] > 0
    for h in range(width // HD):
        cols = slice(h * HD, (h + 1) * HD)
        scores = jnp.where(seen, dot_t(q_ref[:, cols], k_ref[:, cols]) * scaling, MASKED)
        top = jnp.max(scores, axis=1, keepdims=True)
        weights = jnp.exp(scores - top)
        total = jnp.sum(weights, axis=1, keepdims=True)
        out_ref[:, cols] = dot(weights.astype(BF16), v_ref[:, cols]) / total
        lse_ref[:, cols] = jnp.broadcast_to(top + jnp.log(total), (draft, HD))
    accepted = acc_ref.shape[0]
    pick = (lax.broadcasted_iota(I32, (accepted, draft), 1) == acc_ref[...]).astype(F32).astype(BF16)
    rows = jnp.concatenate([dot(pick, k_ref[...]), dot(pick, v_ref[...])], axis=0)
    pack_ref[0, 0 : 2 * accepted, :] = rows.astype(BF16)
    pack_ref[0, 2 * accepted :, :] = jnp.zeros((16, width), BF16)
    zero = jnp.zeros((8, draft), F32)
    for g, part in enumerate((ids_ref[...], *three_parts(rw_ref[...]))):
        pack_ref[0, 2 * accepted :, g * 128 : g * 128 + draft] = jnp.concatenate([part, zero], axis=0).astype(BF16)


def far_kernel(pos_ref, live_ref, key_ref, value_ref, *refs, counts, n_out):
    pieces, outs = refs[: len(counts)], refs[len(counts) : len(counts) + n_out]
    q_s, m_s, l_s, o_s = refs[len(counts) + n_out :]
    pages, page_len, width = key_ref.shape
    draft = q_s.shape[1]
    heads = width // HD
    scaling = 1.0 / math.sqrt(HD)
    at = 0
    for piece, count in zip(pieces, counts):
        q_s[at : at + count] = piece[...]
        at += count

    def clear(i):
        m_s[i] = jnp.full((draft, width), MASKED, F32)
        l_s[i] = jnp.zeros((draft, width), F32)
        o_s[i] = jnp.zeros((draft, width), F32)

    each(at, clear)
    cell = lax.broadcasted_iota(I32, (draft, page_len), 1)
    for p in range(pages):
        pos = pos_ref[p]
        alive = cell < live_ref[p]
        for h in range(heads):
            cols = slice(h * HD, (h + 1) * HD)
            scores = dot_t(q_s[pos, :, cols], key_ref[p, :, cols]) * scaling
            scores = jnp.where(alive, scores, MASKED)
            top = jnp.max(scores, axis=1, keepdims=True)
            weights = jnp.exp(scores - top)
            total = jnp.sum(weights, axis=1, keepdims=True)
            out = dot(weights.astype(BF16), value_ref[p, :, cols])
            old = m_s[pos, :, cols]
            new = jnp.maximum(old, top)
            keep, add = jnp.exp(old - new), jnp.exp(top - new)
            m_s[pos, :, cols] = new
            l_s[pos, :, cols] = l_s[pos, :, cols] * keep + total * add
            o_s[pos, :, cols] = o_s[pos, :, cols] * keep + out * add
    lane = lax.broadcasted_iota(I32, (draft, STAT), 1)

    def finish(i):
        target, row = (outs[i], 0) if n_out > 1 else (outs[0], i)
        stat = jnp.zeros((draft, STAT), F32)
        for h in range(heads):
            cols = slice(h * HD, (h + 1) * HD)
            total = l_s[i, :, cols]
            some = total > 0.0
            safe = jnp.where(some, total, 1.0)
            target[row, :, cols] = (o_s[i, :, cols] / safe).astype(BF16)
            lse = jnp.where(some, m_s[i, :, cols] + jnp.log(safe), MASKED)
            stat = jnp.where(lane % heads == h, lse, stat)
        high, middle, low = three_parts(stat)
        packed = jnp.where(lane < heads, high, jnp.where(lane < 2 * heads, middle, low))
        target[row, :, width:] = packed.astype(BF16)

    each(at, finish)


def merge_kernel(t_ref, near_ref, lse_ref, hidden_ref, w_ref, *refs, counts, n_out):
    pieces, refs = refs[: len(counts)], refs[len(counts) :]
    lse_out, outs = refs[0], refs[1:]
    draft, width = near_ref.shape
    heads = width // HD
    rows = [(piece, i) for piece, count in zip(pieces, counts) for i in range(count)]
    stats = [piece[i, :, width:].astype(F32) for piece, i in rows]
    attended = []
    for h in range(heads):
        cols = slice(h * HD, (h + 1) * HD)
        sums = [
            s[:, h : h + 1] + s[:, heads + h : heads + h + 1] + s[:, 2 * heads + h : 2 * heads + h + 1]
            for s in stats
        ]
        own = lse_ref[:, h * HD : h * HD + 1]
        top = functools.reduce(jnp.maximum, sums, own)
        weight = jnp.exp(own - top)
        total = weight
        summed = near_ref[:, cols] * weight
        for (piece, i), s in zip(rows, sums):
            weight = jnp.exp(s - top)
            total = total + weight
            summed = summed + piece[i, :, cols].astype(F32) * weight
        attended.append((summed / total).astype(BF16))
        lse_out[:, h : h + 1] = top + jnp.log(total)
    attended = jnp.concatenate(attended, axis=1)
    if n_out == 1:
        outs[0][...] = dot(attended, w_ref[...]).astype(outs[0].dtype)
        return
    for n in range(n_out):
        start = pl.multiple_of((t_ref[0] ^ n) * width, width)
        part = dot(attended, w_ref[:, pl.ds(start, width)])
        if n == 0:
            part = part + hidden_ref[:, pl.ds(start, width)].astype(F32)
        outs[n][...] = part.astype(outs[n].dtype)


def slots_kernel(me_ref, *refs, counts, experts, accept):
    pieces, (g_ref, c_ref, w_ref) = refs[: len(counts)], refs[len(counts) :]
    draft = g_ref.shape[2]
    upper = (
        lax.broadcasted_iota(I32, (draft, draft), 0) < lax.broadcasted_iota(I32, (draft, draft), 1)
    ).astype(F32).astype(BF16)
    same = (
        lax.broadcasted_iota(I32, (draft, draft), 0) == lax.broadcasted_iota(I32, (draft, draft), 1)
    ).astype(F32).astype(BF16)
    number = lax.broadcasted_iota(I32, (CAP, draft), 0).astype(F32)
    first = me_ref[0] * experts

    def one(piece, i, m):
        def part(g):
            return piece[i, 2 * accept : 2 * accept + 16, g * 128 : g * 128 + draft].astype(F32)[0:8]

        ids, weight = part(0), part(1) + part(2) + part(3)
        hits, weights = [], []
        for e in range(experts):
            hit = ids == (first + e).astype(F32)
            hits.append(jnp.max(jnp.where(hit, 1.0, 0.0), axis=0, keepdims=True))
            weights.append(jnp.sum(jnp.where(hit, weight, 0.0), axis=0, keepdims=True))
        table = jnp.concatenate(hits + [jnp.zeros((16 - experts, draft), F32)], axis=0)
        rank = dot(table.astype(BF16), upper)
        blocks = []
        for e in range(experts):
            block = jnp.where((number == rank[e : e + 1]) & (hits[e] > 0.0), 1.0, 0.0)
            blocks.append(block)
            row_weight = jnp.sum(block * weights[e], axis=1, keepdims=True)
            w_ref[e, pl.ds(aligned(m, CAP), CAP), :] = jnp.broadcast_to(row_weight, (CAP, 128))
        stacked = jnp.concatenate(blocks, axis=0).astype(BF16)
        g_ref[m] = stacked
        c_ref[m] = dot_t(same, stacked).astype(BF16)

    if len(counts) > 1:
        for m, piece in enumerate(pieces):
            one(piece, 0, m)
    else:
        each(counts[0], lambda m: one(pieces[0], m, m))


def cache_kernel(pos_ref, live_ref, key_ref, value_ref, *refs, counts, accept):
    pieces, (key_out, value_out, table) = refs[: len(counts)], refs[len(counts) :]
    page_len, width = key_ref.shape[1:]
    p = pl.program_id(0)

    @pl.when(p == 0)
    def _():
        at = 0
        for piece, count in zip(pieces, counts):
            table[at : at + count] = piece[:, 0 : 2 * accept, :]
            at += count

    live = live_ref[p]
    reached = (live > -accept) & (live < page_len)

    @pl.when(jnp.logical_not(reached))
    def _():
        key_out[...] = key_ref[...]
        value_out[...] = value_ref[...]

    @pl.when(reached)
    def _():
        rows = table[pos_ref[p]]
        offset = lax.broadcasted_iota(I32, (page_len, 2 * accept), 0) - live
        column = lax.broadcasted_iota(I32, (page_len, 2 * accept), 1)
        cell = lax.broadcasted_iota(I32, (page_len, width), 0) - live
        touched = (cell >= 0) & (cell < accept)
        for source, out, shift in ((key_ref, key_out, 0), (value_ref, value_out, accept)):
            hit = (offset == column - shift) & (offset >= 0) & (offset < accept)
            place = jnp.where(hit, 1.0, 0.0).astype(BF16)
            out[0] = jnp.where(touched, dot(place, rows), source[0].astype(F32)).astype(BF16)


def expert_kernel(t_ref, gain_ref, g_ref, rw_ref, gate_ref, up_ref, *refs, layout):
    pieces, (out_ref, xs) = refs[:-2], refs[-2:]
    e = pl.program_id(0)
    experts, slots, model = xs.shape
    draft = g_ref.shape[2]

    @pl.when(e == 0)
    def _():
        gain = gain_ref[...]

        def one(m):
            parts = layout(pieces, m)
            square = sum(jnp.sum(v * v, axis=1, keepdims=True) for _, v in parts)
            scale = lax.rsqrt(square / model + 1e-6)
            for n, v in parts:
                width = v.shape[1]
                if n is None:
                    cols, sub_gain = slice(0, width), gain
                else:
                    cols = pl.ds(pl.multiple_of((t_ref[0] ^ n) * width, width), width)
                    sub_gain = gain_ref[:, cols]
                normed = (v * scale * sub_gain).astype(BF16)
                picked = dot(g_ref[m], normed).astype(BF16)
                for i in range(experts):
                    xs[i, pl.ds(aligned(m, CAP), CAP), cols] = picked[i * CAP : (i + 1) * CAP]

        each(g_ref.shape[0], one)

    rows = xs[e]
    gate = dot(rows, gate_ref[0])
    up = dot(rows, up_ref[0])
    active = gate / (1.0 + jnp.exp(-gate)) * up
    out_ref[0] = (active * rw_ref[0, :, 0:1]).astype(BF16)


def down_kernel(cols_ref, active_ref, c_ref, down_ref, out_ref, y_s):
    experts, slots, _ = active_ref.shape
    groups, draft = c_ref.shape[0:2]
    for e in range(experts):
        y_s[e] = dot(active_ref[e], down_ref[e]).astype(BF16)

    def one(m):
        rows = pl.ds(aligned(m, CAP), CAP)
        block = jnp.concatenate([y_s[e, rows, :] for e in range(experts)], axis=0)
        out_ref[0, m] = dot(c_ref[m], block).astype(BF16)

    each(groups, one)


def add_kernel(*refs, body, n_in):
    body(refs[:n_in], refs[n_in:])


def small(body, ins, outs):
    return pl.pallas_call(
        functools.partial(add_kernel, body=body, n_in=len(ins)),
        out_shape=outs,
        in_specs=[vmem()] * len(ins),
        out_specs=[vmem()] * len(outs),
        compiler_params=params(),
    )(*ins)


def on_device(
    queries,
    draft_keys,
    draft_values,
    key_cache,
    value_cache,
    page_request,
    page_slot,
    cache_len,
    tree_mask,
    accepted,
    hidden_in,
    out_proj,
    norm_gain,
    gate_proj,
    up_proj,
    down_proj,
    expert_ids,
    route_weight,
):
    draft, width = queries.shape
    pages, page_len, _ = key_cache.shape
    model = hidden_in.shape[1]
    heads = width // HD
    seq, tensor = lax.axis_size("seq"), lax.axis_size("tensor")
    experts = gate_proj.shape[0]
    hidden = gate_proj.shape[2]
    accept = accepted.shape[1]
    slots = seq * CAP
    staged = seq == 8 and tensor == 4
    me, t = lax.axis_index("seq"), lax.axis_index("tensor")

    def hop(axis, mask):
        size = seq if axis == "seq" else tensor
        pairs = [(i, i ^ mask) for i in range(size)]
        return lambda v: lax.ppermute(v, axis, pairs)

    x1, y1, core = hop("seq", 1), hop("tensor", 2), hop("tensor", 1)
    zs = [hop("seq", 2 * k) for k in (1, 2, 3)]

    def gather_seq(v):
        if not staged:
            return [lax.all_gather(v, "seq", axis=0, tiled=True)]
        beside = x1(v)
        line = [z(v) for z in zs]
        return [v, *line, beside, *[x1(b) for b in line]]

    relative = page_request ^ me if staged else page_request
    pos = (relative & 1) * 4 + (relative >> 1) if staged else relative
    pos = pos.astype(I32)
    request_hit = page_request[:, None] == jnp.arange(cache_len.shape[0], dtype=I32)[None, :]
    live = jnp.sum(jnp.where(request_hit, cache_len[None, :], 0), axis=1) - page_slot * page_len
    me1, t1 = me.reshape(1).astype(I32), t.reshape(1).astype(I32)

    every_query = gather_seq(queries[None])
    counts = tuple(a.shape[0] for a in every_query)

    near_out, near_lse, pack = pl.pallas_call(
        near_kernel,
        out_shape=[
            shape((draft, width), F32),
            shape((draft, width), F32),
            shape((1, 2 * accept + 16, width), BF16),
        ],
        in_specs=[vmem()] * 7,
        out_specs=[vmem()] * 3,
        compiler_params=params(),
        name="near",
    )(
        queries,
        draft_keys,
        draft_values,
        tree_mask,
        accepted.reshape(accept, 1),
        expert_ids.T.astype(F32),
        route_weight.T,
    )

    n_out = seq if staged else 1
    partials = pl.pallas_call(
        functools.partial(far_kernel, counts=counts, n_out=n_out),
        out_shape=[shape((seq // n_out, draft, width + STAT), BF16)] * n_out,
        in_specs=[smem(), smem()] + [vmem()] * (2 + len(every_query)),
        out_specs=[vmem()] * n_out,
        scratch_shapes=[
            pltpu.VMEM((seq, draft, width), BF16),
            pltpu.VMEM((seq, draft, width), F32),
            pltpu.VMEM((seq, draft, width), F32),
            pltpu.VMEM((seq, draft, width), F32),
        ],
        compiler_params=params(),
        name="far",
    )(pos, live, key_cache, value_cache, *every_query)

    every_pack = gather_seq(pack)

    if staged:
        back = [partials[0]]
        for place in range(1, 8):
            back.append(hop("seq", (place & 3) * 2 + (place >> 2))(partials[place]))
    else:
        back = [lax.all_to_all(partials[0], "seq", split_axis=0, concat_axis=0, tiled=True)]

    n_parts = tensor if staged else 1
    part_shape = (
        [shape((draft, width), F32)] + [shape((draft, width), BF16)] * 3 if staged else [shape((draft, model), F32)]
    )
    log_sum_exp, *parts = pl.pallas_call(
        functools.partial(merge_kernel, counts=tuple(b.shape[0] for b in back), n_out=n_parts),
        out_shape=[shape((draft, heads), F32)] + part_shape,
        in_specs=[smem()] + [vmem()] * (4 + len(back)),
        out_specs=[vmem()] * (1 + n_parts),
        compiler_params=params(),
        name="merge",
    )(t1, near_out, near_lse, hidden_in, out_proj, *back)

    if staged:
        got = [hop("tensor", n)(parts[n]) for n in (1, 2, 3)]
        mixed = parts[0] + got[0].astype(F32) + got[1].astype(F32) + got[2].astype(F32)
    else:
        summed = lax.psum(parts[0], "tensor") + hidden_in.astype(F32)
        mixed = lax.dynamic_slice_in_dim(summed, t * width, width, 1)
    row = mixed.astype(BF16)[None]

    grouped, combine, slot_weight = pl.pallas_call(
        functools.partial(
            slots_kernel, counts=tuple(a.shape[0] for a in every_pack), experts=experts, accept=accept
        ),
        out_shape=[
            shape((seq, experts * CAP, draft), BF16),
            shape((seq, draft, experts * CAP), BF16),
            shape((experts, slots, 128), F32),
        ],
        in_specs=[smem()] + [vmem()] * len(every_pack),
        out_specs=[vmem()] * 3,
        compiler_params=params(),
        name="slots",
    )(me1, *every_pack)

    page_spec = pl.BlockSpec((1, page_len, width), lambda p: (p, 0, 0))
    key_cache_out, value_cache_out = pl.pallas_call(
        functools.partial(cache_kernel, counts=tuple(a.shape[0] for a in every_pack), accept=accept),
        grid=(pages,),
        out_shape=[shape(key_cache.shape, BF16), shape(value_cache.shape, BF16)],
        in_specs=[smem(), smem(), page_spec, page_spec] + [vmem()] * len(every_pack),
        out_specs=[page_spec, page_spec],
        scratch_shapes=[pltpu.VMEM((seq, 2 * accept, width), BF16)],
        compiler_params=params(),
        name="cache",
    )(pos, live, key_cache, value_cache, *every_pack)

    if staged:
        line = [row] + [z(row) for z in zs]
        line = [jnp.concatenate(line[0:2]), jnp.concatenate(line[2:4])]
        over_x, over_y = [x1(v) for v in line], [y1(v) for v in line]
        far_corner = [y1(over_x[0]), x1(over_y[1])]
        mine = line + over_x + over_y + far_corner
        rows_in = mine + [core(v) for v in mine]

        def layout(refs, m):
            pair, i = m // 2, m % 2
            found = []
            for n in range(4):
                base = (n & 1) * 8 + (n >> 1) * 4
                found.append((n, refs[base + pair][i].astype(F32)))
            return found

    else:
        rows_in = lax.all_gather(row, "seq", axis=0, tiled=True)
        rows_in = [lax.all_gather(rows_in, "tensor", axis=2, tiled=True)]

        def layout(refs, m):
            return [(None, refs[0][m].astype(F32))]

    active = pl.pallas_call(
        functools.partial(expert_kernel, layout=layout),
        grid=(experts,),
        out_shape=shape((experts, slots, hidden), BF16),
        in_specs=[
            smem(),
            vmem(),
            vmem(),
            pl.BlockSpec((1, slots, 128), lambda e: (e, 0, 0)),
            pl.BlockSpec((1, model, hidden), lambda e: (e, 0, 0)),
            pl.BlockSpec((1, model, hidden), lambda e: (e, 0, 0)),
        ]
        + [vmem()] * len(rows_in),
        out_specs=pl.BlockSpec((1, slots, hidden), lambda e: (e, 0, 0)),
        scratch_shapes=[pltpu.VMEM((experts, slots, model), BF16)],
        compiler_params=params(),
        name="gate_up",
    )(t1, norm_gain.reshape(1, model), grouped, slot_weight, gate_proj, up_proj, *rows_in)

    def down(columns):
        steps = columns.shape[0]
        return pl.pallas_call(
            down_kernel,
            grid_spec=pltpu.PrefetchScalarGridSpec(
                num_scalar_prefetch=1,
                grid=(steps,),
                in_specs=[
                    vmem(),
                    vmem(),
                    pl.BlockSpec((experts, hidden, width), lambda i, c: (0, 0, c[i])),
                ],
                out_specs=pl.BlockSpec((1, seq, draft, width), lambda i, c: (i, 0, 0, 0)),
                scratch_shapes=[pltpu.VMEM((experts, slots, width), BF16)],
            ),
            out_shape=shape((steps, seq, draft, width), BF16),
            compiler_params=params(),
            name="down",
        )(columns.astype(I32), active, combine, down_proj)

    if not staged:
        sums = down(jnp.arange(tensor, dtype=I32))
        sums = lax.psum_scatter(sums, "tensor", scatter_dimension=0, tiled=True)[0]
        moe = lax.psum_scatter(sums, "seq", scatter_dimension=0, tiled=True)[0]
        mixed_out = (mixed + moe.astype(F32)).astype(BF16)
        return mixed_out, log_sum_exp, key_cache_out, value_cache_out

    other = core(down(jnp.stack([t ^ 1, t ^ 3])))
    own = down(jnp.stack([t, t ^ 2]))

    def split_first(ins, outs):
        a, b = ins
        first_y, first_x, keep_y, keep_x = outs
        for x in range(2):
            for z in range(2):
                first_y[2 * x + z] = (a[1, 4 * x + z].astype(F32) + b[1, 4 * x + z].astype(F32)).astype(BF16)
                keep_y[2 * x + z] = (a[0, 4 * x + z].astype(F32) + b[0, 4 * x + z].astype(F32)).astype(BF16)
        for y in range(2):
            for z in range(2):
                first_x[2 * y + z] = (a[y, 6 + z].astype(F32) + b[y, 6 + z].astype(F32)).astype(BF16)
                keep_x[2 * y + z] = (a[y, 2 + z].astype(F32) + b[y, 2 + z].astype(F32)).astype(BF16)

    four, two, one = shape((4, draft, width), BF16), shape((2, draft, width), BF16), shape((draft, width), BF16)
    first_y, first_x, keep_y, keep_x = small(split_first, (own, other), [four] * 4)
    got_y, got_x = y1(first_y), x1(first_x)

    def split_second(ins, outs):
        keep_a, got_a, keep_b, got_b = ins
        send_a, stay_a, send_b, stay_b = outs
        for keep, got, send, stay in ((keep_a, got_a, send_a, stay_a), (keep_b, got_b, send_b, stay_b)):
            stay[...] = (keep[0:2].astype(F32) + got[0:2].astype(F32)).astype(BF16)
            send[...] = (keep[2:4].astype(F32) + got[2:4].astype(F32)).astype(BF16)

    send_a, stay_a, send_b, stay_b = small(split_second, (keep_y, got_y, keep_x, got_x), [two] * 4)
    got_a, got_b = x1(send_a), y1(send_b)

    def split_third(ins, outs):
        stay, got = (ins[0], ins[2]), (ins[1], ins[3])
        for z in range(4):
            total = stay[z // 2][z % 2].astype(F32) + got[z // 2][z % 2].astype(F32)
            outs[z][...] = total.astype(BF16)

    line = small(split_third, (stay_a, got_a, stay_b, got_b), [one] * 4)
    moe = line[0].astype(F32)
    for z, v in zip(zs, line[1:]):
        moe = moe + z(v).astype(F32)
    mixed_out = (mixed + moe).astype(BF16)
    return mixed_out, log_sum_exp, key_cache_out, value_cache_out


def solution(mesh):
    return jax.shard_map(
        on_device,
        mesh=mesh,
        in_specs=(
            P("seq", "tensor"),
            P("seq", "tensor"),
            P("seq", "tensor"),
            P("seq", None, "tensor"),
            P("seq", None, "tensor"),
            P("seq"),
            P("seq"),
            P(),
            P("seq", None, None),
            P("seq", None),
            P("seq", None),
            P("tensor", None),
            P(),
            P("seq", None, "tensor"),
            P("seq", None, "tensor"),
            P("seq", "tensor", None),
            P("seq", None),
            P("seq", None),
        ),
        out_specs=(
            P("seq", "tensor"),
            P("seq", "tensor"),
            P("seq", None, "tensor"),
            P("seq", None, "tensor"),
        ),
        check_vma=False,
    )
```

time: 394 us -> 171 us (0.43)
  blocking collectives: 242 us -> 0 us
  Pallas kernels: 0 us -> 61 us
  starting transfers between devices: 19.9 us -> 54.7 us
  matrix products: 32.2 us -> 0 us
  waiting for transfers between devices: 59.5 us -> 42.3 us
  between operations: 14.4 us -> 1.1 us
  other arithmetic: 16.5 us -> 5.39 us
    all_gather x2 -> x0, blocking collectives: 144 us -> none  [the longest x1 111 us: on_device(): lax.all_gather(accept_rows[None], 'seq', axis=0, tiled=True)]
    all_to_all x1 -> x0, blocking collectives: 97.6 us -> none  [on_device(): lax.all_to_all(send_rows, 'seq', split_axis=0, concat_axis=0, tiled=True)]
    pallas_call x0 -> x11, Pallas kernels: none -> 61 us  [the longest x1 14.6 us: on_device(): pl.pallas_call(functools.partial(far_kernel, counts=counts, n_out=n_out),...]
    ppermute x0 -> x49, starting transfers between devices: none -> 54.7 us  [hop(): return lambda v: lax.ppermute(v, axis, pairs)]
    ppermute x0 -> x49, waiting for transfers between devices: none -> 42.3 us  [hop(): return lambda v: lax.ppermute(v, axis, pairs)]
    dot_general x15 -> x0, matrix products: 32.2 us -> none  [the longest x1 4.99 us: expert_block(): jnp.einsum('gecd,edf->gecf', slot_rows, up_proj, preferred_element_type=j...]
    psum x1 -> x0, waiting for transfers between devices: 30.5 us -> none  [on_device(): lax.psum(partial_proj.astype(jnp.bfloat16), 'tensor').astype(jnp.float32)]
    all_to_all x4 -> x0, starting transfers between devices: 19.8 us -> none  [the longest x1 6.01 us: on_device(): lax.all_to_all(dest_max.astype(jnp.bfloat16), 'seq', split_axis=0, concat...]
  transfers between devices with their start and end apart: 6 -> 49, of which waited for: 4 -> 19; matrix products, arithmetic and copies ran while one was open for 5% -> 3% of each run, Pallas kernels for 0% -> 11%
where the time goes in v1:
time: 171 us; the launch traced here: 170 us
  Pallas kernels  61 us (36%)
  starting transfers between devices  54.7 us (32%)
  waiting for transfers between devices  42.3 us (25%)
  local copies, waits for them, and re-layouts  5.64 us (3%)
  other arithmetic  5.39 us (3%)
    ppermute x49, starting transfers between devices, hop(): return lambda v: lax.ppermute(v, axis, pairs)  54.7 us
    ppermute x49, waiting for transfers between devices, hop(): return lambda v: lax.ppermute(v, axis, pairs)  42.3 us
    pallas_call x1, Pallas kernels, on_device(): pl.pallas_call(functools.partial(far_kernel, counts=counts, n_out=n_out),...  14.6 us
    pallas_call x1, Pallas kernels, on_device(): pl.pallas_call(functools.partial(expert_kernel, layout=layout), grid=(exp...  12.6 us
    pallas_call x2, Pallas kernels, down(): pl.pallas_call(down_kernel, grid_spec=pltpu.PrefetchScalarGridSpec(num_sc...  9.26 us
    pallas_call x1, Pallas kernels, on_device(): pl.pallas_call(functools.partial(cache_kernel, counts=tuple((a.shape[0] f...  8.66 us
    pallas_call x3, Pallas kernels, small(): pl.pallas_call(functools.partial(add_kernel, body=body, n_in=len(ins)), o...  6.4 us
    unnamed x98, local copies, waits for them, and re-layouts  4.96 us
  transfers between devices with their start and end apart: 49, of which 19 were waited for; matrix products, arithmetic and copies ran while one was open for 3% of the time, Pallas kernels for 11%

profile of v1, /device:TPU:0, one launch (start us, length us, event | category | flops | bytes accessed | tf_op | source)
XLA Modules:
  0.0 170.1 jit_solution(13011655856200750046)
XLA Ops:
  0.7 3.0 %collective-permute-start.3 = (bf16[1,64,512]{2,1,0:T(8,128)(2,1)}, bf16[1,64,512]{2,1,0:T(8,128)(2,1)S(1)}, u32[]{:S(2)}, u32[]{:S(2)}) collective-permute-start(bf16[1,64,512]{2,1,0:T(8,128)(2,1)} %bitcast.13), channel_id=1, source_target_pairs={{0,4},{4,0},{8,12},{12,8},{16,20},{20,16},{24,28},{28,24},{1,5},{5... | collective-permute-start | bytes 196616 | tf_op jit(solution)/shard_map/ppermute | solution.py:358
  3.7 3.6 %collective-permute-start.2 = (bf16[1,64,512]{2,1,0:T(8,128)(2,1)}, bf16[1,64,512]{2,1,0:T(8,128)(2,1)S(1)}, u32[]{:S(2)}, u32[]{:S(2)}) collective-permute-start(bf16[1,64,512]{2,1,0:T(8,128)(2,1)} %bitcast.14), channel_id=1, source_target_pairs={{0,24},{4,28},{8,16},{12,20},{16,8},{20,12},{24,0},{28,4},{1,25},{... | collective-permute-start | bytes 196616 | tf_op jit(solution)/shard_map/ppermute | solution.py:358
  8.8 1.9 %collective-permute-done.2.refs_3_ = bf16[1,64,512]{2,1,0:T(8,128)(2,1)S(1)} collective-permute-done((bf16[1,64,512]{2,1,0:T(8,128)(2,1)}, bf16[1,64,512]{2,1,0:T(8,128)(2,1)S(1)}, u32[]{:S(2)}, u32[]{:S(2)}) %collective-permute-start.2) | collective-permute-done | bytes 65568 | tf_op jit(solution)/shard_map/ppermute | solution.py:358
  10.8 2.0 %collective-permute-done.1.refs_2_ = bf16[1,64,512]{2,1,0:T(8,128)(2,1)S(1)} collective-permute-done((bf16[1,64,512]{2,1,0:T(8,128)(2,1)}, bf16[1,64,512]{2,1,0:T(8,128)(2,1)S(1)}, u32[]{:S(2)}, u32[]{:S(2)}) %collective-permute-start.1) | collective-permute-done | bytes 65568 | tf_op jit(solution)/shard_map/ppermute | solution.py:358
  13.4 1.5 collective-permute-start.4
  14.9 1.3 multiply_subtract_fusion
  18.5 14.6 %far.1 = (bf16[1,64,640]{2,1,0:T(8,128)(2,1)}, bf16[1,64,640]{2,1,0:T(8,128)(2,1)}, bf16[1,64,640]{2,1,0:T(8,128)(2,1)}, bf16[1,64,640]{2,1,0:T(8,128)(2,1)}, bf...) custom-call(s32[12]{0:T(128)} %get-tuple-element.79.pos_ref, ...), custom_call_target="tpu_custom_call" | custom-call | tf_op jit(solution)/shard_map/far/pallas_call | solution.py:402
  33.4 3.1 %collective-permute-start.8 = (bf16[1,64,640]{2,1,0:T(8,128)(2,1)}, bf16[1,64,640]{2,1,0:T(8,128)(2,1)S(1)}, u32[]{:S(2)}, u32[]{:S(2)}) collective-permute-start(bf16[1,64,640]{2,1,0:T(8,128)(2,1)} %get-tuple-element.41), channel_id=1, source_target_pairs={{0,16},{4,20},{8,24},{12,28},{16,0},{20,4},{24,8},{28,12},{1,17},{... | collective-permute-start | bytes 245768 | tf_op jit(solution)/shard_map/ppermute | solution.py:358
  37.5 1.3 collective-permute-start.10
  38.8 4.0 %collective-permute-start.12 = (bf16[1,64,640]{2,1,0:T(8,128)(2,1)}, bf16[1,64,640]{2,1,0:T(8,128)(2,1)S(1)}, u32[]{:S(2)}, u32[]{:S(2)}) collective-permute-start(bf16[1,64,640]{2,1,0:T(8,128)(2,1)} %get-tuple-element.45), channel_id=1, source_target_pairs={{0,20},{4,16},{8,28},{12,24},{16,4},{20,0},{24,12},{28,8},{1,21},{... | collective-permute-start | bytes 245768 | tf_op jit(solution)/shard_map/ppermute | solution.py:358
  42.8 2.9 %collective-permute-start.13 = (bf16[1,64,640]{2,1,0:T(8,128)(2,1)}, bf16[1,64,640]{2,1,0:T(8,128)(2,1)S(1)}, u32[]{:S(2)}, u32[]{:S(2)}) collective-permute-start(bf16[1,64,640]{2,1,0:T(8,128)(2,1)} %get-tuple-element.46), channel_id=1, source_target_pairs={{0,28},{4,24},{8,20},{12,16},{16,12},{20,8},{24,4},{28,0},{1,29},{... | collective-permute-start | bytes 245768 | tf_op jit(solution)/shard_map/ppermute | solution.py:358
  47.0 2.6 %near.1 = (f32[64,512]{1,0:T(8,128)}, f32[64,512]{1,0:T(8,128)}, bf16[1,32,512]{2,1,0:T(8,128)(2,1)}) custom-call(bf16[64,512]{1,0:T(8,128)(2,1)} %q_ref.1, bf16[64,512]{1,0:T(8,128)(2,1)} %k_ref.1, bf16[64,512]{1,0:T(8,128)(2,1)} %v_ref.1, s32[1,64,64]{2,1,0:T(8,128)} %mask_ref.1, s32[8,1]{1,0:T(8,128)} %copy.24.acc_ref, ...), custom_call_target="tpu_custom_call" | custom-call | tf_op jit(solution)/shard_map/near/pallas_call | solution.py:380
  50.9 4.4 %merge.1 = (f32[64,4]{1,0:T(8,128)}, f32[64,512]{1,0:T(8,128)}, bf16[64,512]{1,0:T(8,128)(2,1)}, bf16[64,512]{1,0:T(8,128)(2,1)}, bf16[64,512]{1,0:T(8,128)(2,1)}) custom-call(s32[1]{0:T(128)} %bitcast.t_ref, f32[64,512]{1,0:T(8,128)} %get-tuple-element.37.near_ref, f32[64,512]{1,0:T(8,128)} %get-tuple-element.38.lse_ref, bf16[64,2048]{1,0:T(8,128)(2,1)} %hidden_ref.1, ...), custom_call_target="tpu_custom_call" | custom-call | tf_op jit(solution)/shard_map/merge/pallas_call | solution.py:430
  55.3 1.6 collective-permute-start.15
  57.2 2.9 %collective-permute-done.15 = bf16[64,512]{1,0:T(8,128)(2,1)S(1)} collective-permute-done((bf16[64,512]{1,0:T(8,128)(2,1)}, bf16[64,512]{1,0:T(8,128)(2,1)S(1)}, u32[]{:S(2)}, u32[]{:S(2)}) %collective-permute-start.15) | collective-permute-done | bytes 65568 | tf_op jit(solution)/shard_map/ppermute | solution.py:358
  60.0 1.2 collective-permute-done.16
  63.3 2.4 %collective-permute-start.19 = (bf16[1,32,512]{2,1,0:T(8,128)(2,1)S(1)}, bf16[1,32,512]{2,1,0:T(8,128)(2,1)S(1)}, u32[]{:S(2)}, u32[]{:S(2)}) collective-permute-start(bf16[1,32,512]{2,1,0:T(8,128)(2,1)S(1)} %copy-done.20), channel_id=1, source_target_pairs={{0,24},{4,28},{8,16},{12,20},{16,8},{20,12},{24,0},{28,4},{1,25},{... | collective-permute-start | bytes 98312 | tf_op jit(solution)/shard_map/ppermute | solution.py:358
  67.7 2.0 %collective-permute-start.25 = (bf16[1,64,512]{2,1,0:T(8,128)(2,1)S(1)}, bf16[1,64,512]{2,1,0:T(8,128)(2,1)S(1)}, u32[]{:S(2)}, u32[]{:S(2)}) collective-permute-start(bf16[1,64,512]{2,1,0:T(8,128)(2,1)S(1)} %convert_bitcast_fusion), channel_id=1, source_target_pairs={{0,16},{4,20},{8,24},{12,28},{16,0},{20,4},{24,8},{28,12},{1,17},{... | collective-permute-start | bytes 196616 | tf_op jit(solution)/shard_map/ppermute | solution.py:358
  69.7 4.0 %collective-permute-done.25 = bf16[1,64,512]{2,1,0:T(8,128)(2,1)S(1)} collective-permute-done((bf16[1,64,512]{2,1,0:T(8,128)(2,1)S(1)}, bf16[1,64,512]{2,1,0:T(8,128)(2,1)S(1)}, u32[]{:S(2)}, u32[]{:S(2)}) %collective-permute-start.25) | collective-permute-done | bytes 65568 | tf_op jit(solution)/shard_map/ppermute | solution.py:358
  73.7 2.3 %collective-permute-start.26 = (bf16[1,64,512]{2,1,0:T(8,128)(2,1)S(1)}, bf16[1,64,512]{2,1,0:T(8,128)(2,1)S(1)}, u32[]{:S(2)}, u32[]{:S(2)}) collective-permute-start(bf16[1,64,512]{2,1,0:T(8,128)(2,1)S(1)} %convert_bitcast_fusion), channel_id=1, source_target_pairs={{0,24},{4,28},{8,16},{12,20},{16,8},{20,12},{24,0},{28,4},{1,25},{... | collective-permute-start | bytes 196616 | tf_op jit(solution)/shard_map/ppermute | solution.py:358
  76.0 3.8 %collective-permute-done.26 = bf16[1,64,512]{2,1,0:T(8,128)(2,1)S(1)} collective-permute-done((bf16[1,64,512]{2,1,0:T(8,128)(2,1)S(1)}, bf16[1,64,512]{2,1,0:T(8,128)(2,1)S(1)}, u32[]{:S(2)}, u32[]{:S(2)}) %collective-permute-start.26) | collective-permute-done | bytes 65568 | tf_op jit(solution)/shard_map/ppermute | solution.py:358
  79.8 1.3 collective-permute-start.29
  81.1 1.8 %collective-permute-start.27 = (bf16[2,64,512]{2,1,0:T(8,128)(2,1)S(1)}, bf16[2,64,512]{2,1,0:T(8,128)(2,1)S(1)}, u32[]{:S(2)}, u32[]{:S(2)}) collective-permute-start(bf16[2,64,512]{2,1,0:T(8,128)(2,1)S(1)} %pad_maximum_fusion.refs_0_), channel_id=1, source_target_pairs={{0,4},{4,0},{8,12},{12,8},{16,20},{20,16},{24,28},{28,24},{1,5},{5... | collective-permute-start | bytes 393224 | tf_op jit(solution)/shard_map/ppermute | solution.py:358
  83.9 3.8 %collective-permute-done.23.refs_7_ = bf16[1,32,512]{2,1,0:T(8,128)(2,1)S(1)} collective-permute-done((bf16[1,32,512]{2,1,0:T(8,128)(2,1)S(1)}, bf16[1,32,512]{2,1,0:T(8,128)(2,1)S(1)}, u32[]{:S(2)}, u32[]{:S(2)}) %collective-permute-start.23) | collective-permute-done | bytes 32800 | tf_op jit(solution)/shard_map/ppermute | solution.py:358
  87.7 1.5 collective-permute-start.22
  89.2 2.4 %collective-permute-done.22.refs_6_ = bf16[1,32,512]{2,1,0:T(8,128)(2,1)S(1)} collective-permute-done((bf16[1,32,512]{2,1,0:T(8,128)(2,1)S(1)}, bf16[1,32,512]{2,1,0:T(8,128)(2,1)S(1)}, u32[]{:S(2)}, u32[]{:S(2)}) %collective-permute-start.22) | collective-permute-done | bytes 32800 | tf_op jit(solution)/shard_map/ppermute | solution.py:358
  91.6 1.5 collective-permute-start.21
  93.1 2.4 %collective-permute-done.21.refs_5_ = bf16[1,32,512]{2,1,0:T(8,128)(2,1)S(1)} collective-permute-done((bf16[1,32,512]{2,1,0:T(8,128)(2,1)S(1)}, bf16[1,32,512]{2,1,0:T(8,128)(2,1)S(1)}, u32[]{:S(2)}, u32[]{:S(2)}) %collective-permute-start.21) | collective-permute-done | bytes 32800 | tf_op jit(solution)/shard_map/ppermute | solution.py:358
  95.5 1.6 collective-permute-start.28
  99.0 2.9 %collective-permute-done.28.refs_3_ = bf16[2,64,512]{2,1,0:T(8,128)(2,1)S(1)} collective-permute-done((bf16[2,64,512]{2,1,0:T(8,128)(2,1)S(1)}, bf16[2,64,512]{2,1,0:T(8,128)(2,1)S(1)}, u32[]{:S(2)}, u32[]{:S(2)}) %collective-permute-start.28) | collective-permute-done | bytes 131104 | tf_op jit(solution)/shard_map/ppermute | solution.py:358
  103.1 1.2 collective-permute-done.32.refs_7_
  104.9 2.5 %slots.1 = (bf16[8,128,64]{2,1,0:T(8,128)(2,1)}, bf16[8,64,128]{2,1,0:T(8,128)(2,1)}, f32[8,128,128]{2,1,0:T(8,128)}) custom-call(s32[1]{0:T(128)} %bitcast.7.me_ref, bf16[1,32,512]{2,1,0:T(8,128)(2,1)} %get-tuple-element.51.refs_0_, bf16[1,32,512]{2,1,0:T(8,128)(2,1)} %copy-done.24, bf16[1,32,512]{2,1,0:T(8,128)(2,1)} %copy-done.23, ...), custom_call_target="tpu_custom_call" | custom-call | tf_op jit(solution)/shard_map/slots/pallas_call | solution.py:447
  108.2 12.6 %gate_up.1.active_ref = bf16[8,128,256]{2,1,0:T(8,128)(2,1)} custom-call(s32[1]{0:T(128)} %bitcast.t_ref, f32[1,2048]{1,0:T(1,128)} %bitcast.18, bf16[8,128,64]{2,1,0:T(8,128)(2,1)} %get-tuple-element.52.g_ref, f32[8,128,128]{2,1,0:T(8,128)} %get-tuple-element.53.rw_ref, bf16[8,2048,256]{2,1,0:T(8,128)(2,1)} %gate_ref.1, bf16[8,2048,256]{2,1,0:T(8,128)(2,1)} %up_ref.1, ...), custom_call_target="tpu_custom_call" | custom-call | tf_op jit(solution)/shard_map/gate_up/pallas_call | solution.py:497
  120.8 4.6 %down.3 = bf16[2,8,64,512]{3,2,1,0:T(8,128)(2,1)} custom-call(s32[2]{0:T(128)} %pad_add_fusion.1.cols_ref, bf16[8,128,256]{2,1,0:T(8,128)(2,1)} %gate_up.1.active_ref, bf16[8,64,128]{2,1,0:T(8,128)(2,1)} %get-tuple-element.54.c_ref, bf16[8,256,2048]{2,1,0:T(8,128)(2,1)} %down_ref.3), custom_call_target="tpu_custom_call" | custom-call | tf_op jit(solution)/shard_map/down/pallas_call | solution.py:518
  126.5 4.6 %down.2.refs_0_ = bf16[2,8,64,512]{3,2,1,0:T(8,128)(2,1)} custom-call(s32[2]{0:T(128)} %pad_add_fusion.cols_ref, bf16[8,128,256]{2,1,0:T(8,128)(2,1)} %gate_up.1.active_ref, bf16[8,64,128]{2,1,0:T(8,128)(2,1)} %get-tuple-element.54.c_ref, bf16[8,256,2048]{2,1,0:T(8,128)(2,1)} %down_ref.3), custom_call_target="tpu_custom_call" | custom-call | tf_op jit(solution)/shard_map/down/pallas_call | solution.py:518
  132.1 2.6 %shard_map.201 = (bf16[4,64,512]{2,1,0:T(8,128)(2,1)}, bf16[4,64,512]{2,1,0:T(8,128)(2,1)}, bf16[4,64,512]{2,1,0:T(8,128)(2,1)}, bf16[4,64,512]{2,1,0:T(8,128)(2,1)}) custom-call(bf16[2,8,64,512]{3,2,1,0:T(8,128)(2,1)} %down.2.refs_0_, bf16[2,8,64,512]{3,2,1,0:T(8,128)(2,1)} %copy-done), custom_call_target="tpu_custom_call" | custom-call | tf_op jit(solution)/shard_map/pallas_call | solution.py:314
  134.7 1.2 collective-permute-start.42
  135.9 1.3 collective-permute-start.43
  137.1 6.0 %collective-permute-done.42.refs_1_ = bf16[4,64,512]{2,1,0:T(8,128)(2,1)S(1)} collective-permute-done((bf16[4,64,512]{2,1,0:T(8,128)(2,1)}, bf16[4,64,512]{2,1,0:T(8,128)(2,1)S(1)}, u32[]{:S(2)}, u32[]{:S(2)}) %collective-permute-start.42) | collective-permute-done | bytes 262176 | tf_op jit(solution)/shard_map/ppermute | solution.py:358
  144.8 2.0 %shard_map.202 = (bf16[2,64,512]{2,1,0:T(8,128)(2,1)}, bf16[2,64,512]{2,1,0:T(8,128)(2,1)}, bf16[2,64,512]{2,1,0:T(8,128)(2,1)}, bf16[2,64,512]{2,1,0:T(8,128)(2,1)}) custom-call(bf16[4,64,512]{2,1,0:T(8,128)(2,1)} %get-tuple-element.55.refs_0_, bf16[4,64,512]{2,1,0:T(8,128)(2,1)} %copy-done.4, bf16[4,64,512]{2,1,0:T(8,128)(2,1)} %get-tuple-element.57.refs_2_, ...), custom_call_target="tpu_custom_call" | custom-call | tf_op jit(solution)/shard_map/pallas_call | solution.py:314
  146.8 1.3 collective-permute-start.44
  148.1 1.2 collective-permute-start.45
  149.2 2.8 %collective-permute-done.44.refs_1_ = bf16[2,64,512]{2,1,0:T(8,128)(2,1)S(1)} collective-permute-done((bf16[2,64,512]{2,1,0:T(8,128)(2,1)}, bf16[2,64,512]{2,1,0:T(8,128)(2,1)S(1)}, u32[]{:S(2)}, u32[]{:S(2)}) %collective-permute-start.44) | collective-permute-done | bytes 131104 | tf_op jit(solution)/shard_map/ppermute | solution.py:358
  152.0 1.2 collective-permute-done.45.refs_3_
  153.9 1.8 %shard_map.203 = (bf16[64,512]{1,0:T(8,128)(2,1)}, bf16[64,512]{1,0:T(8,128)(2,1)}, bf16[64,512]{1,0:T(8,128)(2,1)}, bf16[64,512]{1,0:T(8,128)(2,1)}) custom-call(bf16[2,64,512]{2,1,0:T(8,128)(2,1)} %get-tuple-element.59.refs_0_, bf16[2,64,512]{2,1,0:T(8,128)(2,1)} %copy-done.28, bf16[2,64,512]{2,1,0:T(8,128)(2,1)} %get-tuple-element.61.refs_2_, ...), custom_call_target="tpu_custom_call" | custom-call | tf_op jit(solution)/shard_map/pallas_call | solution.py:314
  155.7 1.9 %collective-permute-start.47 = (bf16[64,512]{1,0:T(8,128)(2,1)}, bf16[64,512]{1,0:T(8,128)(2,1)S(1)}, u32[]{:S(2)}, u32[]{:S(2)}) collective-permute-start(bf16[64,512]{1,0:T(8,128)(2,1)} %get-tuple-element.65), channel_id=1, source_target_pairs={{0,16},{4,20},{8,24},{12,28},{16,0},{20,4},{24,8},{28,12},{1,17},{... | collective-permute-start | bytes 196616 | tf_op jit(solution)/shard_map/ppermute | solution.py:358
  157.6 2.5 %collective-permute-start.48 = (bf16[64,512]{1,0:T(8,128)(2,1)}, bf16[64,512]{1,0:T(8,128)(2,1)S(1)}, u32[]{:S(2)}, u32[]{:S(2)}) collective-permute-start(bf16[64,512]{1,0:T(8,128)(2,1)} %get-tuple-element.66), channel_id=1, source_target_pairs={{0,24},{4,28},{8,16},{12,20},{16,8},{20,12},{24,0},{28,4},{1,25},{... | collective-permute-start | bytes 196616 | tf_op jit(solution)/shard_map/ppermute | solution.py:358
  160.1 8.7 %cache.1 = (bf16[12,128,512]{2,1,0:T(8,128)(2,1)}, bf16[12,128,512]{2,1,0:T(8,128)(2,1)}) custom-call(s32[12]{0:T(128)} %get-tuple-element.79.pos_ref, s32[12]{0:T(128)} %get-tuple-element.78.live_ref, bf16[12,128,512]{2,1,0:T(8,128)(2,1)} %key_ref.3, bf16[12,128,512]{2,1,0:T(8,128)(2,1)} %value_ref.3, bf16[1,32,512]{2,1,0:T(8,128)(2,1)} %get-tuple-element.51.refs_0_, ...), custom_call_target="tpu_custom_call" | custom-call | tf_op jit(solution)/shard_map/cache/pallas_call | solution.py:463
  (169 shorter events, 23.5 us)
Async XLA Ops:
  0.7 15.5 %collective-permute-start.3 = (bf16[1,64,512]{2,1,0:T(8,128)(2,1)}, bf16[1,64,512]{2,1,0:T(8,128)(2,1)S(1)}, u32[]{:S(2)}, u32[]{:S(2)}) collective-permute-start(bf16[1,64,512]{2,1,0:T(8,128)(2,1)} %bitcast.13), channel_id=1, source_target_pairs={{0,4},{4,0},{8,12},{12,8},{16,20},{20,16},{24,28},{28,24},{1,5},{5... | collective-permute-start | bytes 196616 | tf_op jit(solution)/shard_map/ppermute | solution.py:358
  3.7 7.1 %collective-permute-start.2 = (bf16[1,64,512]{2,1,0:T(8,128)(2,1)}, bf16[1,64,512]{2,1,0:T(8,128)(2,1)S(1)}, u32[]{:S(2)}, u32[]{:S(2)}) collective-permute-start(bf16[1,64,512]{2,1,0:T(8,128)(2,1)} %bitcast.14), channel_id=1, source_target_pairs={{0,24},{4,28},{8,16},{12,20},{16,8},{20,12},{24,0},{28,4},{1,25},{... | collective-permute-start | bytes 196616 | tf_op jit(solution)/shard_map/ppermute | solution.py:358
  7.3 5.6 %collective-permute-start.1 = (bf16[1,64,512]{2,1,0:T(8,128)(2,1)}, bf16[1,64,512]{2,1,0:T(8,128)(2,1)S(1)}, u32[]{:S(2)}, u32[]{:S(2)}) collective-permute-start(bf16[1,64,512]{2,1,0:T(8,128)(2,1)} %bitcast.15), channel_id=1, source_target_pairs={{0,16},{4,20},{8,24},{12,28},{16,0},{20,4},{24,8},{28,12},{1,17},{... | collective-permute-start | bytes 196616 | tf_op jit(solution)/shard_map/ppermute | solution.py:358
  7.3 6.2 %collective-permute-start = (bf16[1,64,512]{2,1,0:T(8,128)(2,1)}, bf16[1,64,512]{2,1,0:T(8,128)(2,1)S(1)}, u32[]{:S(2)}, u32[]{:S(2)}) collective-permute-start(bf16[1,64,512]{2,1,0:T(8,128)(2,1)} %bitcast.16), channel_id=1, source_target_pairs={{0,8},{4,12},{8,0},{12,4},{16,24},{20,28},{24,16},{28,20},{1,9},{5... | collective-permute-start | bytes 196616 | tf_op jit(solution)/shard_map/ppermute | solution.py:358
  10.7 5.4 %collective-permute-start.6 = (bf16[1,64,512]{2,1,0:T(8,128)(2,1)S(1)}, bf16[1,64,512]{2,1,0:T(8,128)(2,1)S(1)}, u32[]{:S(2)}, u32[]{:S(2)}) collective-permute-start(bf16[1,64,512]{2,1,0:T(8,128)(2,1)S(1)} %collective-permute-done.2.refs_3_), channel_id=1, source_target_pairs={{0,4},{4,0},{8,12},{12,8},{16,20},{20,16},{24,28},{28,24},{1,5},{5... | collective-permute-start | bytes 196616 | tf_op jit(solution)/shard_map/ppermute | solution.py:358
  12.9 4.3 %collective-permute-start.5 = (bf16[1,64,512]{2,1,0:T(8,128)(2,1)S(1)}, bf16[1,64,512]{2,1,0:T(8,128)(2,1)S(1)}, u32[]{:S(2)}, u32[]{:S(2)}) collective-permute-start(bf16[1,64,512]{2,1,0:T(8,128)(2,1)S(1)} %collective-permute-done.1.refs_2_), channel_id=1, source_target_pairs={{0,4},{4,0},{8,12},{12,8},{16,20},{20,16},{24,28},{28,24},{1,5},{5... | collective-permute-start | bytes 196616 | tf_op jit(solution)/shard_map/ppermute | solution.py:358
  13.4 4.4 %collective-permute-start.4 = (bf16[1,64,512]{2,1,0:T(8,128)(2,1)S(1)}, bf16[1,64,512]{2,1,0:T(8,128)(2,1)S(1)}, u32[]{:S(2)}, u32[]{:S(2)}) collective-permute-start(bf16[1,64,512]{2,1,0:T(8,128)(2,1)S(1)} %collective-permute-done.refs_1_), channel_id=1, source_target_pairs={{0,4},{4,0},{8,12},{12,8},{16,20},{20,16},{24,28},{28,24},{1,5},{5... | collective-permute-start | bytes 196616 | tf_op jit(solution)/shard_map/ppermute | solution.py:358
  33.1 5.7 %collective-permute-start.7 = (bf16[1,64,640]{2,1,0:T(8,128)(2,1)}, bf16[1,64,640]{2,1,0:T(8,128)(2,1)S(1)}, u32[]{:S(2)}, u32[]{:S(2)}) collective-permute-start(bf16[1,64,640]{2,1,0:T(8,128)(2,1)} %get-tuple-element.40), channel_id=1, source_target_pairs={{0,8},{4,12},{8,0},{12,4},{16,24},{20,28},{24,16},{28,20},{1,9},{5... | collective-permute-start | bytes 245768 | tf_op jit(solution)/shard_map/ppermute | solution.py:358
  33.4 9.5 %collective-permute-start.8 = (bf16[1,64,640]{2,1,0:T(8,128)(2,1)}, bf16[1,64,640]{2,1,0:T(8,128)(2,1)S(1)}, u32[]{:S(2)}, u32[]{:S(2)}) collective-permute-start(bf16[1,64,640]{2,1,0:T(8,128)(2,1)} %get-tuple-element.41), channel_id=1, source_target_pairs={{0,16},{4,20},{8,24},{12,28},{16,0},{20,4},{24,8},{28,12},{1,17},{... | collective-permute-start | bytes 245768 | tf_op jit(solution)/shard_map/ppermute | solution.py:358
  36.5 13.2 %collective-permute-start.9 = (bf16[1,64,640]{2,1,0:T(8,128)(2,1)}, bf16[1,64,640]{2,1,0:T(8,128)(2,1)S(1)}, u32[]{:S(2)}, u32[]{:S(2)}) collective-permute-start(bf16[1,64,640]{2,1,0:T(8,128)(2,1)} %get-tuple-element.42), channel_id=1, source_target_pairs={{0,24},{4,28},{8,16},{12,20},{16,8},{20,12},{24,0},{28,4},{1,25},{... | collective-permute-start | bytes 245768 | tf_op jit(solution)/shard_map/ppermute | solution.py:358
  37.5 12.2 %collective-permute-start.10 = (bf16[1,64,640]{2,1,0:T(8,128)(2,1)}, bf16[1,64,640]{2,1,0:T(8,128)(2,1)S(1)}, u32[]{:S(2)}, u32[]{:S(2)}) collective-permute-start(bf16[1,64,640]{2,1,0:T(8,128)(2,1)} %get-tuple-element.43), channel_id=1, source_target_pairs={{0,4},{4,0},{8,12},{12,8},{16,20},{20,16},{24,28},{28,24},{1,5},{5... | collective-permute-start | bytes 245768 | tf_op jit(solution)/shard_map/ppermute | solution.py:358
  38.8 10.9 %collective-permute-start.11 = (bf16[1,64,640]{2,1,0:T(8,128)(2,1)}, bf16[1,64,640]{2,1,0:T(8,128)(2,1)S(1)}, u32[]{:S(2)}, u32[]{:S(2)}) collective-permute-start(bf16[1,64,640]{2,1,0:T(8,128)(2,1)} %get-tuple-element.44), channel_id=1, source_target_pairs={{0,12},{4,8},{8,4},{12,0},{16,28},{20,24},{24,20},{28,16},{1,13},{... | collective-permute-start | bytes 245768 | tf_op jit(solution)/shard_map/ppermute | solution.py:358
  38.8 10.9 %collective-permute-start.12 = (bf16[1,64,640]{2,1,0:T(8,128)(2,1)}, bf16[1,64,640]{2,1,0:T(8,128)(2,1)S(1)}, u32[]{:S(2)}, u32[]{:S(2)}) collective-permute-start(bf16[1,64,640]{2,1,0:T(8,128)(2,1)} %get-tuple-element.45), channel_id=1, source_target_pairs={{0,20},{4,16},{8,28},{12,24},{16,4},{20,0},{24,12},{28,8},{1,21},{... | collective-permute-start | bytes 245768 | tf_op jit(solution)/shard_map/ppermute | solution.py:358
  42.8 7.5 %collective-permute-start.13 = (bf16[1,64,640]{2,1,0:T(8,128)(2,1)}, bf16[1,64,640]{2,1,0:T(8,128)(2,1)S(1)}, u32[]{:S(2)}, u32[]{:S(2)}) collective-permute-start(bf16[1,64,640]{2,1,0:T(8,128)(2,1)} %get-tuple-element.46), channel_id=1, source_target_pairs={{0,28},{4,24},{8,20},{12,16},{16,12},{20,8},{24,4},{28,0},{1,29},{... | collective-permute-start | bytes 245768 | tf_op jit(solution)/shard_map/ppermute | solution.py:358
  55.3 4.7 %collective-permute-start.15 = (bf16[64,512]{1,0:T(8,128)(2,1)}, bf16[64,512]{1,0:T(8,128)(2,1)S(1)}, u32[]{:S(2)}, u32[]{:S(2)}) collective-permute-start(bf16[64,512]{1,0:T(8,128)(2,1)} %get-tuple-element.49), channel_id=1, source_target_pairs={{0,2},{1,3},{2,0},{3,1},{4,6},{5,7},{6,4},{7,5},{8,10},{9,11},{10,... | collective-permute-start | bytes 196616 | tf_op jit(solution)/shard_map/ppermute | solution.py:358
  56.9 4.3 %collective-permute-start.16 = (bf16[64,512]{1,0:T(8,128)(2,1)}, bf16[64,512]{1,0:T(8,128)(2,1)S(1)}, u32[]{:S(2)}, u32[]{:S(2)}) collective-permute-start(bf16[64,512]{1,0:T(8,128)(2,1)} %get-tuple-element.50), channel_id=1, source_target_pairs={{0,3},{1,2},{2,1},{3,0},{4,7},{5,6},{6,5},{7,4},{8,11},{9,10},{10,... | collective-permute-start | bytes 196616 | tf_op jit(solution)/shard_map/ppermute | solution.py:358
  62.2 5.5 %collective-permute-start.24 = (bf16[1,64,512]{2,1,0:T(8,128)(2,1)S(1)}, bf16[1,64,512]{2,1,0:T(8,128)(2,1)S(1)}, u32[]{:S(2)}, u32[]{:S(2)}) collective-permute-start(bf16[1,64,512]{2,1,0:T(8,128)(2,1)S(1)} %convert_bitcast_fusion), channel_id=1, source_target_pairs={{0,8},{4,12},{8,0},{12,4},{16,24},{20,28},{24,16},{28,20},{1,9},{5... | collective-permute-start | bytes 196616 | tf_op jit(solution)/shard_map/ppermute | solution.py:358
  62.9 16.8 %collective-permute-start.20 = (bf16[1,32,512]{2,1,0:T(8,128)(2,1)S(1)}, bf16[1,32,512]{2,1,0:T(8,128)(2,1)S(1)}, u32[]{:S(2)}, u32[]{:S(2)}) collective-permute-start(bf16[1,32,512]{2,1,0:T(8,128)(2,1)S(1)} %copy-done.20), channel_id=1, source_target_pairs={{0,4},{4,0},{8,12},{12,8},{16,20},{20,16},{24,28},{28,24},{1,5},{5... | collective-permute-start | bytes 98312 | tf_op jit(solution)/shard_map/ppermute | solution.py:358
  63.3 17.8 %collective-permute-start.19 = (bf16[1,32,512]{2,1,0:T(8,128)(2,1)S(1)}, bf16[1,32,512]{2,1,0:T(8,128)(2,1)S(1)}, u32[]{:S(2)}, u32[]{:S(2)}) collective-permute-start(bf16[1,32,512]{2,1,0:T(8,128)(2,1)S(1)} %copy-done.20), channel_id=1, source_target_pairs={{0,24},{4,28},{8,16},{12,20},{16,8},{20,12},{24,0},{28,4},{1,25},{... | collective-permute-start | bytes 98312 | tf_op jit(solution)/shard_map/ppermute | solution.py:358
  65.7 17.2 %collective-permute-start.18 = (bf16[1,32,512]{2,1,0:T(8,128)(2,1)S(1)}, bf16[1,32,512]{2,1,0:T(8,128)(2,1)S(1)}, u32[]{:S(2)}, u32[]{:S(2)}) collective-permute-start(bf16[1,32,512]{2,1,0:T(8,128)(2,1)S(1)} %copy-done.20), channel_id=1, source_target_pairs={{0,16},{4,20},{8,24},{12,28},{16,0},{20,4},{24,8},{28,12},{1,17},{... | collective-permute-start | bytes 98312 | tf_op jit(solution)/shard_map/ppermute | solution.py:358
  66.7 17.1 %collective-permute-start.17 = (bf16[1,32,512]{2,1,0:T(8,128)(2,1)S(1)}, bf16[1,32,512]{2,1,0:T(8,128)(2,1)S(1)}, u32[]{:S(2)}, u32[]{:S(2)}) collective-permute-start(bf16[1,32,512]{2,1,0:T(8,128)(2,1)S(1)} %copy-done.20), channel_id=1, source_target_pairs={{0,8},{4,12},{8,0},{12,4},{16,24},{20,28},{24,16},{28,20},{1,9},{5... | collective-permute-start | bytes 98312 | tf_op jit(solution)/shard_map/ppermute | solution.py:358
  67.7 6.0 %collective-permute-start.25 = (bf16[1,64,512]{2,1,0:T(8,128)(2,1)S(1)}, bf16[1,64,512]{2,1,0:T(8,128)(2,1)S(1)}, u32[]{:S(2)}, u32[]{:S(2)}) collective-permute-start(bf16[1,64,512]{2,1,0:T(8,128)(2,1)S(1)} %convert_bitcast_fusion), channel_id=1, source_target_pairs={{0,16},{4,20},{8,24},{12,28},{16,0},{20,4},{24,8},{28,12},{1,17},{... | collective-permute-start | bytes 196616 | tf_op jit(solution)/shard_map/ppermute | solution.py:358
  73.7 6.1 %collective-permute-start.26 = (bf16[1,64,512]{2,1,0:T(8,128)(2,1)S(1)}, bf16[1,64,512]{2,1,0:T(8,128)(2,1)S(1)}, u32[]{:S(2)}, u32[]{:S(2)}) collective-permute-start(bf16[1,64,512]{2,1,0:T(8,128)(2,1)S(1)} %convert_bitcast_fusion), channel_id=1, source_target_pairs={{0,24},{4,28},{8,16},{12,20},{16,8},{20,12},{24,0},{28,4},{1,25},{... | collective-permute-start | bytes 196616 | tf_op jit(solution)/shard_map/ppermute | solution.py:358
  79.7 15.8 %collective-permute-start.33 = (bf16[2,64,512]{2,1,0:T(8,128)(2,1)S(1)}, bf16[2,64,512]{2,1,0:T(8,128)(2,1)S(1)}, u32[]{:S(2)}, u32[]{:S(2)}) collective-permute-start(bf16[2,64,512]{2,1,0:T(8,128)(2,1)S(1)} %pad_maximum_fusion.refs_0_), channel_id=1, source_target_pairs={{0,1},{1,0},{2,3},{3,2},{4,5},{5,4},{6,7},{7,6},{8,9},{9,8},{10,11... | collective-permute-start | bytes 393224 | tf_op jit(solution)/shard_map/ppermute | solution.py:358
  79.8 17.4 %collective-permute-start.29 = (bf16[2,64,512]{2,1,0:T(8,128)(2,1)S(1)}, bf16[2,64,512]{2,1,0:T(8,128)(2,1)S(1)}, u32[]{:S(2)}, u32[]{:S(2)}) collective-permute-start(bf16[2,64,512]{2,1,0:T(8,128)(2,1)S(1)} %pad_maximum_fusion.refs_0_), channel_id=1, source_target_pairs={{0,2},{1,3},{2,0},{3,1},{4,6},{5,7},{6,4},{7,5},{8,10},{9,11},{10,... | collective-permute-start | bytes 393224 | tf_op jit(solution)/shard_map/ppermute | solution.py:358
  81.1 16.2 %collective-permute-start.27 = (bf16[2,64,512]{2,1,0:T(8,128)(2,1)S(1)}, bf16[2,64,512]{2,1,0:T(8,128)(2,1)S(1)}, u32[]{:S(2)}, u32[]{:S(2)}) collective-permute-start(bf16[2,64,512]{2,1,0:T(8,128)(2,1)S(1)} %pad_maximum_fusion.refs_0_), channel_id=1, source_target_pairs={{0,4},{4,0},{8,12},{12,8},{16,20},{20,16},{24,28},{28,24},{1,5},{5... | collective-permute-start | bytes 393224 | tf_op jit(solution)/shard_map/ppermute | solution.py:358
  82.9 15.3 %collective-permute-start.30 = (bf16[2,64,512]{2,1,0:T(8,128)(2,1)S(1)}, bf16[2,64,512]{2,1,0:T(8,128)(2,1)S(1)}, u32[]{:S(2)}, u32[]{:S(2)}) collective-permute-start(bf16[2,64,512]{2,1,0:T(8,128)(2,1)S(1)} %constant_dynamic-update-slice_fusion.refs_1_), channel_id=1, source_target_pairs={{0,2},{1,3},{2,0},{3,1},{4,6},{5,7},{6,4},{7,5},{8,10},{9,11},{10,... | collective-permute-start | bytes 393224 | tf_op jit(solution)/shard_map/ppermute | solution.py:358
  83.8 3.9 %collective-permute-start.23 = (bf16[1,32,512]{2,1,0:T(8,128)(2,1)S(1)}, bf16[1,32,512]{2,1,0:T(8,128)(2,1)S(1)}, u32[]{:S(2)}, u32[]{:S(2)}) collective-permute-start(bf16[1,32,512]{2,1,0:T(8,128)(2,1)S(1)} %collective-permute-done.19.refs_3_), channel_id=1, source_target_pairs={{0,4},{4,0},{8,12},{12,8},{16,20},{20,16},{24,28},{28,24},{1,5},{5... | collective-permute-start | bytes 98312 | tf_op jit(solution)/shard_map/ppermute | solution.py:358
  87.7 3.9 %collective-permute-start.22 = (bf16[1,32,512]{2,1,0:T(8,128)(2,1)S(1)}, bf16[1,32,512]{2,1,0:T(8,128)(2,1)S(1)}, u32[]{:S(2)}, u32[]{:S(2)}) collective-permute-start(bf16[1,32,512]{2,1,0:T(8,128)(2,1)S(1)} %collective-permute-done.18.refs_2_), channel_id=1, source_target_pairs={{0,4},{4,0},{8,12},{12,8},{16,20},{20,16},{24,28},{28,24},{1,5},{5... | collective-permute-start | bytes 98312 | tf_op jit(solution)/shard_map/ppermute | solution.py:358
  91.6 3.9 %collective-permute-start.21 = (bf16[1,32,512]{2,1,0:T(8,128)(2,1)S(1)}, bf16[1,32,512]{2,1,0:T(8,128)(2,1)S(1)}, u32[]{:S(2)}, u32[]{:S(2)}) collective-permute-start(bf16[1,32,512]{2,1,0:T(8,128)(2,1)S(1)} %collective-permute-done.17.refs_1_), channel_id=1, source_target_pairs={{0,4},{4,0},{8,12},{12,8},{16,20},{20,16},{24,28},{28,24},{1,5},{5... | collective-permute-start | bytes 98312 | tf_op jit(solution)/shard_map/ppermute | solution.py:358
  95.5 3.5 %collective-permute-start.34 = (bf16[2,64,512]{2,1,0:T(8,128)(2,1)S(1)}, bf16[2,64,512]{2,1,0:T(8,128)(2,1)S(1)}, u32[]{:S(2)}, u32[]{:S(2)}) collective-permute-start(bf16[2,64,512]{2,1,0:T(8,128)(2,1)S(1)} %constant_dynamic-update-slice_fusion.refs_1_), channel_id=1, source_target_pairs={{0,1},{1,0},{2,3},{3,2},{4,5},{5,4},{6,7},{7,6},{8,9},{9,8},{10,11... | collective-permute-start | bytes 393224 | tf_op jit(solution)/shard_map/ppermute | solution.py:358
  95.5 6.4 %collective-permute-start.28 = (bf16[2,64,512]{2,1,0:T(8,128)(2,1)S(1)}, bf16[2,64,512]{2,1,0:T(8,128)(2,1)S(1)}, u32[]{:S(2)}, u32[]{:S(2)}) collective-permute-start(bf16[2,64,512]{2,1,0:T(8,128)(2,1)S(1)} %constant_dynamic-update-slice_fusion.refs_1_), channel_id=1, source_target_pairs={{0,4},{4,0},{8,12},{12,8},{16,20},{20,16},{24,28},{28,24},{1,5},{5... | collective-permute-start | bytes 393224 | tf_op jit(solution)/shard_map/ppermute | solution.py:358
  97.1 4.8 %collective-permute-start.37 = (bf16[2,64,512]{2,1,0:T(8,128)(2,1)S(1)}, bf16[2,64,512]{2,1,0:T(8,128)(2,1)S(1)}, u32[]{:S(2)}, u32[]{:S(2)}) collective-permute-start(bf16[2,64,512]{2,1,0:T(8,128)(2,1)S(1)} %collective-permute-done.29.refs_4_), channel_id=1, source_target_pairs={{0,1},{1,0},{2,3},{3,2},{4,5},{5,4},{6,7},{7,6},{8,9},{9,8},{10,11... | collective-permute-start | bytes 393224 | tf_op jit(solution)/shard_map/ppermute | solution.py:358
  97.3 5.7 %collective-permute-start.31 = (bf16[2,64,512]{2,1,0:T(8,128)(2,1)S(1)}, bf16[2,64,512]{2,1,0:T(8,128)(2,1)S(1)}, u32[]{:S(2)}, u32[]{:S(2)}) collective-permute-start(bf16[2,64,512]{2,1,0:T(8,128)(2,1)S(1)} %collective-permute-done.27.refs_2_), channel_id=1, source_target_pairs={{0,2},{1,3},{2,0},{3,1},{4,6},{5,7},{6,4},{7,5},{8,10},{9,11},{10,... | collective-permute-start | bytes 393224 | tf_op jit(solution)/shard_map/ppermute | solution.py:358
  98.2 6.1 %collective-permute-start.32 = (bf16[2,64,512]{2,1,0:T(8,128)(2,1)S(1)}, bf16[2,64,512]{2,1,0:T(8,128)(2,1)S(1)}, u32[]{:S(2)}, u32[]{:S(2)}) collective-permute-start(bf16[2,64,512]{2,1,0:T(8,128)(2,1)S(1)} %collective-permute-done.30.refs_5_), channel_id=1, source_target_pairs={{0,4},{4,0},{8,12},{12,8},{16,20},{20,16},{24,28},{28,24},{1,5},{5... | collective-permute-start | bytes 393224 | tf_op jit(solution)/shard_map/ppermute | solution.py:358
  99.0 8.4 %collective-permute-start.35 = (bf16[2,64,512]{2,1,0:T(8,128)(2,1)S(1)}, bf16[2,64,512]{2,1,0:T(8,128)(2,1)S(1)}, u32[]{:S(2)}, u32[]{:S(2)}) collective-permute-start(bf16[2,64,512]{2,1,0:T(8,128)(2,1)S(1)} %collective-permute-done.27.refs_2_), channel_id=1, source_target_pairs={{0,1},{1,0},{2,3},{3,2},{4,5},{5,4},{6,7},{7,6},{8,9},{9,8},{10,11... | collective-permute-start | bytes 393224 | tf_op jit(solution)/shard_map/ppermute | solution.py:358
  101.9 5.5 %collective-permute-start.38 = (bf16[2,64,512]{2,1,0:T(8,128)(2,1)S(1)}, bf16[2,64,512]{2,1,0:T(8,128)(2,1)S(1)}, u32[]{:S(2)}, u32[]{:S(2)}) collective-permute-start(bf16[2,64,512]{2,1,0:T(8,128)(2,1)S(1)} %collective-permute-done.30.refs_5_), channel_id=1, source_target_pairs={{0,1},{1,0},{2,3},{3,2},{4,5},{5,4},{6,7},{7,6},{8,9},{9,8},{10,11... | collective-permute-start | bytes 393224 | tf_op jit(solution)/shard_map/ppermute | solution.py:358
  101.9 5.5 %collective-permute-start.36 = (bf16[2,64,512]{2,1,0:T(8,128)(2,1)S(1)}, bf16[2,64,512]{2,1,0:T(8,128)(2,1)S(1)}, u32[]{:S(2)}, u32[]{:S(2)}) collective-permute-start(bf16[2,64,512]{2,1,0:T(8,128)(2,1)S(1)} %collective-permute-done.28.refs_3_), channel_id=1, source_target_pairs={{0,1},{1,0},{2,3},{3,2},{4,5},{5,4},{6,7},{7,6},{8,9},{9,8},{10,11... | collective-permute-start | bytes 393224 | tf_op jit(solution)/shard_map/ppermute | solution.py:358
  103.1 4.4 %collective-permute-start.39 = (bf16[2,64,512]{2,1,0:T(8,128)(2,1)S(1)}, bf16[2,64,512]{2,1,0:T(8,128)(2,1)S(1)}, u32[]{:S(2)}, u32[]{:S(2)}) collective-permute-start(bf16[2,64,512]{2,1,0:T(8,128)(2,1)S(1)} %collective-permute-done.31.refs_6_), channel_id=1, source_target_pairs={{0,1},{1,0},{2,3},{3,2},{4,5},{5,4},{6,7},{7,6},{8,9},{9,8},{10,11... | collective-permute-start | bytes 393224 | tf_op jit(solution)/shard_map/ppermute | solution.py:358
  104.3 3.2 %collective-permute-start.40 = (bf16[2,64,512]{2,1,0:T(8,128)(2,1)S(1)}, bf16[2,64,512]{2,1,0:T(8,128)(2,1)S(1)}, u32[]{:S(2)}, u32[]{:S(2)}) collective-permute-start(bf16[2,64,512]{2,1,0:T(8,128)(2,1)S(1)} %collective-permute-done.32.refs_7_), channel_id=1, source_target_pairs={{0,1},{1,0},{2,3},{3,2},{4,5},{5,4},{6,7},{7,6},{8,9},{9,8},{10,11... | collective-permute-start | bytes 393224 | tf_op jit(solution)/shard_map/ppermute | solution.py:358
  125.5 5.7 %collective-permute-start.41 = (bf16[2,8,64,512]{3,2,1,0:T(8,128)(2,1)}, bf16[2,8,64,512]{3,2,1,0:T(8,128)(2,1)S(1)}, u32[]{:S(2)}, u32[]{:S(2)}) collective-permute-start(bf16[2,8,64,512]{3,2,1,0:T(8,128)(2,1)} %down.3), channel_id=1, source_target_pairs={{0,1},{1,0},{2,3},{3,2},{4,5},{5,4},{6,7},{7,6},{8,9},{9,8},{10,11... | collective-permute-start | bytes 3145736 | tf_op jit(solution)/shard_map/ppermute | solution.py:358
  134.7 8.5 %collective-permute-start.42 = (bf16[4,64,512]{2,1,0:T(8,128)(2,1)}, bf16[4,64,512]{2,1,0:T(8,128)(2,1)S(1)}, u32[]{:S(2)}, u32[]{:S(2)}) collective-permute-start(bf16[4,64,512]{2,1,0:T(8,128)(2,1)} %get-tuple-element.56), channel_id=1, source_target_pairs={{0,2},{1,3},{2,0},{3,1},{4,6},{5,7},{6,4},{7,5},{8,10},{9,11},{10,... | collective-permute-start | bytes 786440 | tf_op jit(solution)/shard_map/ppermute | solution.py:358
  135.9 8.2 %collective-permute-start.43 = (bf16[4,64,512]{2,1,0:T(8,128)(2,1)}, bf16[4,64,512]{2,1,0:T(8,128)(2,1)S(1)}, u32[]{:S(2)}, u32[]{:S(2)}) collective-permute-start(bf16[4,64,512]{2,1,0:T(8,128)(2,1)} %get-tuple-element.58), channel_id=1, source_target_pairs={{0,4},{4,0},{8,12},{12,8},{16,20},{20,16},{24,28},{28,24},{1,5},{5... | collective-permute-start | bytes 786440 | tf_op jit(solution)/shard_map/ppermute | solution.py:358
  146.8 5.2 %collective-permute-start.44 = (bf16[2,64,512]{2,1,0:T(8,128)(2,1)}, bf16[2,64,512]{2,1,0:T(8,128)(2,1)S(1)}, u32[]{:S(2)}, u32[]{:S(2)}) collective-permute-start(bf16[2,64,512]{2,1,0:T(8,128)(2,1)} %get-tuple-element.60), channel_id=1, source_target_pairs={{0,4},{4,0},{8,12},{12,8},{16,20},{20,16},{24,28},{28,24},{1,5},{5... | collective-permute-start | bytes 393224 | tf_op jit(solution)/shard_map/ppermute | solution.py:358
  148.1 5.2 %collective-permute-start.45 = (bf16[2,64,512]{2,1,0:T(8,128)(2,1)}, bf16[2,64,512]{2,1,0:T(8,128)(2,1)S(1)}, u32[]{:S(2)}, u32[]{:S(2)}) collective-permute-start(bf16[2,64,512]{2,1,0:T(8,128)(2,1)} %get-tuple-element.62), channel_id=1, source_target_pairs={{0,2},{1,3},{2,0},{3,1},{4,6},{5,7},{6,4},{7,5},{8,10},{9,11},{10,... | collective-permute-start | bytes 393224 | tf_op jit(solution)/shard_map/ppermute | solution.py:358
  155.7 13.7 %collective-permute-start.46 = (bf16[64,512]{1,0:T(8,128)(2,1)}, bf16[64,512]{1,0:T(8,128)(2,1)S(1)}, u32[]{:S(2)}, u32[]{:S(2)}) collective-permute-start(bf16[64,512]{1,0:T(8,128)(2,1)} %get-tuple-element.64), channel_id=1, source_target_pairs={{0,8},{4,12},{8,0},{12,4},{16,24},{20,28},{24,16},{28,20},{1,9},{5... | collective-permute-start | bytes 196616 | tf_op jit(solution)/shard_map/ppermute | solution.py:358
  155.7 13.7 %collective-permute-start.47 = (bf16[64,512]{1,0:T(8,128)(2,1)}, bf16[64,512]{1,0:T(8,128)(2,1)S(1)}, u32[]{:S(2)}, u32[]{:S(2)}) collective-permute-start(bf16[64,512]{1,0:T(8,128)(2,1)} %get-tuple-element.65), channel_id=1, source_target_pairs={{0,16},{4,20},{8,24},{12,28},{16,0},{20,4},{24,8},{28,12},{1,17},{... | collective-permute-start | bytes 196616 | tf_op jit(solution)/shard_map/ppermute | solution.py:358
  157.6 11.8 %collective-permute-start.48 = (bf16[64,512]{1,0:T(8,128)(2,1)}, bf16[64,512]{1,0:T(8,128)(2,1)S(1)}, u32[]{:S(2)}, u32[]{:S(2)}) collective-permute-start(bf16[64,512]{1,0:T(8,128)(2,1)} %get-tuple-element.66), channel_id=1, source_target_pairs={{0,24},{4,28},{8,16},{12,20},{16,8},{20,12},{24,0},{28,4},{1,25},{... | collective-permute-start | bytes 196616 | tf_op jit(solution)/shard_map/ppermute | solution.py:358
  (49 other events, 482.4 us)

commit v2 on v1

v2 whole, which is shorter than its diff:
```python
import functools
import math

import jax
import jax.numpy as jnp
from jax import lax
from jax.experimental import pallas as pl
from jax.experimental.pallas import tpu as pltpu
from jax.sharding import PartitionSpec as P

HD = 128
CAP = 16
MASKED = -1e30
F32 = jnp.float32
BF16 = jnp.bfloat16
I32 = jnp.int32
STAT = 128
INFO = 16
EXTRA = 256
MIB = 1024 * 1024


def vmem():
    return pl.BlockSpec(memory_space=pltpu.VMEM)


def hbm():
    return pl.BlockSpec(memory_space=pltpu.HBM)


def smem():
    return pl.BlockSpec(memory_space=pltpu.SMEM)


def shape(dims, dtype):
    return jax.ShapeDtypeStruct(dims, dtype)


def in_hbm(v):
    return pltpu.with_memory_space_constraint(v, pltpu.HBM)


def call(kernel, name, ins, in_specs, out_shape, out_specs, scratch=(), limit=16, busy=3):
    ins = [
        in_hbm(v) if spec.memory_space is pltpu.HBM else v
        for v, spec in zip(ins, in_specs)
    ]
    return pl.pallas_call(
        kernel,
        out_shape=out_shape,
        in_specs=in_specs,
        out_specs=out_specs,
        scratch_shapes=list(scratch),
        compiler_params=pltpu.CompilerParams(vmem_limit_bytes=limit * MIB),
        cost_estimate=pl.CostEstimate(flops=0, bytes_accessed=busy * 3_000_000, transcendentals=0),
        name=name,
    )(*ins)


def each(count, body):
    if count <= 16:
        for i in range(count):
            body(i)
    else:

        @pl.loop(0, count)
        def _(i):
            body(i)


def dot(a, b):
    return jnp.dot(a, b, preferred_element_type=F32)


def dot_t(a, b):
    return lax.dot_general(a, b, (((1,), (1,)), ((), ())), preferred_element_type=F32)


def aligned(index, size):
    return index * size if isinstance(index, int) else pl.multiple_of(index * size, size)


def three_parts(value):
    high = value.astype(BF16).astype(F32)
    rest = value - high
    middle = rest.astype(BF16).astype(F32)
    return high, middle, rest - middle


def near_kernel(
    q_hbm, k_hbm, v_hbm, mask_hbm, key_hbm, value_hbm, acc_ref, ids_ref, rw_ref, *refs
):
    out_ref, lse_ref, info_ref, key_ref, value_ref, q_ref, k_ref, v_ref, mask_ref, s_s, w_s, sems = refs
    loads = [
        pltpu.make_async_copy(source, target, sems.at[i])
        for i, (source, target) in enumerate(
            (
                (q_hbm, q_ref),
                (k_hbm, k_ref),
                (v_hbm, v_ref),
                (mask_hbm, mask_ref),
                (key_hbm, key_ref),
                (value_hbm, value_ref),
            )
        )
    ]
    for load in loads:
        load.start()
    for load in loads[:4]:
        load.wait()
    draft, width = q_ref.shape
    scaling = 1.0 / math.sqrt(HD)
    seen = mask_ref[0] > 0
    heads = [slice(h * HD, (h + 1) * HD) for h in range(width // HD)]
    for h, cols in enumerate(heads):
        s_s[h] = jnp.where(seen, dot_t(q_ref[:, cols], k_ref[:, cols]) * scaling, MASKED)
    for h, cols in enumerate(heads):
        lse_ref[:, cols] = jnp.broadcast_to(jnp.max(s_s[h], axis=1, keepdims=True), (draft, HD))
    for h, cols in enumerate(heads):
        top = lse_ref[:, cols]
        weights = jnp.exp(s_s[h] - top[:, 0:draft])
        total = jnp.sum(weights, axis=1, keepdims=True)
        w_s[h] = (weights / total).astype(BF16)
        lse_ref[:, cols] = top + jnp.log(jnp.broadcast_to(total, (draft, HD)))
    for h, cols in enumerate(heads):
        out_ref[:, cols] = dot(w_s[h], v_ref[:, cols])
    accepted = acc_ref.shape[0]
    pick = (lax.broadcasted_iota(I32, (accepted, draft), 1) == acc_ref[...]).astype(F32).astype(BF16)
    rows = jnp.concatenate([dot(pick, k_ref[...]), dot(pick, v_ref[...])], axis=0)
    picks = ids_ref.shape[1]
    info = jnp.zeros((draft, STAT), F32)
    for g, part in enumerate((ids_ref[...].astype(F32), *three_parts(rw_ref[...]))):
        lane = lax.broadcasted_iota(I32, (picks, STAT), 1) - INFO - g * picks
        spread = jnp.where(lane == lax.broadcasted_iota(I32, (picks, STAT), 0), 1.0, 0.0)
        info = info + dot(part.astype(BF16), spread.astype(BF16))
    info_ref[:, 0:STAT] = info
    for g in range(width // 128):
        part = rows[:, g * 128 : (g + 1) * 128]
        info_ref[g * 2 * accepted : (g + 1) * 2 * accepted, STAT:] = part
    for load in loads[4:]:
        load.wait()


def far_kernel(pos_ref, live_ref, key_ref, value_ref, info_ref, *refs, counts, n_out):
    pieces, outs = refs[: len(counts)], refs[len(counts) : len(counts) + n_out]
    q_s, s_s, mp_s, lp_s, op_s, m_s, l_s, o_s = refs[len(counts) + n_out :]
    pages, page_len, width = key_ref.shape
    draft = q_s.shape[1]
    heads = width // HD
    scaling = 1.0 / math.sqrt(HD)
    at = 0
    for piece, count in zip(pieces, counts):
        q_s[at : at + count] = piece[...]
        at += count
    cell = lax.broadcasted_iota(I32, (draft, page_len), 1)
    pairs = [(p, slice(h * HD, (h + 1) * HD)) for p in range(pages) for h in range(heads)]
    for p, cols in pairs:
        scores = dot_t(q_s[pos_ref[p], :, cols], key_ref[p, :, cols]) * scaling
        s_s[p, :, cols] = jnp.where(cell < live_ref[p], scores, MASKED)
    for p, cols in pairs:
        mp_s[p, :, cols] = jnp.broadcast_to(jnp.max(s_s[p, :, cols], axis=1, keepdims=True), (draft, HD))
    for p, cols in pairs:
        weights = jnp.exp(s_s[p, :, cols] - mp_s[p, :, cols])
        lp_s[p, :, cols] = jnp.broadcast_to(jnp.sum(weights, axis=1, keepdims=True), (draft, HD))
        op_s[p, :, cols] = dot(weights.astype(BF16), value_ref[p, :, cols])

    def clear(i):
        m_s[i] = jnp.full((draft, width), MASKED, F32)
        l_s[i] = jnp.zeros((draft, width), F32)
        o_s[i] = jnp.zeros((draft, width), F32)

    each(at, clear)
    for p in range(pages):
        pos = pos_ref[p]
        m_s[pos] = jnp.maximum(m_s[pos], mp_s[p])
    for p in range(pages):
        pos = pos_ref[p]
        scale = jnp.exp(mp_s[p] - m_s[pos])
        l_s[pos] = l_s[pos] + lp_s[p] * scale
        o_s[pos] = o_s[pos] + op_s[p] * scale
    lane = lax.broadcasted_iota(I32, (draft, STAT), 1)

    def finish(i):
        target, row = (outs[i], 0) if n_out > 1 else (outs[0], i)
        stat = jnp.zeros((draft, STAT), F32)
        for h in range(heads):
            cols = slice(h * HD, (h + 1) * HD)
            total = l_s[i, :, cols]
            some = total > 0.0
            safe = jnp.where(some, total, 1.0)
            target[row, :, cols] = (o_s[i, :, cols] / safe).astype(BF16)
            lse = jnp.where(some, m_s[i, :, cols] + jnp.log(safe), MASKED)
            stat = jnp.where(lane % heads == h, lse, stat)
        high, middle, low = three_parts(stat)
        packed = jnp.where(lane < heads, high, jnp.where(lane < 2 * heads, middle, low))
        packed = jnp.where(lane < 3 * heads, packed, info_ref[:, 0:STAT])
        target[row, :, width : width + STAT] = packed.astype(BF16)
        target[row, :, width + STAT :] = info_ref[:, STAT:].astype(BF16)

    each(at, finish)


def merge_kernel(t_ref, near_ref, lse_ref, hidden_ref, w_ref, *refs, counts, n_out):
    pieces, refs = refs[: len(counts)], refs[len(counts) :]
    lse_out, outs = refs[0], refs[1:]
    draft, width = near_ref.shape
    heads = width // HD
    rows = [(piece, i) for piece, count in zip(pieces, counts) for i in range(count)]
    stats = []
    for piece, i in rows:
        packed = piece[i, :, width : width + STAT].astype(F32)
        stats.append(packed + pltpu.roll(packed, STAT - heads, 1) + pltpu.roll(packed, STAT - 2 * heads, 1))
    attended = []
    for h in range(heads):
        cols = slice(h * HD, (h + 1) * HD)
        sums = [s[:, h : h + 1] for s in stats]
        own = lse_ref[:, h * HD : h * HD + 1]
        top = functools.reduce(jnp.maximum, sums, own)
        weight = jnp.exp(own - top)
        total = weight
        summed = near_ref[:, cols] * weight
        for (piece, i), s in zip(rows, sums):
            weight = jnp.exp(s - top)
            total = total + weight
            summed = summed + piece[i, :, cols].astype(F32) * weight
        attended.append((summed / total).astype(BF16))
        lse_out[:, h : h + 1] = top + jnp.log(total)
    attended = jnp.concatenate(attended, axis=1)
    if n_out == 1:
        outs[0][...] = dot(attended, w_ref[...]).astype(outs[0].dtype)
        return
    for n in range(n_out):
        start = pl.multiple_of((t_ref[0] ^ n) * width, width)
        part = dot(attended, w_ref[:, pl.ds(start, width)])
        if n == 0:
            part = part + hidden_ref[:, pl.ds(start, width)].astype(F32)
        outs[n][...] = part.astype(outs[n].dtype)


def slots_kernel(me_ref, after_hbm, *refs, counts, picks, at_column):
    pieces, (g_ref, c_ref, w_ref) = refs[: len(counts)], refs[len(counts) :]
    draft = g_ref.shape[2]
    experts = w_ref.shape[0]
    row, column = (lax.broadcasted_iota(I32, (draft, draft), axis) for axis in (0, 1))
    upper = jnp.where(row < column, 1.0, 0.0).astype(BF16)
    same = jnp.where(row == column, 1.0, 0.0).astype(BF16)
    number = lax.broadcasted_iota(I32, (CAP, draft), 0).astype(F32)
    first = me_ref[0] * experts

    def one(piece, i, m):
        info = jnp.transpose(piece[i, :, at_column : at_column + STAT].astype(F32))
        ids, *parts = (info[INFO + g * picks : INFO + (g + 1) * picks] for g in range(4))
        weight = parts[0] + parts[1] + parts[2]
        hits, weights = [], []
        for e in range(experts):
            hit = ids == (first + e).astype(F32)
            hits.append(jnp.max(jnp.where(hit, 1.0, 0.0), axis=0, keepdims=True))
            weights.append(jnp.sum(jnp.where(hit, weight, 0.0), axis=0, keepdims=True))
        table = jnp.concatenate(hits + [jnp.zeros((16 - experts, draft), F32)], axis=0)
        rank = dot(table.astype(BF16), upper)
        blocks = []
        for e in range(experts):
            block = jnp.where((number == rank[e : e + 1]) & (hits[e] > 0.0), 1.0, 0.0)
            blocks.append(block)
            row_weight = jnp.sum(block * weights[e], axis=1, keepdims=True)
            w_ref[e, pl.ds(aligned(m, CAP), CAP), :] = jnp.broadcast_to(row_weight, (CAP, 128))
        stacked = jnp.concatenate(blocks, axis=0).astype(BF16)
        g_ref[m] = stacked
        c_ref[m] = dot_t(same, stacked).astype(BF16)

    at = 0
    for piece, count in zip(pieces, counts):
        each(count, lambda i, piece=piece, at=at: one(piece, i, at + i))
        at += count


def mix_kernel(own_ref, a_ref, b_ref, c_ref, after_hbm, mixed_ref, row_ref):
    mixed = own_ref[...] + a_ref[...].astype(F32) + b_ref[...].astype(F32) + c_ref[...].astype(F32)
    mixed_ref[...] = mixed
    row_ref[0] = mixed.astype(BF16)


def cache_kernel(pos_ref, live_ref, key_ref, value_ref, after_hbm, *refs, counts, accept):
    pieces, (key_out, value_out, mark_ref, table) = refs[: len(counts)], refs[len(counts) :]
    block, page_len, width = key_ref.shape
    step = pl.program_id(0)

    @pl.when(step == 0)
    def _():
        at = 0
        for piece, count in zip(pieces, counts):
            for g in range(width // 128):
                rows = slice(g * 2 * accept, (g + 1) * 2 * accept)
                table[at : at + count, :, g * 128 : (g + 1) * 128] = piece[:, rows, width + STAT :]
            at += count
        mark_ref[...] = jnp.zeros_like(mark_ref)

    key_out[...] = key_ref[...]
    value_out[...] = value_ref[...]
    for i in range(block):
        p = step * block + i
        live = live_ref[p]

        @pl.when((live > -accept) & (live < page_len))
        def _():
            rows = table[pos_ref[p]]
            offset = lax.broadcasted_iota(I32, (page_len, 2 * accept), 0) - live
            column = lax.broadcasted_iota(I32, (page_len, 2 * accept), 1)
            cell = lax.broadcasted_iota(I32, (page_len, width), 0) - live
            touched = (cell >= 0) & (cell < accept)
            for source, out, shift in ((key_ref, key_out, 0), (value_ref, value_out, accept)):
                hit = (offset == column - shift) & (offset >= 0) & (offset < accept)
                place = jnp.where(hit, 1.0, 0.0).astype(BF16)
                out[i] = jnp.where(touched, dot(place, rows), source[i].astype(F32)).astype(BF16)


def combine_rows(active_ref, down_ref, c_ref, y_s, put):
    experts = active_ref.shape[0]
    groups = c_ref.shape[0]
    for e in range(experts):
        y = dot(active_ref[e], down_ref[e]).astype(BF16)
        for m in range(groups):
            y_s[m, e * CAP : (e + 1) * CAP, :] = y[m * CAP : (m + 1) * CAP]
    each(groups, lambda m: put(m, dot(c_ref[m], y_s[m])))


def down_loads(cols_ref, first, down_hbm, down_s, sems):
    width = down_s.shape[3]
    loads = []
    for i in range(down_s.shape[0]):
        cols = pl.ds(pl.multiple_of(cols_ref[first + i] * width, width), width)
        loads.append(pltpu.make_async_copy(down_hbm.at[:, :, cols], down_s.at[i], sems.at[i]))
    return loads


def expert_kernel(
    t_ref, cols_ref, gain_ref, g_ref, rw_ref, c_ref, gate_hbm, up_hbm, down_hbm, *refs, layout, put, steps
):
    later = len(steps) - 1
    pieces, refs = refs[: -10 - 2 * len(steps)], refs[-10 - 2 * len(steps) :]
    active_ref, out_ref, refs = refs[0], refs[1], refs[2:]
    later, (xs, xn, sc, down_s, y_s, gate_s, up_s, gate_sem, up_sem, *sems) = refs[:later], refs[later:]
    experts, slots, model = xs.shape
    groups = g_ref.shape[0]
    weights = [
        (
            pltpu.make_async_copy(gate_hbm.at[e], gate_s.at[e], gate_sem.at[e]),
            pltpu.make_async_copy(up_hbm.at[e], up_s.at[e], up_sem.at[e]),
        )
        for e in range(experts)
    ]
    buffers = [down_s, *later]
    loads = [down_loads(cols_ref, first, down_hbm, to, sem) for first, to, sem in zip(steps, buffers, sems)]
    queue = weights + [(load,) for some in loads for load in some]
    ahead = 3
    for some in queue[:ahead]:
        for load in some:
            load.start()

    def columns(n, width):
        return slice(0, width) if n is None else pl.ds(pl.multiple_of((t_ref[0] ^ n) * width, width), width)

    def squares(m, j):
        total = sum(jnp.sum(v * v, axis=1, keepdims=True) for _, v in layout(pieces, m))
        sc[j] = jnp.broadcast_to(lax.rsqrt(total / model + 1e-6), sc.shape[1:])

    def scaled(m, j):
        for n, v in layout(pieces, m):
            cols = columns(n, v.shape[1])
            xn[j, :, cols] = (v * sc[j, :, 0:1] * gain_ref[:, cols]).astype(BF16)

    def picked(m, j):
        rows = dot(g_ref[m], xn[j]).astype(BF16)
        for i in range(experts):
            xs[i, pl.ds(aligned(m, CAP), CAP), :] = rows[i * CAP : (i + 1) * CAP]

    lap = xn.shape[0]

    def requests(i):
        for step in (squares, scaled, picked):
            for j in range(lap):
                step(i * lap + j, j)

    each(groups // lap, requests)
    def arrived(i):
        for load in queue[i]:
            load.wait()
        for load in queue[i + ahead] if i + ahead < len(queue) else ():
            load.start()

    for e in range(experts):
        arrived(e)
        gate = dot(xs[e], gate_s[e])
        up = dot(xs[e], up_s[e])
        active = gate / (1.0 + jnp.exp(-gate)) * up
        active_ref[e] = (active * rw_ref[e, :, 0:1]).astype(BF16)
    for i in range(len(loads[0])):
        arrived(experts + i)
        combine_rows(active_ref, down_s.at[i], c_ref, y_s, functools.partial(put, out_ref, i))
    for i in range(experts + len(loads[0]), len(queue)):
        arrived(i)


def down_kernel(active_ref, c_ref, add_ref, down_ref, *refs, put):
    outs, y_s = refs[:-1], refs[-1]
    for i in range(down_ref.shape[0]):
        combine_rows(active_ref, down_ref.at[i], c_ref, y_s, functools.partial(put, outs, add_ref, i))


def put_plain(out_ref, i, m, value):
    out_ref[i, m] = value.astype(BF16)


def put_added(outs, add_ref, i, m, value):
    value = (value + add_ref[i, m].astype(F32)).astype(BF16)
    side, z = 2 * i + m // 4, m % 4
    if z == 0:
        outs[side][...] = value
    else:
        outs[4 + side][z - 1] = value


def total_kernel(own_ref, x_ref, y_ref, d_ref, mark_ref, *outs):
    for z in range(3):
        total = own_ref[z].astype(F32) + x_ref[z].astype(F32) + y_ref[z].astype(F32) + d_ref[z].astype(F32)
        outs[z][...] = total.astype(BF16)


def on_device(
    queries,
    draft_keys,
    draft_values,
    key_cache,
    value_cache,
    page_request,
    page_slot,
    cache_len,
    tree_mask,
    accepted,
    hidden_in,
    out_proj,
    norm_gain,
    gate_proj,
    up_proj,
    down_proj,
    expert_ids,
    route_weight,
):
    draft, width = queries.shape
    pages, page_len, _ = key_cache.shape
    model = hidden_in.shape[1]
    heads = width // HD
    seq, tensor = lax.axis_size("seq"), lax.axis_size("tensor")
    experts = gate_proj.shape[0]
    hidden = gate_proj.shape[2]
    accept = accepted.shape[1]
    slots = seq * CAP
    staged = seq == 8 and tensor == 4
    me, t = lax.axis_index("seq"), lax.axis_index("tensor")

    def hop(axis, mask):
        size = seq if axis == "seq" else tensor
        pairs = [(i, i ^ mask) for i in range(size)]
        return lambda v: lax.ppermute(v, axis, pairs)

    x1, y1, core = hop("seq", 1), hop("tensor", 2), hop("tensor", 1)
    zs = [hop("seq", 2 * k) for k in (1, 2, 3)]
    big = 16 if staged else 56

    def diagonal(v):
        flip = tensor + 2
        return lax.ppermute(v, ("seq", "tensor"), [(i, i ^ flip) for i in range(seq * tensor)])

    relative = page_request ^ me if staged else page_request
    pos = (relative & 1) * 4 + (relative >> 1) if staged else relative
    pos = pos.astype(I32)
    request_hit = page_request[:, None] == jnp.arange(cache_len.shape[0], dtype=I32)[None, :]
    live = jnp.sum(jnp.where(request_hit, cache_len[None, :], 0), axis=1) - page_slot * page_len
    me1, t1 = me.reshape(1).astype(I32), t.reshape(1).astype(I32)

    if staged:
        own = queries[None]
        beside = x1(own)
        line = [z(own) for z in zs]
        every_query = [own, *line, beside, *[x1(b) for b in line]]
    else:
        every_query = [lax.all_gather(queries[None], "seq", axis=0, tiled=True)]
    counts = tuple(a.shape[0] for a in every_query)

    near_out, near_lse, info, keys, values = call(
        near_kernel,
        "near",
        (
            queries,
            draft_keys,
            draft_values,
            tree_mask,
            key_cache,
            value_cache,
            accepted.reshape(accept, 1),
            expert_ids,
            route_weight,
        ),
        [hbm()] * 6 + [vmem()] * 3,
        [
            shape((draft, width), F32),
            shape((draft, width), F32),
            shape((draft, EXTRA), F32),
            shape(key_cache.shape, BF16),
            shape(value_cache.shape, BF16),
        ],
        [vmem()] * 5,
        [
            *[pltpu.VMEM((draft, width), BF16)] * 3,
            pltpu.VMEM((1, draft, draft), I32),
            pltpu.VMEM((heads, draft, draft), F32),
            pltpu.VMEM((heads, draft, draft), BF16),
            pltpu.SemaphoreType.DMA((6,)),
        ],
        busy=2,
    )

    n_out = seq if staged else 1
    state = pltpu.VMEM((seq, draft, width), F32)
    per_page = pltpu.VMEM((pages, draft, width), F32)
    partials = call(
        functools.partial(far_kernel, counts=counts, n_out=n_out),
        "far",
        (pos, live, keys, values, info, *every_query),
        [smem(), smem()] + [vmem()] * (3 + len(every_query)),
        [shape((seq // n_out, draft, width + EXTRA), BF16)] * n_out,
        [vmem()] * n_out,
        [pltpu.VMEM((seq, draft, width), BF16), *[per_page] * 4, *[state] * 3],
        limit=big,
        busy=5,
    )

    if staged:
        back = [partials[0]]
        for place in range(1, 8):
            back.append(hop("seq", (place & 3) * 2 + (place >> 2))(partials[place]))
    else:
        back = [lax.all_to_all(partials[0], "seq", split_axis=0, concat_axis=0, tiled=True)]

    n_parts = tensor if staged else 1
    part_shape = (
        [shape((draft, width), F32)] + [shape((draft, width), BF16)] * 3 if staged else [shape((draft, model), F32)]
    )
    back_counts = tuple(b.shape[0] for b in back)
    log_sum_exp, *parts = call(
        functools.partial(merge_kernel, counts=back_counts, n_out=n_parts),
        "merge",
        (t1, near_out, near_lse, hidden_in, out_proj, *back),
        [smem()] + [vmem()] * (4 + len(back)),
        [shape((draft, heads), F32)] + part_shape,
        [vmem()] * (1 + n_parts),
        limit=big,
        busy=4,
    )

    grouped, combine, slot_weight = call(
        functools.partial(slots_kernel, counts=back_counts, picks=expert_ids.shape[1], at_column=width),
        "slots",
        (me1, parts[0], *back),
        [smem(), hbm()] + [vmem()] * len(back),
        [
            shape((seq, experts * CAP, draft), BF16),
            shape((seq, draft, experts * CAP), BF16),
            shape((experts, slots, 128), F32),
        ],
        [vmem()] * 3,
        limit=big,
    )

    if staged:
        got = [hop("tensor", n)(parts[n]) for n in (1, 2, 3)]
        mixed, row = call(
            mix_kernel,
            "mix",
            (parts[0], *got, slot_weight),
            [vmem()] * 4 + [hbm()],
            [shape((draft, width), F32), shape((1, draft, width), BF16)],
            [vmem()] * 2,
            busy=1,
        )
    else:
        summed = lax.psum(parts[0], "tensor") + hidden_in.astype(F32)
        mixed = lax.dynamic_slice_in_dim(summed, t * width, width, 1)
        row = mixed.astype(BF16)[None]

    if staged:
        line = [z(row) for z in zs]
        near_by = [row, x1(row), y1(row), diagonal(row)]
        line = jnp.concatenate(line)
        far_off = [line, x1(line), y1(line), diagonal(line)]
        rows_in = near_by + far_off + [core(jnp.concatenate(near_by))] + [core(v) for v in far_off]

        def layout(refs, m):
            found = []
            for n in range(4):
                side, z = (n >> 1) * 2 + m // 4, m % 4
                if n & 1:
                    v = refs[8][side] if z == 0 else refs[9 + side][z - 1]
                else:
                    v = refs[side][0] if z == 0 else refs[4 + side][z - 1]
                found.append((n, v.astype(F32)))
            return found

        columns, steps, n_down = jnp.stack([t ^ 1, t ^ 3, t, t ^ 2]).astype(I32), (0, 2), 2
    else:
        rows_in = lax.all_gather(row, "seq", axis=0, tiled=True)
        rows_in = [lax.all_gather(rows_in, "tensor", axis=2, tiled=True)]

        def layout(refs, m):
            return [(None, refs[0][m].astype(F32))]

        columns, steps, n_down = jnp.arange(tensor, dtype=I32), (0,), tensor

    y_scratch = pltpu.VMEM((seq, experts * CAP, width), BF16)
    down_block = (n_down, experts, hidden, width)
    later = [shape(down_block, BF16)] * (len(steps) - 1)
    lap = math.gcd(seq, 8)
    active, sums, *later = call(
        functools.partial(expert_kernel, layout=layout, put=put_plain, steps=steps),
        "experts",
        (
            t1,
            columns,
            norm_gain.reshape(1, model),
            grouped,
            slot_weight,
            combine,
            gate_proj,
            up_proj,
            down_proj,
            *rows_in,
        ),
        [smem()] * 2 + [vmem()] * 4 + [hbm()] * 3 + [vmem()] * len(rows_in),
        [
            shape((experts, slots, hidden), BF16),
            shape((n_down, seq, draft, width), BF16),
            *later,
        ],
        [vmem()] * (2 + len(later)),
        [
            pltpu.VMEM((experts, slots, model), BF16),
            pltpu.VMEM((lap, draft, model), BF16),
            pltpu.VMEM((lap, draft, 128), F32),
            pltpu.VMEM(down_block, BF16),
            y_scratch,
            *[pltpu.VMEM((experts, model, hidden), BF16)] * 2,
            *[pltpu.SemaphoreType.DMA((experts,))] * 2,
            *[pltpu.SemaphoreType.DMA((n_down,))] * len(steps),
        ],
        limit=36 if staged else 60,
        busy=9,
    )

    if staged:
        sums = call(
            functools.partial(down_kernel, put=put_added),
            "down",
            (active, combine, core(sums), *later),
            [vmem()] * 4,
            [shape((draft, width), BF16)] * 4 + [shape((3, draft, width), BF16)] * 4,
            [vmem()] * 8,
            [y_scratch],
            busy=3,
        )
        first_sums = sums[0]
    else:
        first_sums = sums
    block = 4 if pages % 4 == 0 else 1
    page_spec = pl.BlockSpec((block, page_len, width), lambda p: (p, 0, 0))
    key_cache_out, value_cache_out, cache_mark = pl.pallas_call(
        functools.partial(cache_kernel, counts=back_counts, accept=accept),
        grid=(pages // block,),
        out_shape=[shape(key_cache.shape, BF16), shape(value_cache.shape, BF16), shape((8, 128), F32)],
        in_specs=[smem(), smem(), page_spec, page_spec, hbm()] + [vmem()] * len(back),
        out_specs=[page_spec, page_spec, pl.BlockSpec((8, 128), lambda p: (0, 0))],
        scratch_shapes=[pltpu.VMEM((seq, 2 * accept, width), BF16)],
        compiler_params=pltpu.CompilerParams(vmem_limit_bytes=big * MIB),
        cost_estimate=pl.CostEstimate(flops=0, bytes_accessed=12_000_000, transcendentals=0),
        name="cache",
    )(pos, live, in_hbm(key_cache), in_hbm(value_cache), in_hbm(first_sums), *back)

    if not staged:
        sums = lax.psum_scatter(sums, "tensor", scatter_dimension=0, tiled=True)[0]
        moe = lax.psum_scatter(sums, "seq", scatter_dimension=0, tiled=True)[0]
        mixed_out = (mixed + moe.astype(F32)).astype(BF16)
        return mixed_out, log_sum_exp, key_cache_out, value_cache_out

    line = call(
        total_kernel,
        "total",
        (sums[4], x1(sums[5]), y1(sums[6]), diagonal(sums[7]), cache_mark),
        [vmem()] * 5,
        [shape((draft, width), BF16)] * 3,
        [vmem()] * 3,
        busy=1,
    )
    moe = sums[0].astype(F32)
    for z, v in zip(zs, line):
        moe = moe + z(v).astype(F32)
    for move, v in zip((x1, y1, diagonal), sums[1:4]):
        moe = moe + move(v).astype(F32)
    mixed_out = (mixed + moe).astype(BF16)
    return mixed_out, log_sum_exp, key_cache_out, value_cache_out


def solution(mesh):
    return jax.shard_map(
        on_device,
        mesh=mesh,
        in_specs=(
            P("seq", "tensor"),
            P("seq", "tensor"),
            P("seq", "tensor"),
            P("seq", None, "tensor"),
            P("seq", None, "tensor"),
            P("seq"),
            P("seq"),
            P(),
            P("seq", None, None),
            P("seq", None),
            P("seq", None),
            P("tensor", None),
            P(),
            P("seq", None, "tensor"),
            P("seq", None, "tensor"),
            P("seq", "tensor", None),
            P("seq", None),
            P("seq", None),
        ),
        out_specs=(
            P("seq", "tensor"),
            P("seq", "tensor"),
            P("seq", None, "tensor"),
            P("seq", None, "tensor"),
        ),
        check_vma=False,
    )
```

time: 171 us -> 114 us (0.67)
  Pallas kernels: 61 us -> 25.6 us
  waiting for transfers between devices: 42.3 us -> 32 us
  starting transfers between devices: 54.7 us -> 46 us
  other arithmetic: 5.39 us -> 2.94 us
    pallas_call x11 -> x9, Pallas kernels: 61 us -> 25.6 us  [the longest x8 20.9 us: call(): pl.pallas_call(kernel, out_shape=out_shape, in_specs=in_specs, out_specs=...]
    ppermute x49 -> x37, starting transfers between devices: 54.7 us -> 40.3 us  [hop(): return lambda v: lax.ppermute(v, axis, pairs)]
    ppermute x49 -> x37, waiting for transfers between devices: 42.3 us -> 28 us  [hop(): return lambda v: lax.ppermute(v, axis, pairs)]
    ppermute x0 -> x4, starting transfers between devices: none -> 5.68 us  [diagonal(): lax.ppermute(v, ('seq', 'tensor'), [(i, i ^ flip) for i in range(seq * te...]
    ppermute x0 -> x4, waiting for transfers between devices: none -> 4 us  [diagonal(): lax.ppermute(v, ('seq', 'tensor'), [(i, i ^ flip) for i in range(seq * te...]
    unnamed x98 -> x29, local copies, waits for them, and re-layouts: 4.96 us -> 5.84 us
  transfers between devices with their start and end apart: 49 -> 41, of which waited for: 19 -> 17; matrix products, arithmetic and copies ran while one was open for 3% -> 5% of each run, Pallas kernels for 11% -> 7%
where the time goes in v2:
time: 114 us
  starting transfers between devices  46 us (40%)
  waiting for transfers between devices  32 us (28%)
  Pallas kernels  25.6 us (22%)
  local copies, waits for them, and re-layouts  6.58 us (6%)
  other arithmetic  2.94 us (3%)
    ppermute x37, starting transfers between devices, hop(): return lambda v: lax.ppermute(v, axis, pairs)  40.3 us
    ppermute x37, waiting for transfers between devices, hop(): return lambda v: lax.ppermute(v, axis, pairs)  28 us
    pallas_call x8, Pallas kernels, call(): pl.pallas_call(kernel, out_shape=out_shape, in_specs=in_specs, out_specs=...  20.9 us
    unnamed x29, local copies, waits for them, and re-layouts  5.84 us
    ppermute x4, starting transfers between devices, diagonal(): lax.ppermute(v, ('seq', 'tensor'), [(i, i ^ flip) for i in range(seq * te...  5.68 us
    pallas_call x1, Pallas kernels, on_device(): pl.pallas_call(functools.partial(cache_kernel, counts=back_counts, accept...  4.67 us
    ppermute x4, waiting for transfers between devices, diagonal(): lax.ppermute(v, ('seq', 'tensor'), [(i, i ^ flip) for i in range(seq * te...  4 us
  transfers between devices with their start and end apart: 41, of which 17 were waited for; matrix products, arithmetic and copies ran while one was open for 5% of the time, Pallas kernels for 7%

profile of v2, /device:TPU:0, one launch (start us, length us, event | category | flops | bytes accessed | tf_op | source)
XLA Modules:
  0.0 114.0 jit_solution(16538427192568064530)
XLA Ops:
  0.6 3.0 %collective-permute-start.3 = (bf16[1,64,512]{2,1,0:T(8,128)(2,1)}, bf16[1,64,512]{2,1,0:T(8,128)(2,1)S(1)}, u32[]{:S(2)}, u32[]{:S(2)}) collective-permute-start(bf16[1,64,512]{2,1,0:T(8,128)(2,1)} %bitcast.8), channel_id=1, source_target_pairs={{0,4},{4,0},{8,12},{12,8},{16,20},{20,16},{24,28},{28,24},{1,5},{5... | collective-permute-start | bytes 196616 | tf_op jit(solution)/shard_map/ppermute | solution.py:464
  3.6 3.6 %collective-permute-start.2 = (bf16[1,64,512]{2,1,0:T(8,128)(2,1)}, bf16[1,64,512]{2,1,0:T(8,128)(2,1)S(1)}, u32[]{:S(2)}, u32[]{:S(2)}) collective-permute-start(bf16[1,64,512]{2,1,0:T(8,128)(2,1)} %bitcast.9), channel_id=1, source_target_pairs={{0,24},{4,28},{8,16},{12,20},{16,8},{20,12},{24,0},{28,4},{1,25},{... | collective-permute-start | bytes 196616 | tf_op jit(solution)/shard_map/ppermute | solution.py:464
  7.2 0.8 collective-permute-start
  8.8 1.9 %collective-permute-done.2.refs_3_ = bf16[1,64,512]{2,1,0:T(8,128)(2,1)S(1)} collective-permute-done((bf16[1,64,512]{2,1,0:T(8,128)(2,1)}, bf16[1,64,512]{2,1,0:T(8,128)(2,1)S(1)}, u32[]{:S(2)}, u32[]{:S(2)}) %collective-permute-start.2) | collective-permute-done | bytes 65568 | tf_op jit(solution)/shard_map/ppermute | solution.py:464
  10.8 2.0 %collective-permute-done.1.refs_2_ = bf16[1,64,512]{2,1,0:T(8,128)(2,1)S(1)} collective-permute-done((bf16[1,64,512]{2,1,0:T(8,128)(2,1)}, bf16[1,64,512]{2,1,0:T(8,128)(2,1)S(1)}, u32[]{:S(2)}, u32[]{:S(2)}) %collective-permute-start.1) | collective-permute-done | bytes 65568 | tf_op jit(solution)/shard_map/ppermute | solution.py:464
  13.4 1.5 %collective-permute-start.4 = (bf16[1,64,512]{2,1,0:T(8,128)(2,1)S(1)}, bf16[1,64,512]{2,1,0:T(8,128)(2,1)S(1)}, u32[]{:S(2)}, u32[]{:S(2)}) collective-permute-start(bf16[1,64,512]{2,1,0:T(8,128)(2,1)S(1)} %collective-permute-done.refs_1_), channel_id=1, source_target_pairs={{0,4},{4,0},{8,12},{12,8},{16,20},{20,16},{24,28},{28,24},{1,5},{5... | collective-permute-start | bytes 196616 | tf_op jit(solution)/shard_map/ppermute | solution.py:464
  17.8 2.1 %near.1 = (f32[64,512]{1,0:T(8,128)S(1)}, f32[64,512]{1,0:T(8,128)S(1)}, f32[64,256]{1,0:T(8,128)S(1)}, bf16[12,128,512]{2,1,0:T(8,128)(2,1)S(1)}, bf16[12,128,512]{2,1,0:T(8,128)(2,1)S(1)}) custom-call(bf16[64,512]{1,0:T(8,128)(2,1)} %q_hbm.1, bf16[64,512]{1,0:T(8,128)(2,1)} %k_hbm.1, bf16[64,512]{1,0:T(8,128)(2,1)} %v_hbm.1, s32[1,64,64]{2,1,0:T(8,128)} %mask_hbm.1, ...), custom_call_target="tpu_custom_call" | custom-call | bytes 6000000 | tf_op jit(solution)/shard_map/near/pallas_call | solution.py:48
  20.0 3.9 %far.1 = (bf16[1,64,768]{2,1,0:T(8,128)(2,1)S(1)}, bf16[1,64,768]{2,1,0:T(8,128)(2,1)S(1)}, bf16[1,64,768]{2,1,0:T(8,128)(2,1)S(1)}, bf16[1,64,768]{2,1,0:T(8,12...) custom-call(s32[12]{0:T(128)S(1)} %get-tuple-element.93.pos_ref, ...), custom_call_target="tpu_custom_call" | custom-call | bytes 15000000 | tf_op jit(solution)/shard_map/far/pallas_call | solution.py:48
  23.9 3.1 %collective-permute-start.8 = (bf16[1,64,768]{2,1,0:T(8,128)(2,1)S(1)}, bf16[1,64,768]{2,1,0:T(8,128)(2,1)S(1)}, u32[]{:S(2)}, u32[]{:S(2)}) collective-permute-start(bf16[1,64,768]{2,1,0:T(8,128)(2,1)S(1)} %get-tuple-element.51), channel_id=1, source_target_pairs={{0,16},{4,20},{8,24},{12,28},{16,0},{20,4},{24,8},{28,12},{1,17},{... | collective-permute-start | bytes 294920 | tf_op jit(solution)/shard_map/ppermute | solution.py:464
  27.0 1.3 %collective-permute-start.9 = (bf16[1,64,768]{2,1,0:T(8,128)(2,1)}, bf16[1,64,768]{2,1,0:T(8,128)(2,1)S(1)}, u32[]{:S(2)}, u32[]{:S(2)}) collective-permute-start(bf16[1,64,768]{2,1,0:T(8,128)(2,1)} %get-tuple-element.52), channel_id=1, source_target_pairs={{0,24},{4,28},{8,16},{12,20},{16,8},{20,12},{24,0},{28,4},{1,25},{... | collective-permute-start | bytes 294920 | tf_op jit(solution)/shard_map/ppermute | solution.py:464
  29.1 4.2 %collective-permute-start.12 = (bf16[1,64,768]{2,1,0:T(8,128)(2,1)}, bf16[1,64,768]{2,1,0:T(8,128)(2,1)S(1)}, u32[]{:S(2)}, u32[]{:S(2)}) collective-permute-start(bf16[1,64,768]{2,1,0:T(8,128)(2,1)} %get-tuple-element.55), channel_id=1, source_target_pairs={{0,20},{4,16},{8,28},{12,24},{16,4},{20,0},{24,12},{28,8},{1,21},{... | collective-permute-start | bytes 294920 | tf_op jit(solution)/shard_map/ppermute | solution.py:464
  33.3 2.2 %collective-permute-done.8.refs_2_ = bf16[1,64,768]{2,1,0:T(8,128)(2,1)S(1)} collective-permute-done((bf16[1,64,768]{2,1,0:T(8,128)(2,1)S(1)}, bf16[1,64,768]{2,1,0:T(8,128)(2,1)S(1)}, u32[]{:S(2)}, u32[]{:S(2)}) %collective-permute-start.8) | collective-permute-done | bytes 98336 | tf_op jit(solution)/shard_map/ppermute | solution.py:464
  35.5 2.1 %collective-permute-start.13 = (bf16[1,64,768]{2,1,0:T(8,128)(2,1)S(1)}, bf16[1,64,768]{2,1,0:T(8,128)(2,1)S(1)}, u32[]{:S(2)}, u32[]{:S(2)}) collective-permute-start(bf16[1,64,768]{2,1,0:T(8,128)(2,1)S(1)} %get-tuple-element.56), channel_id=1, source_target_pairs={{0,28},{4,24},{8,20},{12,16},{16,12},{20,8},{24,4},{28,0},{1,29},{... | collective-permute-start | bytes 294920 | tf_op jit(solution)/shard_map/ppermute | solution.py:464
  37.7 3.4 %collective-permute-done.12.refs_6_ = bf16[1,64,768]{2,1,0:T(8,128)(2,1)S(1)} collective-permute-done((bf16[1,64,768]{2,1,0:T(8,128)(2,1)}, bf16[1,64,768]{2,1,0:T(8,128)(2,1)S(1)}, u32[]{:S(2)}, u32[]{:S(2)}) %collective-permute-start.12) | collective-permute-done | bytes 98336 | tf_op jit(solution)/shard_map/ppermute | solution.py:464
  41.1 1.8 %collective-permute-done.13.refs_7_ = bf16[1,64,768]{2,1,0:T(8,128)(2,1)S(1)} collective-permute-done((bf16[1,64,768]{2,1,0:T(8,128)(2,1)S(1)}, bf16[1,64,768]{2,1,0:T(8,128)(2,1)S(1)}, u32[]{:S(2)}, u32[]{:S(2)}) %collective-permute-start.13) | collective-permute-done | bytes 98336 | tf_op jit(solution)/shard_map/ppermute | solution.py:464
  42.9 1.9 %merge.1 = (f32[64,4]{1,0:T(8,128)S(1)}, f32[64,512]{1,0:T(8,128)S(1)}, bf16[64,512]{1,0:T(8,128)(2,1)S(1)}, bf16[64,512]{1,0:T(8,128)(2,1)S(1)}, bf16[64,512]{1,0:T(8,128)(2,1)S(1)}) custom-call(s32[1]{0:T(128)} %bitcast.t_ref, f32[64,512]{1,0:T(8,128)S(1)} %get-tuple-element.44.near_ref, f32[64,512]{1,0:T(8,128)S(1)} %get-tuple-element.45.lse_ref, ...), custom_call_target="tpu_custom_call" | custom-call | bytes 12000000 | tf_op jit(solution)/shard_map/merge/pallas_call | solution.py:48
  45.5 1.5 %collective-permute-start.15 = (bf16[64,512]{1,0:T(8,128)(2,1)S(1)}, bf16[64,512]{1,0:T(8,128)(2,1)S(1)}, u32[]{:S(2)}, u32[]{:S(2)}) collective-permute-start(bf16[64,512]{1,0:T(8,128)(2,1)S(1)} %get-tuple-element.59), channel_id=1, source_target_pairs={{0,2},{1,3},{2,0},{3,1},{4,6},{5,7},{6,4},{7,5},{8,10},{9,11},{10,... | collective-permute-start | bytes 196616 | tf_op jit(solution)/shard_map/ppermute | solution.py:464
  47.3 0.9 slots.1
  48.2 0.8 copy-done
  49.0 1.0 collective-permute-done.15.b_ref
  50.0 1.1 collective-permute-done.16.c_ref
  51.1 0.9 copy-done.4
  52.7 0.8 collective-permute-start.20
  53.5 1.8 %collective-permute-start.22 = (bf16[1,64,512]{2,1,0:T(8,128)(2,1)S(1)}, bf16[1,64,512]{2,1,0:T(8,128)(2,1)S(1)}, u32[]{:S(2)}, u32[]{:S(2)}) collective-permute-start(bf16[1,64,512]{2,1,0:T(8,128)(2,1)S(1)} %get-tuple-element.65.refs_0_), channel_id=1, source_target_pairs={{0,24},{4,28},{8,16},{12,20},{16,8},{20,12},{24,0},{28,4},{1,25},{... | collective-permute-start | bytes 196616 | tf_op jit(solution)/shard_map/ppermute | solution.py:464
  55.3 0.9 collective-permute-start.21
  56.2 1.6 %collective-permute-start.19 = (bf16[1,64,512]{2,1,0:T(8,128)(2,1)S(1)}, bf16[1,64,512]{2,1,0:T(8,128)(2,1)S(1)}, u32[]{:S(2)}, u32[]{:S(2)}) collective-permute-start(bf16[1,64,512]{2,1,0:T(8,128)(2,1)S(1)} %get-tuple-element.65.refs_0_), channel_id=1, source_target_pairs={{0,6},{1,7},{2,4},{3,5},{4,2},{5,3},{6,0},{7,1},{8,14},{9,15},{10,... | collective-permute-start | bytes 196616 | tf_op jit(solution)/shard_map/ppermute | solution.py:472
  58.3 1.3 %collective-permute-start.17 = (bf16[1,64,512]{2,1,0:T(8,128)(2,1)S(1)}, bf16[1,64,512]{2,1,0:T(8,128)(2,1)S(1)}, u32[]{:S(2)}, u32[]{:S(2)}) collective-permute-start(bf16[1,64,512]{2,1,0:T(8,128)(2,1)S(1)} %get-tuple-element.65.refs_0_), channel_id=1, source_target_pairs={{0,4},{4,0},{8,12},{12,8},{16,20},{20,16},{24,28},{28,24},{1,5},{5... | collective-permute-start | bytes 196616 | tf_op jit(solution)/shard_map/ppermute | solution.py:464
  59.7 3.0 %collective-permute-done.21 = bf16[1,64,512]{2,1,0:T(8,128)(2,1)S(1)} collective-permute-done((bf16[1,64,512]{2,1,0:T(8,128)(2,1)S(1)}, bf16[1,64,512]{2,1,0:T(8,128)(2,1)S(1)}, u32[]{:S(2)}, u32[]{:S(2)}) %collective-permute-start.21) | collective-permute-done | bytes 65568 | tf_op jit(solution)/shard_map/ppermute | solution.py:464
  62.6 1.9 %collective-permute-start.25 = (bf16[3,64,512]{2,1,0:T(8,128)(2,1)S(1)}, bf16[3,64,512]{2,1,0:T(8,128)(2,1)S(1)}, u32[]{:S(2)}, u32[]{:S(2)}) collective-permute-start(bf16[3,64,512]{2,1,0:T(8,128)(2,1)S(1)} %constant_dynamic-update-slice_fusion.refs_4_), channel_id=1, source_target_pairs={{0,6},{1,7},{2,4},{3,5},{4,2},{5,3},{6,0},{7,1},{8,14},{9,15},{10,... | collective-permute-start | bytes 589832 | tf_op jit(solution)/shard_map/ppermute | solution.py:472
  65.0 1.2 %collective-permute-start.23 = (bf16[3,64,512]{2,1,0:T(8,128)(2,1)S(1)}, bf16[3,64,512]{2,1,0:T(8,128)(2,1)S(1)}, u32[]{:S(2)}, u32[]{:S(2)}) collective-permute-start(bf16[3,64,512]{2,1,0:T(8,128)(2,1)S(1)} %constant_dynamic-update-slice_fusion.refs_4_), channel_id=1, source_target_pairs={{0,4},{4,0},{8,12},{12,8},{16,20},{20,16},{24,28},{28,24},{1,5},{5... | collective-permute-start | bytes 589832 | tf_op jit(solution)/shard_map/ppermute | solution.py:464
  67.5 4.0 %collective-permute-done.25.refs_7_ = bf16[3,64,512]{2,1,0:T(8,128)(2,1)S(1)} collective-permute-done((bf16[3,64,512]{2,1,0:T(8,128)(2,1)S(1)}, bf16[3,64,512]{2,1,0:T(8,128)(2,1)S(1)}, u32[]{:S(2)}, u32[]{:S(2)}) %collective-permute-start.25) | collective-permute-done | bytes 196640 | tf_op jit(solution)/shard_map/ppermute | solution.py:472
  71.5 2.7 %collective-permute-done.24.refs_6_ = bf16[3,64,512]{2,1,0:T(8,128)(2,1)S(1)} collective-permute-done((bf16[3,64,512]{2,1,0:T(8,128)(2,1)S(1)}, bf16[3,64,512]{2,1,0:T(8,128)(2,1)S(1)}, u32[]{:S(2)}, u32[]{:S(2)}) %collective-permute-start.24) | collective-permute-done | bytes 196640 | tf_op jit(solution)/shard_map/ppermute | solution.py:464
  74.8 1.0 collective-permute-done.29.refs_11_
  76.0 10.8 %experts.1 = (bf16[8,128,256]{2,1,0:T(8,128)(2,1)S(1)}, bf16[2,8,64,512]{3,2,1,0:T(8,128)(2,1)S(1)}, bf16[2,8,256,512]{3,2,1,0:T(8,128)(2,1)S(1)}) custom-call(s32[1]{0:T(128)} %bitcast.t_ref, s32[4]{0:T(128)S(1)} %pad_add_fusion.cols_ref, f32[1,2048]{1,0:T(1,128)S(1)} %bitcast.13, bf16[8,128,64]{2,1,0:T(8,128)(2,1)S(1)} %get-tuple-element.63.g_ref, ...), custom_call_target="tpu_custom_call" | custom-call | bytes 27000000 | tf_op jit(solution)/shard_map/experts/pallas_call | solution.py:48
  87.2 2.4 %collective-permute-done.31.add_ref = bf16[2,8,64,512]{3,2,1,0:T(8,128)(2,1)S(1)} collective-permute-done((bf16[2,8,64,512]{3,2,1,0:T(8,128)(2,1)S(1)}, bf16[2,8,64,512]{3,2,1,0:T(8,128)(2,1)S(1)}, u32[]{:S(2)}, u32[]{:S(2)}) %collective-permute-start.31) | collective-permute-done | bytes 1048608 | tf_op jit(solution)/shard_map/ppermute | solution.py:464
  89.6 1.3 %down.1 = (bf16[64,512]{1,0:T(8,128)(2,1)S(1)}, bf16[64,512]{1,0:T(8,128)(2,1)S(1)}, bf16[64,512]{1,0:T(8,128)(2,1)S(1)}, bf16[64,512]{1,0:T(8,128)(2,1)S(1)}, b...) custom-call(bf16[8,128,256]{2,1,0:T(8,128)(2,1)S(1)} %get-tuple-elem, ...), custom_call_target="tpu_custom_call" | custom-call | bytes 9000000 | tf_op jit(solution)/shard_map/down/pallas_call | solution.py:48
  91.5 1.3 %collective-permute-start.32 = (bf16[3,64,512]{2,1,0:T(8,128)(2,1)S(1)}, bf16[3,64,512]{2,1,0:T(8,128)(2,1)S(1)}, u32[]{:S(2)}, u32[]{:S(2)}) collective-permute-start(bf16[3,64,512]{2,1,0:T(8,128)(2,1)S(1)} %get-tuple-element.71), channel_id=1, source_target_pairs={{0,4},{4,0},{8,12},{12,8},{16,20},{20,16},{24,28},{28,24},{1,5},{5... | collective-permute-start | bytes 589832 | tf_op jit(solution)/shard_map/ppermute | solution.py:464
  92.8 1.0 collective-permute-start.33
  93.8 1.2 %collective-permute-start.34 = (bf16[3,64,512]{2,1,0:T(8,128)(2,1)S(1)}, bf16[3,64,512]{2,1,0:T(8,128)(2,1)S(1)}, u32[]{:S(2)}, u32[]{:S(2)}) collective-permute-start(bf16[3,64,512]{2,1,0:T(8,128)(2,1)S(1)} %get-tuple-element.73), channel_id=1, source_target_pairs={{0,6},{1,7},{2,4},{3,5},{4,2},{5,3},{6,0},{7,1},{8,14},{9,15},{10,... | collective-permute-start | bytes 589832 | tf_op jit(solution)/shard_map/ppermute | solution.py:472
  95.0 1.3 %collective-permute-start.38 = (bf16[64,512]{1,0:T(8,128)(2,1)S(1)}, bf16[64,512]{1,0:T(8,128)(2,1)S(1)}, u32[]{:S(2)}, u32[]{:S(2)}) collective-permute-start(bf16[64,512]{1,0:T(8,128)(2,1)S(1)} %get-tuple-element.78), channel_id=1, source_target_pairs={{0,4},{4,0},{8,12},{12,8},{16,20},{20,16},{24,28},{28,24},{1,5},{5... | collective-permute-start | bytes 196616 | tf_op jit(solution)/shard_map/ppermute | solution.py:464
  96.3 1.0 collective-permute-start.39
  97.3 4.7 %cache.1 = (bf16[12,128,512]{2,1,0:T(8,128)(2,1)}, bf16[12,128,512]{2,1,0:T(8,128)(2,1)}, f32[8,128]{1,0:T(8,128)S(1)}) custom-call(s32[12]{0:T(128)S(1)} %get-tuple-element.93.pos_ref, s32[12]{0:T(128)S(1)} %get-tuple-element.92.live_ref, bf16[12,128,512]{2,1,0:T(8,128)(2,1)} %key_ref.1, bf16[12,128,512]{2,1,0:T(8,128)(2,1)} %value_ref.1, ...), custom_call_target="tpu_custom_call" | custom-call | bytes 12000000 | tf_op jit(solution)/shard_map/cache/pallas_call | solution.py:675
  102.0 1.1 collective-permute-start.40
  103.1 1.4 %collective-permute-done.33.y_ref = bf16[3,64,512]{2,1,0:T(8,128)(2,1)S(1)} collective-permute-done((bf16[3,64,512]{2,1,0:T(8,128)(2,1)S(1)}, bf16[3,64,512]{2,1,0:T(8,128)(2,1)S(1)}, u32[]{:S(2)}, u32[]{:S(2)}) %collective-permute-start.33) | collective-permute-done | bytes 196640 | tf_op jit(solution)/shard_map/ppermute | solution.py:464
  104.7 2.5 %collective-permute-start.36 = (bf16[64,512]{1,0:T(8,128)(2,1)S(1)}, bf16[64,512]{1,0:T(8,128)(2,1)S(1)}, u32[]{:S(2)}, u32[]{:S(2)}) collective-permute-start(bf16[64,512]{1,0:T(8,128)(2,1)S(1)} %get-tuple-element.76), channel_id=1, source_target_pairs={{0,16},{4,20},{8,24},{12,28},{16,0},{20,4},{24,8},{28,12},{1,17},{... | collective-permute-start | bytes 196616 | tf_op jit(solution)/shard_map/ppermute | solution.py:464
  107.2 1.8 %collective-permute-start.37 = (bf16[64,512]{1,0:T(8,128)(2,1)S(1)}, bf16[64,512]{1,0:T(8,128)(2,1)S(1)}, u32[]{:S(2)}, u32[]{:S(2)}) collective-permute-start(bf16[64,512]{1,0:T(8,128)(2,1)S(1)} %get-tuple-element.77), channel_id=1, source_target_pairs={{0,24},{4,28},{8,16},{12,20},{16,8},{20,12},{24,0},{28,4},{1,25},{... | collective-permute-start | bytes 196616 | tf_op jit(solution)/shard_map/ppermute | solution.py:464
  109.7 1.6 %collective-permute-done.36 = bf16[64,512]{1,0:T(8,128)(2,1)S(1)} collective-permute-done((bf16[64,512]{1,0:T(8,128)(2,1)S(1)}, bf16[64,512]{1,0:T(8,128)(2,1)S(1)}, u32[]{:S(2)}, u32[]{:S(2)}) %collective-permute-start.36) | collective-permute-done | bytes 65568 | tf_op jit(solution)/shard_map/ppermute | solution.py:464
  111.3 2.0 %collective-permute-done.37 = bf16[64,512]{1,0:T(8,128)(2,1)S(1)} collective-permute-done((bf16[64,512]{1,0:T(8,128)(2,1)S(1)}, bf16[64,512]{1,0:T(8,128)(2,1)S(1)}, u32[]{:S(2)}, u32[]{:S(2)}) %collective-permute-start.37) | collective-permute-done | bytes 65568 | tf_op jit(solution)/shard_map/ppermute | solution.py:464
  (79 shorter events, 12.5 us)
Async XLA Ops:
  0.6 19.3 %collective-permute-start.3 = (bf16[1,64,512]{2,1,0:T(8,128)(2,1)}, bf16[1,64,512]{2,1,0:T(8,128)(2,1)S(1)}, u32[]{:S(2)}, u32[]{:S(2)}) collective-permute-start(bf16[1,64,512]{2,1,0:T(8,128)(2,1)} %bitcast.8), channel_id=1, source_target_pairs={{0,4},{4,0},{8,12},{12,8},{16,20},{20,16},{24,28},{28,24},{1,5},{5... | collective-permute-start | bytes 196616 | tf_op jit(solution)/shard_map/ppermute | solution.py:464
  3.6 7.1 %collective-permute-start.2 = (bf16[1,64,512]{2,1,0:T(8,128)(2,1)}, bf16[1,64,512]{2,1,0:T(8,128)(2,1)S(1)}, u32[]{:S(2)}, u32[]{:S(2)}) collective-permute-start(bf16[1,64,512]{2,1,0:T(8,128)(2,1)} %bitcast.9), channel_id=1, source_target_pairs={{0,24},{4,28},{8,16},{12,20},{16,8},{20,12},{24,0},{28,4},{1,25},{... | collective-permute-start | bytes 196616 | tf_op jit(solution)/shard_map/ppermute | solution.py:464
  7.2 5.6 %collective-permute-start.1 = (bf16[1,64,512]{2,1,0:T(8,128)(2,1)}, bf16[1,64,512]{2,1,0:T(8,128)(2,1)S(1)}, u32[]{:S(2)}, u32[]{:S(2)}) collective-permute-start(bf16[1,64,512]{2,1,0:T(8,128)(2,1)} %bitcast.10), channel_id=1, source_target_pairs={{0,16},{4,20},{8,24},{12,28},{16,0},{20,4},{24,8},{28,12},{1,17},{... | collective-permute-start | bytes 196616 | tf_op jit(solution)/shard_map/ppermute | solution.py:464
  7.2 6.2 %collective-permute-start = (bf16[1,64,512]{2,1,0:T(8,128)(2,1)}, bf16[1,64,512]{2,1,0:T(8,128)(2,1)S(1)}, u32[]{:S(2)}, u32[]{:S(2)}) collective-permute-start(bf16[1,64,512]{2,1,0:T(8,128)(2,1)} %bitcast.11), channel_id=1, source_target_pairs={{0,8},{4,12},{8,0},{12,4},{16,24},{20,28},{24,16},{28,20},{1,9},{5... | collective-permute-start | bytes 196616 | tf_op jit(solution)/shard_map/ppermute | solution.py:464
  10.7 9.3 %collective-permute-start.6 = (bf16[1,64,512]{2,1,0:T(8,128)(2,1)S(1)}, bf16[1,64,512]{2,1,0:T(8,128)(2,1)S(1)}, u32[]{:S(2)}, u32[]{:S(2)}) collective-permute-start(bf16[1,64,512]{2,1,0:T(8,128)(2,1)S(1)} %collective-permute-done.2.refs_3_), channel_id=1, source_target_pairs={{0,4},{4,0},{8,12},{12,8},{16,20},{20,16},{24,28},{28,24},{1,5},{5... | collective-permute-start | bytes 196616 | tf_op jit(solution)/shard_map/ppermute | solution.py:464
  12.9 7.1 %collective-permute-start.5 = (bf16[1,64,512]{2,1,0:T(8,128)(2,1)S(1)}, bf16[1,64,512]{2,1,0:T(8,128)(2,1)S(1)}, u32[]{:S(2)}, u32[]{:S(2)}) collective-permute-start(bf16[1,64,512]{2,1,0:T(8,128)(2,1)S(1)} %collective-permute-done.1.refs_2_), channel_id=1, source_target_pairs={{0,4},{4,0},{8,12},{12,8},{16,20},{20,16},{24,28},{28,24},{1,5},{5... | collective-permute-start | bytes 196616 | tf_op jit(solution)/shard_map/ppermute | solution.py:464
  13.4 6.6 %collective-permute-start.4 = (bf16[1,64,512]{2,1,0:T(8,128)(2,1)S(1)}, bf16[1,64,512]{2,1,0:T(8,128)(2,1)S(1)}, u32[]{:S(2)}, u32[]{:S(2)}) collective-permute-start(bf16[1,64,512]{2,1,0:T(8,128)(2,1)S(1)} %collective-permute-done.refs_1_), channel_id=1, source_target_pairs={{0,4},{4,0},{8,12},{12,8},{16,20},{20,16},{24,28},{28,24},{1,5},{5... | collective-permute-start | bytes 196616 | tf_op jit(solution)/shard_map/ppermute | solution.py:464
  17.8 2.2 %copy-start.8 = (bf16[64,512]{1,0:T(8,128)(2,1)S(1)}, bf16[64,512]{1,0:T(8,128)(2,1)}, u32[]{:S(2)}) copy-start(bf16[64,512]{1,0:T(8,128)(2,1)} %q_hbm.1) | copy-start | bytes 196612
  20.0 22.9 %copy-start.2 = (bf16[512,2048]{1,0:T(8,128)(2,1)S(1)}, bf16[512,2048]{1,0:T(8,128)(2,1)}, u32[]{:S(2)}) copy-start(bf16[512,2048]{1,0:T(8,128)(2,1)} %w_ref.1) | copy-start | bytes 6291460
  20.0 22.9 %copy-start.7 = (bf16[64,2048]{1,0:T(8,128)(2,1)S(1)}, bf16[64,2048]{1,0:T(8,128)(2,1)}, u32[]{:S(2)}) copy-start(bf16[64,2048]{1,0:T(8,128)(2,1)} %hidden_ref.1) | copy-start | bytes 786436
  23.9 5.2 %collective-permute-start.7 = (bf16[1,64,768]{2,1,0:T(8,128)(2,1)S(1)}, bf16[1,64,768]{2,1,0:T(8,128)(2,1)S(1)}, u32[]{:S(2)}, u32[]{:S(2)}) collective-permute-start(bf16[1,64,768]{2,1,0:T(8,128)(2,1)S(1)} %get-tuple-element.50), channel_id=1, source_target_pairs={{0,8},{4,12},{8,0},{12,4},{16,24},{20,28},{24,16},{28,20},{1,9},{5... | collective-permute-start | bytes 294920 | tf_op jit(solution)/shard_map/ppermute | solution.py:464
  23.9 11.6 %collective-permute-start.8 = (bf16[1,64,768]{2,1,0:T(8,128)(2,1)S(1)}, bf16[1,64,768]{2,1,0:T(8,128)(2,1)S(1)}, u32[]{:S(2)}, u32[]{:S(2)}) collective-permute-start(bf16[1,64,768]{2,1,0:T(8,128)(2,1)S(1)} %get-tuple-element.51), channel_id=1, source_target_pairs={{0,16},{4,20},{8,24},{12,28},{16,0},{20,4},{24,8},{28,12},{1,17},{... | collective-permute-start | bytes 294920 | tf_op jit(solution)/shard_map/ppermute | solution.py:464
  27.0 10.6 %collective-permute-start.9 = (bf16[1,64,768]{2,1,0:T(8,128)(2,1)}, bf16[1,64,768]{2,1,0:T(8,128)(2,1)S(1)}, u32[]{:S(2)}, u32[]{:S(2)}) collective-permute-start(bf16[1,64,768]{2,1,0:T(8,128)(2,1)} %get-tuple-element.52), channel_id=1, source_target_pairs={{0,24},{4,28},{8,16},{12,20},{16,8},{20,12},{24,0},{28,4},{1,25},{... | collective-permute-start | bytes 294920 | tf_op jit(solution)/shard_map/ppermute | solution.py:464
  28.3 9.4 %collective-permute-start.10 = (bf16[1,64,768]{2,1,0:T(8,128)(2,1)}, bf16[1,64,768]{2,1,0:T(8,128)(2,1)S(1)}, u32[]{:S(2)}, u32[]{:S(2)}) collective-permute-start(bf16[1,64,768]{2,1,0:T(8,128)(2,1)} %get-tuple-element.53), channel_id=1, source_target_pairs={{0,4},{4,0},{8,12},{12,8},{16,20},{20,16},{24,28},{28,24},{1,5},{5... | collective-permute-start | bytes 294920 | tf_op jit(solution)/shard_map/ppermute | solution.py:464
  28.8 8.8 %collective-permute-start.11 = (bf16[1,64,768]{2,1,0:T(8,128)(2,1)}, bf16[1,64,768]{2,1,0:T(8,128)(2,1)S(1)}, u32[]{:S(2)}, u32[]{:S(2)}) collective-permute-start(bf16[1,64,768]{2,1,0:T(8,128)(2,1)} %get-tuple-element.54), channel_id=1, source_target_pairs={{0,12},{4,8},{8,4},{12,0},{16,28},{20,24},{24,20},{28,16},{1,13},{... | collective-permute-start | bytes 294920 | tf_op jit(solution)/shard_map/ppermute | solution.py:464
  29.1 12.0 %collective-permute-start.12 = (bf16[1,64,768]{2,1,0:T(8,128)(2,1)}, bf16[1,64,768]{2,1,0:T(8,128)(2,1)S(1)}, u32[]{:S(2)}, u32[]{:S(2)}) collective-permute-start(bf16[1,64,768]{2,1,0:T(8,128)(2,1)} %get-tuple-element.55), channel_id=1, source_target_pairs={{0,20},{4,16},{8,28},{12,24},{16,4},{20,0},{24,12},{28,8},{1,21},{... | collective-permute-start | bytes 294920 | tf_op jit(solution)/shard_map/ppermute | solution.py:464
  35.5 7.4 %collective-permute-start.13 = (bf16[1,64,768]{2,1,0:T(8,128)(2,1)S(1)}, bf16[1,64,768]{2,1,0:T(8,128)(2,1)S(1)}, u32[]{:S(2)}, u32[]{:S(2)}) collective-permute-start(bf16[1,64,768]{2,1,0:T(8,128)(2,1)S(1)} %get-tuple-element.56), channel_id=1, source_target_pairs={{0,28},{4,24},{8,20},{12,16},{16,12},{20,8},{24,4},{28,0},{1,29},{... | collective-permute-start | bytes 294920 | tf_op jit(solution)/shard_map/ppermute | solution.py:464
  45.5 30.6 %copy-start.11 = (f32[2048]{0:T(1024)S(1)}, f32[2048]{0:T(1024)}, u32[]{:S(2)}) copy-start(f32[2048]{0:T(1024)} %param.30) | copy-start | bytes 24580
  45.5 3.5 %collective-permute-start.14 = (bf16[64,512]{1,0:T(8,128)(2,1)S(1)}, bf16[64,512]{1,0:T(8,128)(2,1)S(1)}, u32[]{:S(2)}, u32[]{:S(2)}) collective-permute-start(bf16[64,512]{1,0:T(8,128)(2,1)S(1)} %get-tuple-element.58), channel_id=1, source_target_pairs={{0,1},{1,0},{2,3},{3,2},{4,5},{5,4},{6,7},{7,6},{8,9},{9,8},{10,11... | collective-permute-start | bytes 196616 | tf_op jit(solution)/shard_map/ppermute | solution.py:464
  45.5 4.5 %collective-permute-start.15 = (bf16[64,512]{1,0:T(8,128)(2,1)S(1)}, bf16[64,512]{1,0:T(8,128)(2,1)S(1)}, u32[]{:S(2)}, u32[]{:S(2)}) collective-permute-start(bf16[64,512]{1,0:T(8,128)(2,1)S(1)} %get-tuple-element.59), channel_id=1, source_target_pairs={{0,2},{1,3},{2,0},{3,1},{4,6},{5,7},{6,4},{7,5},{8,10},{9,11},{10,... | collective-permute-start | bytes 196616 | tf_op jit(solution)/shard_map/ppermute | solution.py:464
  47.0 4.1 %collective-permute-start.16 = (bf16[64,512]{1,0:T(8,128)(2,1)S(1)}, bf16[64,512]{1,0:T(8,128)(2,1)S(1)}, u32[]{:S(2)}, u32[]{:S(2)}) collective-permute-start(bf16[64,512]{1,0:T(8,128)(2,1)S(1)} %get-tuple-element.60), channel_id=1, source_target_pairs={{0,3},{1,2},{2,1},{3,0},{4,7},{5,6},{6,5},{7,4},{8,11},{9,10},{10,... | collective-permute-start | bytes 196616 | tf_op jit(solution)/shard_map/ppermute | solution.py:464
  49.0 27.0 %copy-start.1 = (f32[8,128,128]{2,1,0:T(8,128)S(1)}, f32[8,128,128]{2,1,0:T(8,128)}, u32[]{:S(2)}) copy-start(f32[8,128,128]{2,1,0:T(8,128)} %copy-done) | copy-start | bytes 1572868
  52.7 5.7 %collective-permute-start.20 = (bf16[1,64,512]{2,1,0:T(8,128)(2,1)S(1)}, bf16[1,64,512]{2,1,0:T(8,128)(2,1)S(1)}, u32[]{:S(2)}, u32[]{:S(2)}) collective-permute-start(bf16[1,64,512]{2,1,0:T(8,128)(2,1)S(1)} %get-tuple-element.65.refs_0_), channel_id=1, source_target_pairs={{0,8},{4,12},{8,0},{12,4},{16,24},{20,28},{24,16},{28,20},{1,9},{5... | collective-permute-start | bytes 196616 | tf_op jit(solution)/shard_map/ppermute | solution.py:464
  53.5 9.1 %collective-permute-start.22 = (bf16[1,64,512]{2,1,0:T(8,128)(2,1)S(1)}, bf16[1,64,512]{2,1,0:T(8,128)(2,1)S(1)}, u32[]{:S(2)}, u32[]{:S(2)}) collective-permute-start(bf16[1,64,512]{2,1,0:T(8,128)(2,1)S(1)} %get-tuple-element.65.refs_0_), channel_id=1, source_target_pairs={{0,24},{4,28},{8,16},{12,20},{16,8},{20,12},{24,0},{28,4},{1,25},{... | collective-permute-start | bytes 196616 | tf_op jit(solution)/shard_map/ppermute | solution.py:464
  55.3 7.3 %collective-permute-start.21 = (bf16[1,64,512]{2,1,0:T(8,128)(2,1)S(1)}, bf16[1,64,512]{2,1,0:T(8,128)(2,1)S(1)}, u32[]{:S(2)}, u32[]{:S(2)}) collective-permute-start(bf16[1,64,512]{2,1,0:T(8,128)(2,1)S(1)} %get-tuple-element.65.refs_0_), channel_id=1, source_target_pairs={{0,16},{4,20},{8,24},{12,28},{16,0},{20,4},{24,8},{28,12},{1,17},{... | collective-permute-start | bytes 196616 | tf_op jit(solution)/shard_map/ppermute | solution.py:464
  56.2 8.8 %collective-permute-start.19 = (bf16[1,64,512]{2,1,0:T(8,128)(2,1)S(1)}, bf16[1,64,512]{2,1,0:T(8,128)(2,1)S(1)}, u32[]{:S(2)}, u32[]{:S(2)}) collective-permute-start(bf16[1,64,512]{2,1,0:T(8,128)(2,1)S(1)} %get-tuple-element.65.refs_0_), channel_id=1, source_target_pairs={{0,6},{1,7},{2,4},{3,5},{4,2},{5,3},{6,0},{7,1},{8,14},{9,15},{10,... | collective-permute-start | bytes 196616 | tf_op jit(solution)/shard_map/ppermute | solution.py:472
  57.8 8.5 %collective-permute-start.18 = (bf16[1,64,512]{2,1,0:T(8,128)(2,1)S(1)}, bf16[1,64,512]{2,1,0:T(8,128)(2,1)S(1)}, u32[]{:S(2)}, u32[]{:S(2)}) collective-permute-start(bf16[1,64,512]{2,1,0:T(8,128)(2,1)S(1)} %get-tuple-element.65.refs_0_), channel_id=1, source_target_pairs={{0,2},{1,3},{2,0},{3,1},{4,6},{5,7},{6,4},{7,5},{8,10},{9,11},{10,... | collective-permute-start | bytes 196616 | tf_op jit(solution)/shard_map/ppermute | solution.py:464
  58.3 7.9 %collective-permute-start.17 = (bf16[1,64,512]{2,1,0:T(8,128)(2,1)S(1)}, bf16[1,64,512]{2,1,0:T(8,128)(2,1)S(1)}, u32[]{:S(2)}, u32[]{:S(2)}) collective-permute-start(bf16[1,64,512]{2,1,0:T(8,128)(2,1)S(1)} %get-tuple-element.65.refs_0_), channel_id=1, source_target_pairs={{0,4},{4,0},{8,12},{12,8},{16,20},{20,16},{24,28},{28,24},{1,5},{5... | collective-permute-start | bytes 196616 | tf_op jit(solution)/shard_map/ppermute | solution.py:464
  62.6 8.8 %collective-permute-start.25 = (bf16[3,64,512]{2,1,0:T(8,128)(2,1)S(1)}, bf16[3,64,512]{2,1,0:T(8,128)(2,1)S(1)}, u32[]{:S(2)}, u32[]{:S(2)}) collective-permute-start(bf16[3,64,512]{2,1,0:T(8,128)(2,1)S(1)} %constant_dynamic-update-slice_fusion.refs_4_), channel_id=1, source_target_pairs={{0,6},{1,7},{2,4},{3,5},{4,2},{5,3},{6,0},{7,1},{8,14},{9,15},{10,... | collective-permute-start | bytes 589832 | tf_op jit(solution)/shard_map/ppermute | solution.py:472
  64.5 9.7 %collective-permute-start.24 = (bf16[3,64,512]{2,1,0:T(8,128)(2,1)S(1)}, bf16[3,64,512]{2,1,0:T(8,128)(2,1)S(1)}, u32[]{:S(2)}, u32[]{:S(2)}) collective-permute-start(bf16[3,64,512]{2,1,0:T(8,128)(2,1)S(1)} %constant_dynamic-update-slice_fusion.refs_4_), channel_id=1, source_target_pairs={{0,2},{1,3},{2,0},{3,1},{4,6},{5,7},{6,4},{7,5},{8,10},{9,11},{10,... | collective-permute-start | bytes 589832 | tf_op jit(solution)/shard_map/ppermute | solution.py:464
  65.0 9.3 %collective-permute-start.23 = (bf16[3,64,512]{2,1,0:T(8,128)(2,1)S(1)}, bf16[3,64,512]{2,1,0:T(8,128)(2,1)S(1)}, u32[]{:S(2)}, u32[]{:S(2)}) collective-permute-start(bf16[3,64,512]{2,1,0:T(8,128)(2,1)S(1)} %constant_dynamic-update-slice_fusion.refs_4_), channel_id=1, source_target_pairs={{0,4},{4,0},{8,12},{12,8},{16,20},{20,16},{24,28},{28,24},{1,5},{5... | collective-permute-start | bytes 589832 | tf_op jit(solution)/shard_map/ppermute | solution.py:464
  67.0 7.8 %collective-permute-start.26 = (bf16[4,64,512]{2,1,0:T(8,128)(2,1)}, bf16[4,64,512]{2,1,0:T(8,128)(2,1)S(1)}, u32[]{:S(2)}, u32[]{:S(2)}) collective-permute-start(bf16[4,64,512]{2,1,0:T(8,128)(2,1)} %pad_maximum_fusion), channel_id=1, source_target_pairs={{0,1},{1,0},{2,3},{3,2},{4,5},{5,4},{6,7},{7,6},{8,9},{9,8},{10,11... | collective-permute-start | bytes 786440 | tf_op jit(solution)/shard_map/ppermute | solution.py:464
  67.0 7.8 %collective-permute-start.27 = (bf16[3,64,512]{2,1,0:T(8,128)(2,1)S(1)}, bf16[3,64,512]{2,1,0:T(8,128)(2,1)S(1)}, u32[]{:S(2)}, u32[]{:S(2)}) collective-permute-start(bf16[3,64,512]{2,1,0:T(8,128)(2,1)S(1)} %constant_dynamic-update-slice_fusion.refs_4_), channel_id=1, source_target_pairs={{0,1},{1,0},{2,3},{3,2},{4,5},{5,4},{6,7},{7,6},{8,9},{9,8},{10,11... | collective-permute-start | bytes 589832 | tf_op jit(solution)/shard_map/ppermute | solution.py:464
  71.5 3.3 %collective-permute-start.30 = (bf16[3,64,512]{2,1,0:T(8,128)(2,1)S(1)}, bf16[3,64,512]{2,1,0:T(8,128)(2,1)S(1)}, u32[]{:S(2)}, u32[]{:S(2)}) collective-permute-start(bf16[3,64,512]{2,1,0:T(8,128)(2,1)S(1)} %collective-permute-done.25.refs_7_), channel_id=1, source_target_pairs={{0,1},{1,0},{2,3},{3,2},{4,5},{5,4},{6,7},{7,6},{8,9},{9,8},{10,11... | collective-permute-start | bytes 589832 | tf_op jit(solution)/shard_map/ppermute | solution.py:464
  74.2 1.6 %collective-permute-start.29 = (bf16[3,64,512]{2,1,0:T(8,128)(2,1)S(1)}, bf16[3,64,512]{2,1,0:T(8,128)(2,1)}, u32[]{:S(2)}, u32[]{:S(2)}) collective-permute-start(bf16[3,64,512]{2,1,0:T(8,128)(2,1)S(1)} %collective-permute-done.24.refs_6_), channel_id=1, source_target_pairs={{0,1},{1,0},{2,3},{3,2},{4,5},{5,4},{6,7},{7,6},{8,9},{9,8},{10,11... | collective-permute-start | bytes 589832 | tf_op jit(solution)/shard_map/ppermute | solution.py:464
  74.3 1.8 %collective-permute-start.28 = (bf16[3,64,512]{2,1,0:T(8,128)(2,1)S(1)}, bf16[3,64,512]{2,1,0:T(8,128)(2,1)}, u32[]{:S(2)}, u32[]{:S(2)}) collective-permute-start(bf16[3,64,512]{2,1,0:T(8,128)(2,1)S(1)} %collective-permute-done.23.refs_5_), channel_id=1, source_target_pairs={{0,1},{1,0},{2,3},{3,2},{4,5},{5,4},{6,7},{7,6},{8,9},{9,8},{10,11... | collective-permute-start | bytes 589832 | tf_op jit(solution)/shard_map/ppermute | solution.py:464
  86.9 2.7 %collective-permute-start.31 = (bf16[2,8,64,512]{3,2,1,0:T(8,128)(2,1)S(1)}, bf16[2,8,64,512]{3,2,1,0:T(8,128)(2,1)S(1)}, u32[]{:S(2)}, u32[]{:S(2)}) collective-permute-start(bf16[2,8,64,512]{3,2,1,0:T(8,128)(2,1)S(1)} %get-tuple-element.67), channel_id=1, source_target_pairs={{0,1},{1,0},{2,3},{3,2},{4,5},{5,4},{6,7},{7,6},{8,9},{9,8},{10,11... | collective-permute-start | bytes 3145736 | tf_op jit(solution)/shard_map/ppermute | solution.py:464
  91.5 10.5 %collective-permute-start.32 = (bf16[3,64,512]{2,1,0:T(8,128)(2,1)S(1)}, bf16[3,64,512]{2,1,0:T(8,128)(2,1)S(1)}, u32[]{:S(2)}, u32[]{:S(2)}) collective-permute-start(bf16[3,64,512]{2,1,0:T(8,128)(2,1)S(1)} %get-tuple-element.71), channel_id=1, source_target_pairs={{0,4},{4,0},{8,12},{12,8},{16,20},{20,16},{24,28},{28,24},{1,5},{5... | collective-permute-start | bytes 589832 | tf_op jit(solution)/shard_map/ppermute | solution.py:464
  92.8 11.7 %collective-permute-start.33 = (bf16[3,64,512]{2,1,0:T(8,128)(2,1)S(1)}, bf16[3,64,512]{2,1,0:T(8,128)(2,1)S(1)}, u32[]{:S(2)}, u32[]{:S(2)}) collective-permute-start(bf16[3,64,512]{2,1,0:T(8,128)(2,1)S(1)} %get-tuple-element.72), channel_id=1, source_target_pairs={{0,2},{1,3},{2,0},{3,1},{4,6},{5,7},{6,4},{7,5},{8,10},{9,11},{10,... | collective-permute-start | bytes 589832 | tf_op jit(solution)/shard_map/ppermute | solution.py:464
  93.8 10.7 %collective-permute-start.34 = (bf16[3,64,512]{2,1,0:T(8,128)(2,1)S(1)}, bf16[3,64,512]{2,1,0:T(8,128)(2,1)S(1)}, u32[]{:S(2)}, u32[]{:S(2)}) collective-permute-start(bf16[3,64,512]{2,1,0:T(8,128)(2,1)S(1)} %get-tuple-element.73), channel_id=1, source_target_pairs={{0,6},{1,7},{2,4},{3,5},{4,2},{5,3},{6,0},{7,1},{8,14},{9,15},{10,... | collective-permute-start | bytes 589832 | tf_op jit(solution)/shard_map/ppermute | solution.py:472
  95.0 12.3 %collective-permute-start.38 = (bf16[64,512]{1,0:T(8,128)(2,1)S(1)}, bf16[64,512]{1,0:T(8,128)(2,1)S(1)}, u32[]{:S(2)}, u32[]{:S(2)}) collective-permute-start(bf16[64,512]{1,0:T(8,128)(2,1)S(1)} %get-tuple-element.78), channel_id=1, source_target_pairs={{0,4},{4,0},{8,12},{12,8},{16,20},{20,16},{24,28},{28,24},{1,5},{5... | collective-permute-start | bytes 196616 | tf_op jit(solution)/shard_map/ppermute | solution.py:464
  96.3 13.4 %collective-permute-start.39 = (bf16[64,512]{1,0:T(8,128)(2,1)S(1)}, bf16[64,512]{1,0:T(8,128)(2,1)S(1)}, u32[]{:S(2)}, u32[]{:S(2)}) collective-permute-start(bf16[64,512]{1,0:T(8,128)(2,1)S(1)} %get-tuple-element.79), channel_id=1, source_target_pairs={{0,2},{1,3},{2,0},{3,1},{4,6},{5,7},{6,4},{7,5},{8,10},{9,11},{10,... | collective-permute-start | bytes 196616 | tf_op jit(solution)/shard_map/ppermute | solution.py:464
  97.3 16.0 %copy-start.6 = (bf16[64,512]{1,0:T(8,128)(2,1)S(1)}, bf16[64,512]{1,0:T(8,128)(2,1)}, u32[]{:S(2)}) copy-start(bf16[64,512]{1,0:T(8,128)(2,1)} %copy-done.5) | copy-start | bytes 196612
  97.3 16.0 %copy-start.10 = (f32[64,512]{1,0:T(8,128)S(1)}, f32[64,512]{1,0:T(8,128)}, u32[]{:S(2)}) copy-start(f32[64,512]{1,0:T(8,128)} %copy-done.9) | copy-start | bytes 393220
  102.0 7.7 %collective-permute-start.40 = (bf16[64,512]{1,0:T(8,128)(2,1)S(1)}, bf16[64,512]{1,0:T(8,128)(2,1)S(1)}, u32[]{:S(2)}, u32[]{:S(2)}) collective-permute-start(bf16[64,512]{1,0:T(8,128)(2,1)S(1)} %get-tuple-element.80), channel_id=1, source_target_pairs={{0,6},{1,7},{2,4},{3,5},{4,2},{5,3},{6,0},{7,1},{8,14},{9,15},{10,... | collective-permute-start | bytes 196616 | tf_op jit(solution)/shard_map/ppermute | solution.py:472
  104.6 5.1 %collective-permute-start.35 = (bf16[64,512]{1,0:T(8,128)(2,1)S(1)}, bf16[64,512]{1,0:T(8,128)(2,1)S(1)}, u32[]{:S(2)}, u32[]{:S(2)}) collective-permute-start(bf16[64,512]{1,0:T(8,128)(2,1)S(1)} %get-tuple-element.75), channel_id=1, source_target_pairs={{0,8},{4,12},{8,0},{12,4},{16,24},{20,28},{24,16},{28,20},{1,9},{5... | collective-permute-start | bytes 196616 | tf_op jit(solution)/shard_map/ppermute | solution.py:464
  104.7 6.6 %collective-permute-start.36 = (bf16[64,512]{1,0:T(8,128)(2,1)S(1)}, bf16[64,512]{1,0:T(8,128)(2,1)S(1)}, u32[]{:S(2)}, u32[]{:S(2)}) collective-permute-start(bf16[64,512]{1,0:T(8,128)(2,1)S(1)} %get-tuple-element.76), channel_id=1, source_target_pairs={{0,16},{4,20},{8,24},{12,28},{16,0},{20,4},{24,8},{28,12},{1,17},{... | collective-permute-start | bytes 196616 | tf_op jit(solution)/shard_map/ppermute | solution.py:464
  107.2 6.1 %collective-permute-start.37 = (bf16[64,512]{1,0:T(8,128)(2,1)S(1)}, bf16[64,512]{1,0:T(8,128)(2,1)S(1)}, u32[]{:S(2)}, u32[]{:S(2)}) collective-permute-start(bf16[64,512]{1,0:T(8,128)(2,1)S(1)} %get-tuple-element.77), channel_id=1, source_target_pairs={{0,24},{4,28},{8,16},{12,20},{16,8},{20,12},{24,0},{28,4},{1,25},{... | collective-permute-start | bytes 196616 | tf_op jit(solution)/shard_map/ppermute | solution.py:464
  (5 other events, 3.6 us)

commit v3 on v2

--- a/solution.py
+++ b/solution.py
@@ -74,6 +74,10 @@
 
 def dot_t(a, b):
     return lax.dot_general(a, b, (((1,), (1,)), ((), ())), preferred_element_type=F32)
+
+
+def dot_0(a, b):
+    return lax.dot_general(a, b, (((0,), (0,)), ((), ())), preferred_element_type=F32)
 
 
 def aligned(index, size):
@@ -124,15 +128,15 @@
         lse_ref[:, cols] = top + jnp.log(jnp.broadcast_to(total, (draft, HD)))
     for h, cols in enumerate(heads):
         out_ref[:, cols] = dot(w_s[h], v_ref[:, cols])
-    accepted = acc_ref.shape[0]
-    pick = (lax.broadcasted_iota(I32, (accepted, draft), 1) == acc_ref[...]).astype(F32).astype(BF16)
-    rows = jnp.concatenate([dot(pick, k_ref[...]), dot(pick, v_ref[...])], axis=0)
-    picks = ids_ref.shape[1]
+    accepted = acc_ref.shape[1]
+    pick = (lax.broadcasted_iota(I32, (draft, accepted), 0) == acc_ref[...]).astype(F32).astype(BF16)
+    rows = jnp.concatenate([dot_0(pick, k_ref[...]), dot_0(pick, v_ref[...])], axis=0)
+    picks = ids_ref.shape[0]
     info = jnp.zeros((draft, STAT), F32)
     for g, part in enumerate((ids_ref[...].astype(F32), *three_parts(rw_ref[...]))):
         lane = lax.broadcasted_iota(I32, (picks, STAT), 1) - INFO - g * picks
         spread = jnp.where(lane == lax.broadcasted_iota(I32, (picks, STAT), 0), 1.0, 0.0)
-        info = info + dot(part.astype(BF16), spread.astype(BF16))
+        info = info + dot_0(part.astype(BF16), spread.astype(BF16))
     info_ref[:, 0:STAT] = info
     for g in range(width // 128):
         part = rows[:, g * 128 : (g + 1) * 128]
@@ -237,7 +241,7 @@
         outs[n][...] = part.astype(outs[n].dtype)
 
 
-def slots_kernel(me_ref, after_hbm, *refs, counts, picks, at_column):
+def slots_kernel(me_ref, after_ref, *refs, counts, picks, at_column):
     pieces, (g_ref, c_ref, w_ref) = refs[: len(counts)], refs[len(counts) :]
     draft = g_ref.shape[2]
     experts = w_ref.shape[0]
@@ -274,13 +278,13 @@
         at += count
 
 
-def mix_kernel(own_ref, a_ref, b_ref, c_ref, after_hbm, mixed_ref, row_ref):
+def mix_kernel(own_ref, a_ref, b_ref, c_ref, after_ref, mixed_ref, row_ref):
     mixed = own_ref[...] + a_ref[...].astype(F32) + b_ref[...].astype(F32) + c_ref[...].astype(F32)
     mixed_ref[...] = mixed
     row_ref[0] = mixed.astype(BF16)
 
 
-def cache_kernel(pos_ref, live_ref, key_ref, value_ref, after_hbm, *refs, counts, accept):
+def cache_kernel(pos_ref, live_ref, key_ref, value_ref, after_ref, *refs, counts, accept):
     pieces, (key_out, value_out, mark_ref, table) = refs[: len(counts)], refs[len(counts) :]
     block, page_len, width = key_ref.shape
     step = pl.program_id(0)
@@ -331,6 +335,11 @@
         cols = pl.ds(pl.multiple_of(cols_ref[first + i] * width, width), width)
         loads.append(pltpu.make_async_copy(down_hbm.at[:, :, cols], down_s.at[i], sems.at[i]))
     return loads
+
+
+def stack_kernel(*refs):
+    for i, block in enumerate(refs[:-1]):
+        refs[-1][i] = block[0]
 
 
 def expert_kernel(
@@ -351,11 +360,11 @@
     ]
     buffers = [down_s, *later]
     loads = [down_loads(cols_ref, first, down_hbm, to, sem) for first, to, sem in zip(steps, buffers, sems)]
-    queue = weights + [(load,) for some in loads for load in some]
-    ahead = 3
-    for some in queue[:ahead]:
+    for some in weights:
         for load in some:
             load.start()
+    for load in loads[0]:
+        load.start()
 
     def columns(n, width):
         return slice(0, width) if n is None else pl.ds(pl.multiple_of((t_ref[0] ^ n) * width, width), width)
@@ -382,23 +391,21 @@
                 step(i * lap + j, j)
 
     each(groups // lap, requests)
-    def arrived(i):
-        for load in queue[i]:
+    for e in range(experts):
+        for load in weights[e]:
             load.wait()
-        for load in queue[i + ahead] if i + ahead < len(queue) else ():
-            load.start()
-
-    for e in range(experts):
-        arrived(e)
+        if e == experts // 2:
+            for load in [v for some in loads[1:] for v in some]:
+                load.start()
         gate = dot(xs[e], gate_s[e])
         up = dot(xs[e], up_s[e])
         active = gate / (1.0 + jnp.exp(-gate)) * up
         active_ref[e] = (active * rw_ref[e, :, 0:1]).astype(BF16)
-    for i in range(len(loads[0])):
-        arrived(experts + i)
+    for i, load in enumerate(loads[0]):
+        load.wait()
         combine_rows(active_ref, down_s.at[i], c_ref, y_s, functools.partial(put, out_ref, i))
-    for i in range(experts + len(loads[0]), len(queue)):
-        arrived(i)
+    for load in [v for some in loads[1:] for v in some]:
+        load.wait()
 
 
 def down_kernel(active_ref, c_ref, add_ref, down_ref, *refs, put):
@@ -480,8 +487,8 @@
 
     if staged:
         own = queries[None]
+        line = [z(own) for z in zs]
         beside = x1(own)
-        line = [z(own) for z in zs]
         every_query = [own, *line, beside, *[x1(b) for b in line]]
     else:
         every_query = [lax.all_gather(queries[None], "seq", axis=0, tiled=True)]
@@ -497,9 +504,9 @@
             tree_mask,
             key_cache,
             value_cache,
-            accepted.reshape(accept, 1),
-            expert_ids,
-            route_weight,
+            accepted,
+            expert_ids.T,
+            route_weight.T,
         ),
         [hbm()] * 6 + [vmem()] * 3,
         [
@@ -562,7 +569,7 @@
         functools.partial(slots_kernel, counts=back_counts, picks=expert_ids.shape[1], at_column=width),
         "slots",
         (me1, parts[0], *back),
-        [smem(), hbm()] + [vmem()] * len(back),
+        [smem(), vmem()] + [vmem()] * len(back),
         [
             shape((seq, experts * CAP, draft), BF16),
             shape((seq, draft, experts * CAP), BF16),
@@ -577,8 +584,8 @@
         mixed, row = call(
             mix_kernel,
             "mix",
-            (parts[0], *got, slot_weight),
-            [vmem()] * 4 + [hbm()],
+            (parts[0], *got, grouped),
+            [vmem()] * 5,
             [shape((draft, width), F32), shape((1, draft, width), BF16)],
             [vmem()] * 2,
             busy=1,
@@ -591,7 +598,9 @@
     if staged:
         line = [z(row) for z in zs]
         near_by = [row, x1(row), y1(row), diagonal(row)]
-        line = jnp.concatenate(line)
+        line = call(
+            stack_kernel, "stack", line, [vmem()] * 3, shape((3, draft, width), BF16), vmem(), limit=1, busy=0
+        )
         far_off = [line, x1(line), y1(line), diagonal(line)]
         rows_in = near_by + far_off + [core(jnp.concatenate(near_by))] + [core(v) for v in far_off]
 
@@ -676,13 +685,13 @@
         functools.partial(cache_kernel, counts=back_counts, accept=accept),
         grid=(pages // block,),
         out_shape=[shape(key_cache.shape, BF16), shape(value_cache.shape, BF16), shape((8, 128), F32)],
-        in_specs=[smem(), smem(), page_spec, page_spec, hbm()] + [vmem()] * len(back),
+        in_specs=[smem(), smem(), page_spec, page_spec, vmem()] + [vmem()] * len(back),
         out_specs=[page_spec, page_spec, pl.BlockSpec((8, 128), lambda p: (0, 0))],
         scratch_shapes=[pltpu.VMEM((seq, 2 * accept, width), BF16)],
         compiler_params=pltpu.CompilerParams(vmem_limit_bytes=big * MIB),
         cost_estimate=pl.CostEstimate(flops=0, bytes_accessed=12_000_000, transcendentals=0),
         name="cache",
-    )(pos, live, in_hbm(key_cache), in_hbm(value_cache), in_hbm(first_sums), *back)
+    )(pos, live, in_hbm(key_cache), in_hbm(value_cache), first_sums, *back)
 
     if not staged:
         sums = lax.psum_scatter(sums, "tensor", scatter_dimension=0, tiled=True)[0]

time: 114 us -> 110 us (0.965)
  local copies, waits for them, and re-layouts: 6.58 us -> 2.71 us
    unnamed x29 -> x19, local copies, waits for them, and re-layouts: 5.84 us -> 2.71 us
    ppermute x37, waiting for transfers between devices: 28 us -> 26.9 us  [hop(): return lambda v: lax.ppermute(v, axis, pairs)]
    pallas_call x8 -> x9, Pallas kernels: 20.9 us -> 20.6 us  [call(): pl.pallas_call(kernel, out_shape=out_shape, in_specs=in_specs, out_specs=...]
  transfers between devices with their start and end apart: 41 -> 41, of which waited for: 17 -> 17; matrix products, arithmetic and copies ran while one was open for 5% -> 3% of each run, Pallas kernels for 7% -> 7%
where the time goes in v3:
time: 110 us
  starting transfers between devices  47.1 us (43%)
  waiting for transfers between devices  30.9 us (28%)
  Pallas kernels  25.2 us (23%)
  other arithmetic  2.94 us (3%)
  local copies, waits for them, and re-layouts  2.71 us (2%)
    ppermute x37, starting transfers between devices, hop(): return lambda v: lax.ppermute(v, axis, pairs)  40.9 us
    ppermute x37, waiting for transfers between devices, hop(): return lambda v: lax.ppermute(v, axis, pairs)  26.9 us
    pallas_call x9, Pallas kernels, call(): pl.pallas_call(kernel, out_shape=out_shape, in_specs=in_specs, out_specs=...  20.6 us
    ppermute x4, starting transfers between devices, diagonal(): lax.ppermute(v, ('seq', 'tensor'), [(i, i ^ flip) for i in range(seq * te...  6.17 us
    pallas_call x1, Pallas kernels, on_device(): pl.pallas_call(functools.partial(cache_kernel, counts=back_counts, accept...  4.66 us
    ppermute x4, waiting for transfers between devices, diagonal(): lax.ppermute(v, ('seq', 'tensor'), [(i, i ^ flip) for i in range(seq * te...  4.01 us
    unnamed x19, local copies, waits for them, and re-layouts  2.71 us
  transfers between devices with their start and end apart: 41, of which 17 were waited for; matrix products, arithmetic and copies ran while one was open for 3% of the time, Pallas kernels for 7%

profile of v3, /device:TPU:0, one launch (start us, length us, event | category | flops | bytes accessed | tf_op | source)
XLA Modules:
  0.0 109.7 jit_solution(13981799498960032300)
XLA Ops:
  0.6 3.0 %collective-permute-start.3 = (bf16[1,64,512]{2,1,0:T(8,128)(2,1)}, bf16[1,64,512]{2,1,0:T(8,128)(2,1)S(1)}, u32[]{:S(2)}, u32[]{:S(2)}) collective-permute-start(bf16[1,64,512]{2,1,0:T(8,128)(2,1)} %bitcast.9), channel_id=1, source_target_pairs={{0,4},{4,0},{8,12},{12,8},{16,20},{20,16},{24,28},{28,24},{1,5},{5... | collective-permute-start | bytes 196616 | tf_op jit(solution)/shard_map/ppermute | solution.py:471
  3.6 3.6 %collective-permute-start.2 = (bf16[1,64,512]{2,1,0:T(8,128)(2,1)}, bf16[1,64,512]{2,1,0:T(8,128)(2,1)S(1)}, u32[]{:S(2)}, u32[]{:S(2)}) collective-permute-start(bf16[1,64,512]{2,1,0:T(8,128)(2,1)} %bitcast.10), channel_id=1, source_target_pairs={{0,24},{4,28},{8,16},{12,20},{16,8},{20,12},{24,0},{28,4},{1,25},{... | collective-permute-start | bytes 196616 | tf_op jit(solution)/shard_map/ppermute | solution.py:471
  7.2 0.8 collective-permute-start
  8.0 0.8 select_reduce_fusion
  8.8 1.9 %collective-permute-done.2.refs_3_ = bf16[1,64,512]{2,1,0:T(8,128)(2,1)S(1)} collective-permute-done((bf16[1,64,512]{2,1,0:T(8,128)(2,1)}, bf16[1,64,512]{2,1,0:T(8,128)(2,1)S(1)}, u32[]{:S(2)}, u32[]{:S(2)}) %collective-permute-start.2) | collective-permute-done | bytes 65568 | tf_op jit(solution)/shard_map/ppermute | solution.py:471
  10.8 2.0 %collective-permute-done.1.refs_2_ = bf16[1,64,512]{2,1,0:T(8,128)(2,1)S(1)} collective-permute-done((bf16[1,64,512]{2,1,0:T(8,128)(2,1)}, bf16[1,64,512]{2,1,0:T(8,128)(2,1)S(1)}, u32[]{:S(2)}, u32[]{:S(2)}) %collective-permute-start.1) | collective-permute-done | bytes 65568 | tf_op jit(solution)/shard_map/ppermute | solution.py:471
  13.4 1.5 %collective-permute-start.4 = (bf16[1,64,512]{2,1,0:T(8,128)(2,1)S(1)}, bf16[1,64,512]{2,1,0:T(8,128)(2,1)S(1)}, u32[]{:S(2)}, u32[]{:S(2)}) collective-permute-start(bf16[1,64,512]{2,1,0:T(8,128)(2,1)S(1)} %collective-permute-done.refs_1_), channel_id=1, source_target_pairs={{0,4},{4,0},{8,12},{12,8},{16,20},{20,16},{24,28},{28,24},{1,5},{5... | collective-permute-start | bytes 196616 | tf_op jit(solution)/shard_map/ppermute | solution.py:471
  17.6 2.1 %near.1 = (f32[64,512]{1,0:T(8,128)S(1)}, f32[64,512]{1,0:T(8,128)S(1)}, f32[64,256]{1,0:T(8,128)S(1)}, bf16[12,128,512]{2,1,0:T(8,128)(2,1)S(1)}, bf16[12,128,512]{2,1,0:T(8,128)(2,1)S(1)}) custom-call(bf16[64,512]{1,0:T(8,128)(2,1)} %q_hbm.1, bf16[64,512]{1,0:T(8,128)(2,1)} %k_hbm.1, bf16[64,512]{1,0:T(8,128)(2,1)} %v_hbm.1, s32[1,64,64]{2,1,0:T(8,128)} %mask_hbm.1, ...), custom_call_target="tpu_custom_call" | custom-call | bytes 6000000 | tf_op jit(solution)/shard_map/near/pallas_call | solution.py:48
  19.8 3.9 %far.1 = (bf16[1,64,768]{2,1,0:T(8,128)(2,1)S(1)}, bf16[1,64,768]{2,1,0:T(8,128)(2,1)S(1)}, bf16[1,64,768]{2,1,0:T(8,128)(2,1)S(1)}, bf16[1,64,768]{2,1,0:T(8,12...) custom-call(s32[12]{0:T(128)S(1)} %get-tuple-element.93.pos_ref, ...), custom_call_target="tpu_custom_call" | custom-call | bytes 15000000 | tf_op jit(solution)/shard_map/far/pallas_call | solution.py:48
  23.7 3.1 %collective-permute-start.8 = (bf16[1,64,768]{2,1,0:T(8,128)(2,1)S(1)}, bf16[1,64,768]{2,1,0:T(8,128)(2,1)S(1)}, u32[]{:S(2)}, u32[]{:S(2)}) collective-permute-start(bf16[1,64,768]{2,1,0:T(8,128)(2,1)S(1)} %get-tuple-element.51), channel_id=1, source_target_pairs={{0,16},{4,20},{8,24},{12,28},{16,0},{20,4},{24,8},{28,12},{1,17},{... | collective-permute-start | bytes 294920 | tf_op jit(solution)/shard_map/ppermute | solution.py:471
  26.8 1.3 %collective-permute-start.9 = (bf16[1,64,768]{2,1,0:T(8,128)(2,1)}, bf16[1,64,768]{2,1,0:T(8,128)(2,1)S(1)}, u32[]{:S(2)}, u32[]{:S(2)}) collective-permute-start(bf16[1,64,768]{2,1,0:T(8,128)(2,1)} %get-tuple-element.52), channel_id=1, source_target_pairs={{0,24},{4,28},{8,16},{12,20},{16,8},{20,12},{24,0},{28,4},{1,25},{... | collective-permute-start | bytes 294920 | tf_op jit(solution)/shard_map/ppermute | solution.py:471
  28.8 4.2 %collective-permute-start.12 = (bf16[1,64,768]{2,1,0:T(8,128)(2,1)}, bf16[1,64,768]{2,1,0:T(8,128)(2,1)S(1)}, u32[]{:S(2)}, u32[]{:S(2)}) collective-permute-start(bf16[1,64,768]{2,1,0:T(8,128)(2,1)} %get-tuple-element.55), channel_id=1, source_target_pairs={{0,20},{4,16},{8,28},{12,24},{16,4},{20,0},{24,12},{28,8},{1,21},{... | collective-permute-start | bytes 294920 | tf_op jit(solution)/shard_map/ppermute | solution.py:471
  33.1 2.2 %collective-permute-done.8.refs_2_ = bf16[1,64,768]{2,1,0:T(8,128)(2,1)S(1)} collective-permute-done((bf16[1,64,768]{2,1,0:T(8,128)(2,1)S(1)}, bf16[1,64,768]{2,1,0:T(8,128)(2,1)S(1)}, u32[]{:S(2)}, u32[]{:S(2)}) %collective-permute-start.8) | collective-permute-done | bytes 98336 | tf_op jit(solution)/shard_map/ppermute | solution.py:471
  35.3 2.1 %collective-permute-start.13 = (bf16[1,64,768]{2,1,0:T(8,128)(2,1)S(1)}, bf16[1,64,768]{2,1,0:T(8,128)(2,1)S(1)}, u32[]{:S(2)}, u32[]{:S(2)}) collective-permute-start(bf16[1,64,768]{2,1,0:T(8,128)(2,1)S(1)} %get-tuple-element.56), channel_id=1, source_target_pairs={{0,28},{4,24},{8,20},{12,16},{16,12},{20,8},{24,4},{28,0},{1,29},{... | collective-permute-start | bytes 294920 | tf_op jit(solution)/shard_map/ppermute | solution.py:471
  37.4 3.4 %collective-permute-done.12.refs_6_ = bf16[1,64,768]{2,1,0:T(8,128)(2,1)S(1)} collective-permute-done((bf16[1,64,768]{2,1,0:T(8,128)(2,1)}, bf16[1,64,768]{2,1,0:T(8,128)(2,1)S(1)}, u32[]{:S(2)}, u32[]{:S(2)}) %collective-permute-start.12) | collective-permute-done | bytes 98336 | tf_op jit(solution)/shard_map/ppermute | solution.py:471
  40.9 1.9 %collective-permute-done.13.refs_7_ = bf16[1,64,768]{2,1,0:T(8,128)(2,1)S(1)} collective-permute-done((bf16[1,64,768]{2,1,0:T(8,128)(2,1)S(1)}, bf16[1,64,768]{2,1,0:T(8,128)(2,1)S(1)}, u32[]{:S(2)}, u32[]{:S(2)}) %collective-permute-start.13) | collective-permute-done | bytes 98336 | tf_op jit(solution)/shard_map/ppermute | solution.py:471
  42.7 1.9 %merge.1 = (f32[64,4]{1,0:T(8,128)S(1)}, f32[64,512]{1,0:T(8,128)S(1)}, bf16[64,512]{1,0:T(8,128)(2,1)S(1)}, bf16[64,512]{1,0:T(8,128)(2,1)S(1)}, bf16[64,512]{1,0:T(8,128)(2,1)S(1)}) custom-call(s32[1]{0:T(128)} %bitcast.t_ref, f32[64,512]{1,0:T(8,128)S(1)} %get-tuple-element.44.near_ref, f32[64,512]{1,0:T(8,128)S(1)} %get-tuple-element.45.lse_ref, ...), custom_call_target="tpu_custom_call" | custom-call | bytes 12000000 | tf_op jit(solution)/shard_map/merge/pallas_call | solution.py:48
  44.7 1.6 %collective-permute-start.15 = (bf16[64,512]{1,0:T(8,128)(2,1)S(1)}, bf16[64,512]{1,0:T(8,128)(2,1)S(1)}, u32[]{:S(2)}, u32[]{:S(2)}) collective-permute-start(bf16[64,512]{1,0:T(8,128)(2,1)S(1)} %get-tuple-element.59), channel_id=1, source_target_pairs={{0,2},{1,3},{2,0},{3,1},{4,6},{5,7},{6,4},{7,5},{8,10},{9,11},{10,... | collective-permute-start | bytes 196616 | tf_op jit(solution)/shard_map/ppermute | solution.py:471
  46.6 0.9 slots.1
  47.4 1.8 %collective-permute-done.15.b_ref = bf16[64,512]{1,0:T(8,128)(2,1)S(1)} collective-permute-done((bf16[64,512]{1,0:T(8,128)(2,1)S(1)}, bf16[64,512]{1,0:T(8,128)(2,1)S(1)}, u32[]{:S(2)}, u32[]{:S(2)}) %collective-permute-start.15) | collective-permute-done | bytes 65568 | tf_op jit(solution)/shard_map/ppermute | solution.py:471
  49.2 1.1 %collective-permute-done.16.c_ref = bf16[64,512]{1,0:T(8,128)(2,1)S(1)} collective-permute-done((bf16[64,512]{1,0:T(8,128)(2,1)S(1)}, bf16[64,512]{1,0:T(8,128)(2,1)S(1)}, u32[]{:S(2)}, u32[]{:S(2)}) %collective-permute-start.16) | collective-permute-done | bytes 65568 | tf_op jit(solution)/shard_map/ppermute | solution.py:471
  50.4 1.5 %collective-permute-start.22 = (bf16[1,64,512]{2,1,0:T(8,128)(2,1)S(1)}, bf16[1,64,512]{2,1,0:T(8,128)(2,1)S(1)}, u32[]{:S(2)}, u32[]{:S(2)}) collective-permute-start(bf16[1,64,512]{2,1,0:T(8,128)(2,1)S(1)} %get-tuple-element.65.refs_0_), channel_id=1, source_target_pairs={{0,24},{4,28},{8,16},{12,20},{16,8},{20,12},{24,0},{28,4},{1,25},{... | collective-permute-start | bytes 196616 | tf_op jit(solution)/shard_map/ppermute | solution.py:471
  51.8 0.9 collective-permute-start.21
  52.7 2.1 %collective-permute-start.20 = (bf16[1,64,512]{2,1,0:T(8,128)(2,1)S(1)}, bf16[1,64,512]{2,1,0:T(8,128)(2,1)S(1)}, u32[]{:S(2)}, u32[]{:S(2)}) collective-permute-start(bf16[1,64,512]{2,1,0:T(8,128)(2,1)S(1)} %get-tuple-element.65.refs_0_), channel_id=1, source_target_pairs={{0,8},{4,12},{8,0},{12,4},{16,24},{20,28},{24,16},{28,20},{1,9},{5... | collective-permute-start | bytes 196616 | tf_op jit(solution)/shard_map/ppermute | solution.py:471
  54.8 1.5 %collective-permute-start.19 = (bf16[1,64,512]{2,1,0:T(8,128)(2,1)S(1)}, bf16[1,64,512]{2,1,0:T(8,128)(2,1)S(1)}, u32[]{:S(2)}, u32[]{:S(2)}) collective-permute-start(bf16[1,64,512]{2,1,0:T(8,128)(2,1)S(1)} %get-tuple-element.65.refs_0_), channel_id=1, source_target_pairs={{0,6},{1,7},{2,4},{3,5},{4,2},{5,3},{6,0},{7,1},{8,14},{9,15},{10,... | collective-permute-start | bytes 196616 | tf_op jit(solution)/shard_map/ppermute | solution.py:479
  57.2 1.1 %collective-permute-start.17 = (bf16[1,64,512]{2,1,0:T(8,128)(2,1)S(1)}, bf16[1,64,512]{2,1,0:T(8,128)(2,1)S(1)}, u32[]{:S(2)}, u32[]{:S(2)}) collective-permute-start(bf16[1,64,512]{2,1,0:T(8,128)(2,1)S(1)} %get-tuple-element.65.refs_0_), channel_id=1, source_target_pairs={{0,4},{4,0},{8,12},{12,8},{16,20},{20,16},{24,28},{28,24},{1,5},{5... | collective-permute-start | bytes 196616 | tf_op jit(solution)/shard_map/ppermute | solution.py:471
  58.3 0.9 collective-permute-done.21.refs_1_
  59.2 2.3 %collective-permute-start.25 = (bf16[3,64,512]{2,1,0:T(8,128)(2,1)S(1)}, bf16[3,64,512]{2,1,0:T(8,128)(2,1)S(1)}, u32[]{:S(2)}, u32[]{:S(2)}) collective-permute-start(bf16[3,64,512]{2,1,0:T(8,128)(2,1)S(1)} %stack.18.refs_4_), channel_id=1, source_target_pairs={{0,6},{1,7},{2,4},{3,5},{4,2},{5,3},{6,0},{7,1},{8,14},{9,15},{10,... | collective-permute-start | bytes 589832 | tf_op jit(solution)/shard_map/ppermute | solution.py:479
  62.8 0.7 pad_maximum_fusion
  64.0 4.0 %collective-permute-done.25.refs_7_ = bf16[3,64,512]{2,1,0:T(8,128)(2,1)S(1)} collective-permute-done((bf16[3,64,512]{2,1,0:T(8,128)(2,1)S(1)}, bf16[3,64,512]{2,1,0:T(8,128)(2,1)S(1)}, u32[]{:S(2)}, u32[]{:S(2)}) %collective-permute-start.25) | collective-permute-done | bytes 196640 | tf_op jit(solution)/shard_map/ppermute | solution.py:479
  68.0 3.2 %collective-permute-done.24.refs_6_ = bf16[3,64,512]{2,1,0:T(8,128)(2,1)S(1)} collective-permute-done((bf16[3,64,512]{2,1,0:T(8,128)(2,1)S(1)}, bf16[3,64,512]{2,1,0:T(8,128)(2,1)S(1)}, u32[]{:S(2)}, u32[]{:S(2)}) %collective-permute-start.24) | collective-permute-done | bytes 196640 | tf_op jit(solution)/shard_map/ppermute | solution.py:471
  71.8 1.0 collective-permute-done.29.refs_11_
  73.1 10.4 %experts.1 = (bf16[8,128,256]{2,1,0:T(8,128)(2,1)S(1)}, bf16[2,8,64,512]{3,2,1,0:T(8,128)(2,1)S(1)}, bf16[2,8,256,512]{3,2,1,0:T(8,128)(2,1)S(1)}) custom-call(s32[1]{0:T(128)} %bitcast.t_ref, s32[4]{0:T(128)S(1)} %pad_add_fusion.cols_ref, f32[1,2048]{1,0:T(1,128)S(1)} %bitcast.14, bf16[8,128,64]{2,1,0:T(8,128)(2,1)S(1)} %get-tuple-element.61.after_ref.g_ref, ...), custom_call_target="tpu_custom_call" | custom-call | bytes 27000000 | tf_op jit(solution)/shard_map/experts/pallas_call | solution.py:48
  83.8 2.4 %collective-permute-done.31.add_ref = bf16[2,8,64,512]{3,2,1,0:T(8,128)(2,1)S(1)} collective-permute-done((bf16[2,8,64,512]{3,2,1,0:T(8,128)(2,1)S(1)}, bf16[2,8,64,512]{3,2,1,0:T(8,128)(2,1)S(1)}, u32[]{:S(2)}, u32[]{:S(2)}) %collective-permute-start.31) | collective-permute-done | bytes 1048608 | tf_op jit(solution)/shard_map/ppermute | solution.py:471
  86.2 1.3 %down.1 = (bf16[64,512]{1,0:T(8,128)(2,1)S(1)}, bf16[64,512]{1,0:T(8,128)(2,1)S(1)}, bf16[64,512]{1,0:T(8,128)(2,1)S(1)}, bf16[64,512]{1,0:T(8,128)(2,1)S(1)}, b...) custom-call(bf16[8,128,256]{2,1,0:T(8,128)(2,1)S(1)} %get-tuple-elem, ...), custom_call_target="tpu_custom_call" | custom-call | bytes 9000000 | tf_op jit(solution)/shard_map/down/pallas_call | solution.py:48
  87.5 0.9 collective-permute-start.32
  88.5 1.4 %collective-permute-start.33 = (bf16[3,64,512]{2,1,0:T(8,128)(2,1)S(1)}, bf16[3,64,512]{2,1,0:T(8,128)(2,1)S(1)}, u32[]{:S(2)}, u32[]{:S(2)}) collective-permute-start(bf16[3,64,512]{2,1,0:T(8,128)(2,1)S(1)} %get-tuple-element.72), channel_id=1, source_target_pairs={{0,2},{1,3},{2,0},{3,1},{4,6},{5,7},{6,4},{7,5},{8,10},{9,11},{10,... | collective-permute-start | bytes 589832 | tf_op jit(solution)/shard_map/ppermute | solution.py:471
  89.9 1.2 %collective-permute-start.34 = (bf16[3,64,512]{2,1,0:T(8,128)(2,1)S(1)}, bf16[3,64,512]{2,1,0:T(8,128)(2,1)S(1)}, u32[]{:S(2)}, u32[]{:S(2)}) collective-permute-start(bf16[3,64,512]{2,1,0:T(8,128)(2,1)S(1)} %get-tuple-element.73), channel_id=1, source_target_pairs={{0,6},{1,7},{2,4},{3,5},{4,2},{5,3},{6,0},{7,1},{8,14},{9,15},{10,... | collective-permute-start | bytes 589832 | tf_op jit(solution)/shard_map/ppermute | solution.py:479
  91.1 0.9 collective-permute-start.38
  91.9 1.4 %collective-permute-start.39 = (bf16[64,512]{1,0:T(8,128)(2,1)S(1)}, bf16[64,512]{1,0:T(8,128)(2,1)S(1)}, u32[]{:S(2)}, u32[]{:S(2)}) collective-permute-start(bf16[64,512]{1,0:T(8,128)(2,1)S(1)} %get-tuple-element.79), channel_id=1, source_target_pairs={{0,2},{1,3},{2,0},{3,1},{4,6},{5,7},{6,4},{7,5},{8,10},{9,11},{10,... | collective-permute-start | bytes 196616 | tf_op jit(solution)/shard_map/ppermute | solution.py:471
  93.4 4.7 %cache.1 = (bf16[12,128,512]{2,1,0:T(8,128)(2,1)}, bf16[12,128,512]{2,1,0:T(8,128)(2,1)}, f32[8,128]{1,0:T(8,128)S(1)}) custom-call(s32[12]{0:T(128)S(1)} %get-tuple-element.93.pos_ref, s32[12]{0:T(128)S(1)} %get-tuple-element.92.live_ref, bf16[12,128,512]{2,1,0:T(8,128)(2,1)} %key_ref.1, bf16[12,128,512]{2,1,0:T(8,128)(2,1)} %value_ref.1, ...), custom_call_target="tpu_custom_call" | custom-call | bytes 12000000 | tf_op jit(solution)/shard_map/cache/pallas_call | solution.py:684
  98.1 1.2 %collective-permute-start.40 = (bf16[64,512]{1,0:T(8,128)(2,1)S(1)}, bf16[64,512]{1,0:T(8,128)(2,1)S(1)}, u32[]{:S(2)}, u32[]{:S(2)}) collective-permute-start(bf16[64,512]{1,0:T(8,128)(2,1)S(1)} %get-tuple-element.80), channel_id=1, source_target_pairs={{0,6},{1,7},{2,4},{3,5},{4,2},{5,3},{6,0},{7,1},{8,14},{9,15},{10,... | collective-permute-start | bytes 196616 | tf_op jit(solution)/shard_map/ppermute | solution.py:479
  99.3 0.9 collective-permute-done.33.y_ref
  100.5 2.4 %collective-permute-start.36 = (bf16[64,512]{1,0:T(8,128)(2,1)S(1)}, bf16[64,512]{1,0:T(8,128)(2,1)S(1)}, u32[]{:S(2)}, u32[]{:S(2)}) collective-permute-start(bf16[64,512]{1,0:T(8,128)(2,1)S(1)} %get-tuple-element.76), channel_id=1, source_target_pairs={{0,16},{4,20},{8,24},{12,28},{16,0},{20,4},{24,8},{28,12},{1,17},{... | collective-permute-start | bytes 196616 | tf_op jit(solution)/shard_map/ppermute | solution.py:471
  102.9 1.8 %collective-permute-start.37 = (bf16[64,512]{1,0:T(8,128)(2,1)S(1)}, bf16[64,512]{1,0:T(8,128)(2,1)S(1)}, u32[]{:S(2)}, u32[]{:S(2)}) collective-permute-start(bf16[64,512]{1,0:T(8,128)(2,1)S(1)} %get-tuple-element.77), channel_id=1, source_target_pairs={{0,24},{4,28},{8,16},{12,20},{16,8},{20,12},{24,0},{28,4},{1,25},{... | collective-permute-start | bytes 196616 | tf_op jit(solution)/shard_map/ppermute | solution.py:471
  105.4 1.7 %collective-permute-done.36 = bf16[64,512]{1,0:T(8,128)(2,1)S(1)} collective-permute-done((bf16[64,512]{1,0:T(8,128)(2,1)S(1)}, bf16[64,512]{1,0:T(8,128)(2,1)S(1)}, u32[]{:S(2)}, u32[]{:S(2)}) %collective-permute-start.36) | collective-permute-done | bytes 65568 | tf_op jit(solution)/shard_map/ppermute | solution.py:471
  107.1 1.8 %collective-permute-done.37 = bf16[64,512]{1,0:T(8,128)(2,1)S(1)} collective-permute-done((bf16[64,512]{1,0:T(8,128)(2,1)S(1)}, bf16[64,512]{1,0:T(8,128)(2,1)S(1)}, u32[]{:S(2)}, u32[]{:S(2)}) %collective-permute-start.37) | collective-permute-done | bytes 65568 | tf_op jit(solution)/shard_map/ppermute | solution.py:471
  109.0 0.7 add_convert_fusion
  (68 shorter events, 9.5 us)
Async XLA Ops:
  0.6 19.1 %collective-permute-start.3 = (bf16[1,64,512]{2,1,0:T(8,128)(2,1)}, bf16[1,64,512]{2,1,0:T(8,128)(2,1)S(1)}, u32[]{:S(2)}, u32[]{:S(2)}) collective-permute-start(bf16[1,64,512]{2,1,0:T(8,128)(2,1)} %bitcast.9), channel_id=1, source_target_pairs={{0,4},{4,0},{8,12},{12,8},{16,20},{20,16},{24,28},{28,24},{1,5},{5... | collective-permute-start | bytes 196616 | tf_op jit(solution)/shard_map/ppermute | solution.py:471
  3.6 7.1 %collective-permute-start.2 = (bf16[1,64,512]{2,1,0:T(8,128)(2,1)}, bf16[1,64,512]{2,1,0:T(8,128)(2,1)S(1)}, u32[]{:S(2)}, u32[]{:S(2)}) collective-permute-start(bf16[1,64,512]{2,1,0:T(8,128)(2,1)} %bitcast.10), channel_id=1, source_target_pairs={{0,24},{4,28},{8,16},{12,20},{16,8},{20,12},{24,0},{28,4},{1,25},{... | collective-permute-start | bytes 196616 | tf_op jit(solution)/shard_map/ppermute | solution.py:471
  7.2 5.6 %collective-permute-start.1 = (bf16[1,64,512]{2,1,0:T(8,128)(2,1)}, bf16[1,64,512]{2,1,0:T(8,128)(2,1)S(1)}, u32[]{:S(2)}, u32[]{:S(2)}) collective-permute-start(bf16[1,64,512]{2,1,0:T(8,128)(2,1)} %bitcast.11), channel_id=1, source_target_pairs={{0,16},{4,20},{8,24},{12,28},{16,0},{20,4},{24,8},{28,12},{1,17},{... | collective-permute-start | bytes 196616 | tf_op jit(solution)/shard_map/ppermute | solution.py:471
  7.2 6.2 %collective-permute-start = (bf16[1,64,512]{2,1,0:T(8,128)(2,1)}, bf16[1,64,512]{2,1,0:T(8,128)(2,1)S(1)}, u32[]{:S(2)}, u32[]{:S(2)}) collective-permute-start(bf16[1,64,512]{2,1,0:T(8,128)(2,1)} %bitcast.12), channel_id=1, source_target_pairs={{0,8},{4,12},{8,0},{12,4},{16,24},{20,28},{24,16},{28,20},{1,9},{5... | collective-permute-start | bytes 196616 | tf_op jit(solution)/shard_map/ppermute | solution.py:471
  10.7 9.0 %collective-permute-start.6 = (bf16[1,64,512]{2,1,0:T(8,128)(2,1)S(1)}, bf16[1,64,512]{2,1,0:T(8,128)(2,1)S(1)}, u32[]{:S(2)}, u32[]{:S(2)}) collective-permute-start(bf16[1,64,512]{2,1,0:T(8,128)(2,1)S(1)} %collective-permute-done.2.refs_3_), channel_id=1, source_target_pairs={{0,4},{4,0},{8,12},{12,8},{16,20},{20,16},{24,28},{28,24},{1,5},{5... | collective-permute-start | bytes 196616 | tf_op jit(solution)/shard_map/ppermute | solution.py:471
  12.9 6.9 %collective-permute-start.5 = (bf16[1,64,512]{2,1,0:T(8,128)(2,1)S(1)}, bf16[1,64,512]{2,1,0:T(8,128)(2,1)S(1)}, u32[]{:S(2)}, u32[]{:S(2)}) collective-permute-start(bf16[1,64,512]{2,1,0:T(8,128)(2,1)S(1)} %collective-permute-done.1.refs_2_), channel_id=1, source_target_pairs={{0,4},{4,0},{8,12},{12,8},{16,20},{20,16},{24,28},{28,24},{1,5},{5... | collective-permute-start | bytes 196616 | tf_op jit(solution)/shard_map/ppermute | solution.py:471
  13.4 6.3 %collective-permute-start.4 = (bf16[1,64,512]{2,1,0:T(8,128)(2,1)S(1)}, bf16[1,64,512]{2,1,0:T(8,128)(2,1)S(1)}, u32[]{:S(2)}, u32[]{:S(2)}) collective-permute-start(bf16[1,64,512]{2,1,0:T(8,128)(2,1)S(1)} %collective-permute-done.refs_1_), channel_id=1, source_target_pairs={{0,4},{4,0},{8,12},{12,8},{16,20},{20,16},{24,28},{28,24},{1,5},{5... | collective-permute-start | bytes 196616 | tf_op jit(solution)/shard_map/ppermute | solution.py:471
  15.6 0.7 copy-start.6
  17.6 2.2 %copy-start.1 = (bf16[64,512]{1,0:T(8,128)(2,1)S(1)}, bf16[64,512]{1,0:T(8,128)(2,1)}, u32[]{:S(2)}) copy-start(bf16[64,512]{1,0:T(8,128)(2,1)} %q_hbm.1) | copy-start | bytes 196612
  19.8 23.0 %copy-start = (bf16[512,2048]{1,0:T(8,128)(2,1)S(1)}, bf16[512,2048]{1,0:T(8,128)(2,1)}, u32[]{:S(2)}) copy-start(bf16[512,2048]{1,0:T(8,128)(2,1)} %w_ref.1) | copy-start | bytes 6291460
  19.8 23.0 %copy-start.2 = (bf16[64,2048]{1,0:T(8,128)(2,1)S(1)}, bf16[64,2048]{1,0:T(8,128)(2,1)}, u32[]{:S(2)}) copy-start(bf16[64,2048]{1,0:T(8,128)(2,1)} %hidden_ref.1) | copy-start | bytes 786436
  23.7 5.2 %collective-permute-start.7 = (bf16[1,64,768]{2,1,0:T(8,128)(2,1)S(1)}, bf16[1,64,768]{2,1,0:T(8,128)(2,1)S(1)}, u32[]{:S(2)}, u32[]{:S(2)}) collective-permute-start(bf16[1,64,768]{2,1,0:T(8,128)(2,1)S(1)} %get-tuple-element.50), channel_id=1, source_target_pairs={{0,8},{4,12},{8,0},{12,4},{16,24},{20,28},{24,16},{28,20},{1,9},{5... | collective-permute-start | bytes 294920 | tf_op jit(solution)/shard_map/ppermute | solution.py:471
  23.7 11.6 %collective-permute-start.8 = (bf16[1,64,768]{2,1,0:T(8,128)(2,1)S(1)}, bf16[1,64,768]{2,1,0:T(8,128)(2,1)S(1)}, u32[]{:S(2)}, u32[]{:S(2)}) collective-permute-start(bf16[1,64,768]{2,1,0:T(8,128)(2,1)S(1)} %get-tuple-element.51), channel_id=1, source_target_pairs={{0,16},{4,20},{8,24},{12,28},{16,0},{20,4},{24,8},{28,12},{1,17},{... | collective-permute-start | bytes 294920 | tf_op jit(solution)/shard_map/ppermute | solution.py:471
  26.8 10.6 %collective-permute-start.9 = (bf16[1,64,768]{2,1,0:T(8,128)(2,1)}, bf16[1,64,768]{2,1,0:T(8,128)(2,1)S(1)}, u32[]{:S(2)}, u32[]{:S(2)}) collective-permute-start(bf16[1,64,768]{2,1,0:T(8,128)(2,1)} %get-tuple-element.52), channel_id=1, source_target_pairs={{0,24},{4,28},{8,16},{12,20},{16,8},{20,12},{24,0},{28,4},{1,25},{... | collective-permute-start | bytes 294920 | tf_op jit(solution)/shard_map/ppermute | solution.py:471
  28.1 9.3 %collective-permute-start.10 = (bf16[1,64,768]{2,1,0:T(8,128)(2,1)}, bf16[1,64,768]{2,1,0:T(8,128)(2,1)S(1)}, u32[]{:S(2)}, u32[]{:S(2)}) collective-permute-start(bf16[1,64,768]{2,1,0:T(8,128)(2,1)} %get-tuple-element.53), channel_id=1, source_target_pairs={{0,4},{4,0},{8,12},{12,8},{16,20},{20,16},{24,28},{28,24},{1,5},{5... | collective-permute-start | bytes 294920 | tf_op jit(solution)/shard_map/ppermute | solution.py:471
  28.6 8.8 %collective-permute-start.11 = (bf16[1,64,768]{2,1,0:T(8,128)(2,1)}, bf16[1,64,768]{2,1,0:T(8,128)(2,1)S(1)}, u32[]{:S(2)}, u32[]{:S(2)}) collective-permute-start(bf16[1,64,768]{2,1,0:T(8,128)(2,1)} %get-tuple-element.54), channel_id=1, source_target_pairs={{0,12},{4,8},{8,4},{12,0},{16,28},{20,24},{24,20},{28,16},{1,13},{... | collective-permute-start | bytes 294920 | tf_op jit(solution)/shard_map/ppermute | solution.py:471
  28.8 12.0 %collective-permute-start.12 = (bf16[1,64,768]{2,1,0:T(8,128)(2,1)}, bf16[1,64,768]{2,1,0:T(8,128)(2,1)S(1)}, u32[]{:S(2)}, u32[]{:S(2)}) collective-permute-start(bf16[1,64,768]{2,1,0:T(8,128)(2,1)} %get-tuple-element.55), channel_id=1, source_target_pairs={{0,20},{4,16},{8,28},{12,24},{16,4},{20,0},{24,12},{28,8},{1,21},{... | collective-permute-start | bytes 294920 | tf_op jit(solution)/shard_map/ppermute | solution.py:471
  35.3 7.4 %collective-permute-start.13 = (bf16[1,64,768]{2,1,0:T(8,128)(2,1)S(1)}, bf16[1,64,768]{2,1,0:T(8,128)(2,1)S(1)}, u32[]{:S(2)}, u32[]{:S(2)}) collective-permute-start(bf16[1,64,768]{2,1,0:T(8,128)(2,1)S(1)} %get-tuple-element.56), channel_id=1, source_target_pairs={{0,28},{4,24},{8,20},{12,16},{16,12},{20,8},{24,4},{28,0},{1,29},{... | collective-permute-start | bytes 294920 | tf_op jit(solution)/shard_map/ppermute | solution.py:471
  44.6 28.5 %copy-start.5 = (f32[2048]{0:T(1024)S(1)}, f32[2048]{0:T(1024)}, u32[]{:S(2)}) copy-start(f32[2048]{0:T(1024)} %param.30) | copy-start | bytes 24580
  44.6 2.8 %collective-permute-start.14 = (bf16[64,512]{1,0:T(8,128)(2,1)S(1)}, bf16[64,512]{1,0:T(8,128)(2,1)S(1)}, u32[]{:S(2)}, u32[]{:S(2)}) collective-permute-start(bf16[64,512]{1,0:T(8,128)(2,1)S(1)} %get-tuple-element.58), channel_id=1, source_target_pairs={{0,1},{1,0},{2,3},{3,2},{4,5},{5,4},{6,7},{7,6},{8,9},{9,8},{10,11... | collective-permute-start | bytes 196616 | tf_op jit(solution)/shard_map/ppermute | solution.py:471
  44.7 4.5 %collective-permute-start.15 = (bf16[64,512]{1,0:T(8,128)(2,1)S(1)}, bf16[64,512]{1,0:T(8,128)(2,1)S(1)}, u32[]{:S(2)}, u32[]{:S(2)}) collective-permute-start(bf16[64,512]{1,0:T(8,128)(2,1)S(1)} %get-tuple-element.59), channel_id=1, source_target_pairs={{0,2},{1,3},{2,0},{3,1},{4,6},{5,7},{6,4},{7,5},{8,10},{9,11},{10,... | collective-permute-start | bytes 196616 | tf_op jit(solution)/shard_map/ppermute | solution.py:471
  46.3 4.0 %collective-permute-start.16 = (bf16[64,512]{1,0:T(8,128)(2,1)S(1)}, bf16[64,512]{1,0:T(8,128)(2,1)S(1)}, u32[]{:S(2)}, u32[]{:S(2)}) collective-permute-start(bf16[64,512]{1,0:T(8,128)(2,1)S(1)} %get-tuple-element.60), channel_id=1, source_target_pairs={{0,3},{1,2},{2,1},{3,0},{4,7},{5,6},{6,5},{7,4},{8,11},{9,10},{10,... | collective-permute-start | bytes 196616 | tf_op jit(solution)/shard_map/ppermute | solution.py:471
  50.4 20.9 %copy-start.3 = (f32[64,512]{1,0:T(8,128)}, f32[64,512]{1,0:T(8,128)S(1)}, u32[]{:S(2)}) copy-start(f32[64,512]{1,0:T(8,128)S(1)} %get-tuple-element.62) | copy-start | bytes 393220
  50.4 6.8 %collective-permute-start.22 = (bf16[1,64,512]{2,1,0:T(8,128)(2,1)S(1)}, bf16[1,64,512]{2,1,0:T(8,128)(2,1)S(1)}, u32[]{:S(2)}, u32[]{:S(2)}) collective-permute-start(bf16[1,64,512]{2,1,0:T(8,128)(2,1)S(1)} %get-tuple-element.65.refs_0_), channel_id=1, source_target_pairs={{0,24},{4,28},{8,16},{12,20},{16,8},{20,12},{24,0},{28,4},{1,25},{... | collective-permute-start | bytes 196616 | tf_op jit(solution)/shard_map/ppermute | solution.py:471
  51.8 7.4 %collective-permute-start.21 = (bf16[1,64,512]{2,1,0:T(8,128)(2,1)S(1)}, bf16[1,64,512]{2,1,0:T(8,128)(2,1)S(1)}, u32[]{:S(2)}, u32[]{:S(2)}) collective-permute-start(bf16[1,64,512]{2,1,0:T(8,128)(2,1)S(1)} %get-tuple-element.65.refs_0_), channel_id=1, source_target_pairs={{0,16},{4,20},{8,24},{12,28},{16,0},{20,4},{24,8},{28,12},{1,17},{... | collective-permute-start | bytes 196616 | tf_op jit(solution)/shard_map/ppermute | solution.py:471
  52.7 6.5 %collective-permute-start.20 = (bf16[1,64,512]{2,1,0:T(8,128)(2,1)S(1)}, bf16[1,64,512]{2,1,0:T(8,128)(2,1)S(1)}, u32[]{:S(2)}, u32[]{:S(2)}) collective-permute-start(bf16[1,64,512]{2,1,0:T(8,128)(2,1)S(1)} %get-tuple-element.65.refs_0_), channel_id=1, source_target_pairs={{0,8},{4,12},{8,0},{12,4},{16,24},{20,28},{24,16},{28,20},{1,9},{5... | collective-permute-start | bytes 196616 | tf_op jit(solution)/shard_map/ppermute | solution.py:471
  54.8 7.3 %collective-permute-start.19 = (bf16[1,64,512]{2,1,0:T(8,128)(2,1)S(1)}, bf16[1,64,512]{2,1,0:T(8,128)(2,1)S(1)}, u32[]{:S(2)}, u32[]{:S(2)}) collective-permute-start(bf16[1,64,512]{2,1,0:T(8,128)(2,1)S(1)} %get-tuple-element.65.refs_0_), channel_id=1, source_target_pairs={{0,6},{1,7},{2,4},{3,5},{4,2},{5,3},{6,0},{7,1},{8,14},{9,15},{10,... | collective-permute-start | bytes 196616 | tf_op jit(solution)/shard_map/ppermute | solution.py:479
  56.3 6.5 %collective-permute-start.18 = (bf16[1,64,512]{2,1,0:T(8,128)(2,1)S(1)}, bf16[1,64,512]{2,1,0:T(8,128)(2,1)S(1)}, u32[]{:S(2)}, u32[]{:S(2)}) collective-permute-start(bf16[1,64,512]{2,1,0:T(8,128)(2,1)S(1)} %get-tuple-element.65.refs_0_), channel_id=1, source_target_pairs={{0,2},{1,3},{2,0},{3,1},{4,6},{5,7},{6,4},{7,5},{8,10},{9,11},{10,... | collective-permute-start | bytes 196616 | tf_op jit(solution)/shard_map/ppermute | solution.py:471
  57.2 5.6 %collective-permute-start.17 = (bf16[1,64,512]{2,1,0:T(8,128)(2,1)S(1)}, bf16[1,64,512]{2,1,0:T(8,128)(2,1)S(1)}, u32[]{:S(2)}, u32[]{:S(2)}) collective-permute-start(bf16[1,64,512]{2,1,0:T(8,128)(2,1)S(1)} %get-tuple-element.65.refs_0_), channel_id=1, source_target_pairs={{0,4},{4,0},{8,12},{12,8},{16,20},{20,16},{24,28},{28,24},{1,5},{5... | collective-permute-start | bytes 196616 | tf_op jit(solution)/shard_map/ppermute | solution.py:471
  59.2 8.8 %collective-permute-start.25 = (bf16[3,64,512]{2,1,0:T(8,128)(2,1)S(1)}, bf16[3,64,512]{2,1,0:T(8,128)(2,1)S(1)}, u32[]{:S(2)}, u32[]{:S(2)}) collective-permute-start(bf16[3,64,512]{2,1,0:T(8,128)(2,1)S(1)} %stack.18.refs_4_), channel_id=1, source_target_pairs={{0,6},{1,7},{2,4},{3,5},{4,2},{5,3},{6,0},{7,1},{8,14},{9,15},{10,... | collective-permute-start | bytes 589832 | tf_op jit(solution)/shard_map/ppermute | solution.py:479
  61.5 9.7 %collective-permute-start.24 = (bf16[3,64,512]{2,1,0:T(8,128)(2,1)S(1)}, bf16[3,64,512]{2,1,0:T(8,128)(2,1)S(1)}, u32[]{:S(2)}, u32[]{:S(2)}) collective-permute-start(bf16[3,64,512]{2,1,0:T(8,128)(2,1)S(1)} %stack.18.refs_4_), channel_id=1, source_target_pairs={{0,2},{1,3},{2,0},{3,1},{4,6},{5,7},{6,4},{7,5},{8,10},{9,11},{10,... | collective-permute-start | bytes 589832 | tf_op jit(solution)/shard_map/ppermute | solution.py:471
  62.2 9.1 %collective-permute-start.23 = (bf16[3,64,512]{2,1,0:T(8,128)(2,1)S(1)}, bf16[3,64,512]{2,1,0:T(8,128)(2,1)S(1)}, u32[]{:S(2)}, u32[]{:S(2)}) collective-permute-start(bf16[3,64,512]{2,1,0:T(8,128)(2,1)S(1)} %stack.18.refs_4_), channel_id=1, source_target_pairs={{0,4},{4,0},{8,12},{12,8},{16,20},{20,16},{24,28},{28,24},{1,5},{5... | collective-permute-start | bytes 589832 | tf_op jit(solution)/shard_map/ppermute | solution.py:471
  63.5 8.3 %collective-permute-start.26 = (bf16[4,64,512]{2,1,0:T(8,128)(2,1)}, bf16[4,64,512]{2,1,0:T(8,128)(2,1)S(1)}, u32[]{:S(2)}, u32[]{:S(2)}) collective-permute-start(bf16[4,64,512]{2,1,0:T(8,128)(2,1)} %pad_maximum_fusion), channel_id=1, source_target_pairs={{0,1},{1,0},{2,3},{3,2},{4,5},{5,4},{6,7},{7,6},{8,9},{9,8},{10,11... | collective-permute-start | bytes 786440 | tf_op jit(solution)/shard_map/ppermute | solution.py:471
  63.5 8.3 %collective-permute-start.27 = (bf16[3,64,512]{2,1,0:T(8,128)(2,1)S(1)}, bf16[3,64,512]{2,1,0:T(8,128)(2,1)S(1)}, u32[]{:S(2)}, u32[]{:S(2)}) collective-permute-start(bf16[3,64,512]{2,1,0:T(8,128)(2,1)S(1)} %stack.18.refs_4_), channel_id=1, source_target_pairs={{0,1},{1,0},{2,3},{3,2},{4,5},{5,4},{6,7},{7,6},{8,9},{9,8},{10,11... | collective-permute-start | bytes 589832 | tf_op jit(solution)/shard_map/ppermute | solution.py:471
  68.0 3.8 %collective-permute-start.30 = (bf16[3,64,512]{2,1,0:T(8,128)(2,1)S(1)}, bf16[3,64,512]{2,1,0:T(8,128)(2,1)S(1)}, u32[]{:S(2)}, u32[]{:S(2)}) collective-permute-start(bf16[3,64,512]{2,1,0:T(8,128)(2,1)S(1)} %collective-permute-done.25.refs_7_), channel_id=1, source_target_pairs={{0,1},{1,0},{2,3},{3,2},{4,5},{5,4},{6,7},{7,6},{8,9},{9,8},{10,11... | collective-permute-start | bytes 589832 | tf_op jit(solution)/shard_map/ppermute | solution.py:471
  71.2 1.6 %collective-permute-start.29 = (bf16[3,64,512]{2,1,0:T(8,128)(2,1)S(1)}, bf16[3,64,512]{2,1,0:T(8,128)(2,1)}, u32[]{:S(2)}, u32[]{:S(2)}) collective-permute-start(bf16[3,64,512]{2,1,0:T(8,128)(2,1)S(1)} %collective-permute-done.24.refs_6_), channel_id=1, source_target_pairs={{0,1},{1,0},{2,3},{3,2},{4,5},{5,4},{6,7},{7,6},{8,9},{9,8},{10,11... | collective-permute-start | bytes 589832 | tf_op jit(solution)/shard_map/ppermute | solution.py:471
  71.3 1.8 %collective-permute-start.28 = (bf16[3,64,512]{2,1,0:T(8,128)(2,1)S(1)}, bf16[3,64,512]{2,1,0:T(8,128)(2,1)}, u32[]{:S(2)}, u32[]{:S(2)}) collective-permute-start(bf16[3,64,512]{2,1,0:T(8,128)(2,1)S(1)} %collective-permute-done.23.refs_5_), channel_id=1, source_target_pairs={{0,1},{1,0},{2,3},{3,2},{4,5},{5,4},{6,7},{7,6},{8,9},{9,8},{10,11... | collective-permute-start | bytes 589832 | tf_op jit(solution)/shard_map/ppermute | solution.py:471
  83.5 2.7 %collective-permute-start.31 = (bf16[2,8,64,512]{3,2,1,0:T(8,128)(2,1)S(1)}, bf16[2,8,64,512]{3,2,1,0:T(8,128)(2,1)S(1)}, u32[]{:S(2)}, u32[]{:S(2)}) collective-permute-start(bf16[2,8,64,512]{3,2,1,0:T(8,128)(2,1)S(1)} %get-tuple-element.67), channel_id=1, source_target_pairs={{0,1},{1,0},{2,3},{3,2},{4,5},{5,4},{6,7},{7,6},{8,9},{9,8},{10,11... | collective-permute-start | bytes 3145736 | tf_op jit(solution)/shard_map/ppermute | solution.py:471
  87.5 10.5 %collective-permute-start.32 = (bf16[3,64,512]{2,1,0:T(8,128)(2,1)S(1)}, bf16[3,64,512]{2,1,0:T(8,128)(2,1)S(1)}, u32[]{:S(2)}, u32[]{:S(2)}) collective-permute-start(bf16[3,64,512]{2,1,0:T(8,128)(2,1)S(1)} %get-tuple-element.71), channel_id=1, source_target_pairs={{0,4},{4,0},{8,12},{12,8},{16,20},{20,16},{24,28},{28,24},{1,5},{5... | collective-permute-start | bytes 589832 | tf_op jit(solution)/shard_map/ppermute | solution.py:471
  88.5 11.7 %collective-permute-start.33 = (bf16[3,64,512]{2,1,0:T(8,128)(2,1)S(1)}, bf16[3,64,512]{2,1,0:T(8,128)(2,1)S(1)}, u32[]{:S(2)}, u32[]{:S(2)}) collective-permute-start(bf16[3,64,512]{2,1,0:T(8,128)(2,1)S(1)} %get-tuple-element.72), channel_id=1, source_target_pairs={{0,2},{1,3},{2,0},{3,1},{4,6},{5,7},{6,4},{7,5},{8,10},{9,11},{10,... | collective-permute-start | bytes 589832 | tf_op jit(solution)/shard_map/ppermute | solution.py:471
  89.9 10.3 %collective-permute-start.34 = (bf16[3,64,512]{2,1,0:T(8,128)(2,1)S(1)}, bf16[3,64,512]{2,1,0:T(8,128)(2,1)S(1)}, u32[]{:S(2)}, u32[]{:S(2)}) collective-permute-start(bf16[3,64,512]{2,1,0:T(8,128)(2,1)S(1)} %get-tuple-element.73), channel_id=1, source_target_pairs={{0,6},{1,7},{2,4},{3,5},{4,2},{5,3},{6,0},{7,1},{8,14},{9,15},{10,... | collective-permute-start | bytes 589832 | tf_op jit(solution)/shard_map/ppermute | solution.py:479
  91.1 11.8 %collective-permute-start.38 = (bf16[64,512]{1,0:T(8,128)(2,1)S(1)}, bf16[64,512]{1,0:T(8,128)(2,1)S(1)}, u32[]{:S(2)}, u32[]{:S(2)}) collective-permute-start(bf16[64,512]{1,0:T(8,128)(2,1)S(1)} %get-tuple-element.78), channel_id=1, source_target_pairs={{0,4},{4,0},{8,12},{12,8},{16,20},{20,16},{24,28},{28,24},{1,5},{5... | collective-permute-start | bytes 196616 | tf_op jit(solution)/shard_map/ppermute | solution.py:471
  91.9 13.4 %collective-permute-start.39 = (bf16[64,512]{1,0:T(8,128)(2,1)S(1)}, bf16[64,512]{1,0:T(8,128)(2,1)S(1)}, u32[]{:S(2)}, u32[]{:S(2)}) collective-permute-start(bf16[64,512]{1,0:T(8,128)(2,1)S(1)} %get-tuple-element.79), channel_id=1, source_target_pairs={{0,2},{1,3},{2,0},{3,1},{4,6},{5,7},{6,4},{7,5},{8,10},{9,11},{10,... | collective-permute-start | bytes 196616 | tf_op jit(solution)/shard_map/ppermute | solution.py:471
  93.4 15.6 %copy-start.4 = (f32[64,512]{1,0:T(8,128)S(1)}, f32[64,512]{1,0:T(8,128)}, u32[]{:S(2)}) copy-start(f32[64,512]{1,0:T(8,128)} %copy-done.3) | copy-start | bytes 393220
  98.1 7.3 %collective-permute-start.40 = (bf16[64,512]{1,0:T(8,128)(2,1)S(1)}, bf16[64,512]{1,0:T(8,128)(2,1)S(1)}, u32[]{:S(2)}, u32[]{:S(2)}) collective-permute-start(bf16[64,512]{1,0:T(8,128)(2,1)S(1)} %get-tuple-element.80), channel_id=1, source_target_pairs={{0,6},{1,7},{2,4},{3,5},{4,2},{5,3},{6,0},{7,1},{8,14},{9,15},{10,... | collective-permute-start | bytes 196616 | tf_op jit(solution)/shard_map/ppermute | solution.py:479
  100.3 5.1 %collective-permute-start.35 = (bf16[64,512]{1,0:T(8,128)(2,1)S(1)}, bf16[64,512]{1,0:T(8,128)(2,1)S(1)}, u32[]{:S(2)}, u32[]{:S(2)}) collective-permute-start(bf16[64,512]{1,0:T(8,128)(2,1)S(1)} %get-tuple-element.75), channel_id=1, source_target_pairs={{0,8},{4,12},{8,0},{12,4},{16,24},{20,28},{24,16},{28,20},{1,9},{5... | collective-permute-start | bytes 196616 | tf_op jit(solution)/shard_map/ppermute | solution.py:471
  100.5 6.6 %collective-permute-start.36 = (bf16[64,512]{1,0:T(8,128)(2,1)S(1)}, bf16[64,512]{1,0:T(8,128)(2,1)S(1)}, u32[]{:S(2)}, u32[]{:S(2)}) collective-permute-start(bf16[64,512]{1,0:T(8,128)(2,1)S(1)} %get-tuple-element.76), channel_id=1, source_target_pairs={{0,16},{4,20},{8,24},{12,28},{16,0},{20,4},{24,8},{28,12},{1,17},{... | collective-permute-start | bytes 196616 | tf_op jit(solution)/shard_map/ppermute | solution.py:471
  102.9 6.1 %collective-permute-start.37 = (bf16[64,512]{1,0:T(8,128)(2,1)S(1)}, bf16[64,512]{1,0:T(8,128)(2,1)S(1)}, u32[]{:S(2)}, u32[]{:S(2)}) collective-permute-start(bf16[64,512]{1,0:T(8,128)(2,1)S(1)} %get-tuple-element.77), channel_id=1, source_target_pairs={{0,24},{4,28},{8,16},{12,20},{16,8},{20,12},{24,0},{28,4},{1,25},{... | collective-permute-start | bytes 196616 | tf_op jit(solution)/shard_map/ppermute | solution.py:471
  (2 other events, 1.3 us)

commit v4 on v3

--- a/solution.py
+++ b/solution.py
@@ -408,23 +408,24 @@
         load.wait()
 
 
-def down_kernel(active_ref, c_ref, add_ref, down_ref, *refs, put):
-    outs, y_s = refs[:-1], refs[-1]
+def down_kernel(active_ref, c_ref, down_ref, out_ref, y_s, *, put):
     for i in range(down_ref.shape[0]):
-        combine_rows(active_ref, down_ref.at[i], c_ref, y_s, functools.partial(put, outs, add_ref, i))
-
-
-def put_plain(out_ref, i, m, value):
-    out_ref[i, m] = value.astype(BF16)
-
-
-def put_added(outs, add_ref, i, m, value):
-    value = (value + add_ref[i, m].astype(F32)).astype(BF16)
-    side, z = 2 * i + m // 4, m % 4
-    if z == 0:
-        outs[side][...] = value
-    else:
-        outs[4 + side][z - 1] = value
+        combine_rows(active_ref, down_ref.at[i], c_ref, y_s, functools.partial(put, out_ref, i))
+
+
+def put_rows(out_ref, i, m, value):
+    out_ref[i, m] = value.astype(out_ref.dtype)
+
+
+def split_kernel(own_ref, add_ref, *outs):
+    for side in range(4):
+        for z in range(4):
+            at = (side // 2, side % 2 * 4 + z)
+            value = (own_ref[at] + add_ref[at].astype(F32)).astype(BF16)
+            if z == 0:
+                outs[side][...] = value
+            else:
+                outs[4 + side][z - 1] = value
 
 
 def total_kernel(own_ref, x_ref, y_ref, d_ref, mark_ref, *outs):
@@ -630,7 +631,7 @@
     later = [shape(down_block, BF16)] * (len(steps) - 1)
     lap = math.gcd(seq, 8)
     active, sums, *later = call(
-        functools.partial(expert_kernel, layout=layout, put=put_plain, steps=steps),
+        functools.partial(expert_kernel, layout=layout, put=put_rows, steps=steps),
         "experts",
         (
             t1,
@@ -666,15 +667,26 @@
     )
 
     if staged:
+        other = core(sums)
+        own = call(
+            functools.partial(down_kernel, put=put_rows),
+            "down",
+            (active, combine, *later),
+            [vmem()] * 3,
+            shape((2, seq, draft, width), F32),
+            vmem(),
+            [y_scratch],
+            busy=2,
+        )
         sums = call(
-            functools.partial(down_kernel, put=put_added),
-            "down",
-            (active, combine, core(sums), *later),
-            [vmem()] * 4,
+            split_kernel,
+            "split",
+            (own, other),
+            [vmem()] * 2,
             [shape((draft, width), BF16)] * 4 + [shape((3, draft, width), BF16)] * 4,
             [vmem()] * 8,
-            [y_scratch],
-            busy=3,
+            limit=4,
+            busy=1,
         )
         first_sums = sums[0]
     else:

time: 110 us -> 109 us (level)
    ppermute x37, waiting for transfers between devices: 26.9 us -> 25.7 us  [hop(): return lambda v: lax.ppermute(v, axis, pairs)]
    pallas_call x9 -> x10, Pallas kernels: 20.6 us -> 20.7 us  [call(): pl.pallas_call(kernel, out_shape=out_shape, in_specs=in_specs, out_specs=...]
  transfers between devices with their start and end apart: 41 -> 41, of which waited for: 17 -> 18; matrix products, arithmetic and copies ran while one was open for 3% -> 3% of each run, Pallas kernels for 7% -> 8%
where the time goes in v4:
time: 109 us
  starting transfers between devices  47.1 us (43%)
  waiting for transfers between devices  29.8 us (27%)
  Pallas kernels  25.2 us (23%)
  other arithmetic  2.94 us (3%)
  local copies, waits for them, and re-layouts  2.71 us (2%)
    ppermute x37, starting transfers between devices, hop(): return lambda v: lax.ppermute(v, axis, pairs)  40.9 us
    ppermute x37, waiting for transfers between devices, hop(): return lambda v: lax.ppermute(v, axis, pairs)  25.7 us
    pallas_call x10, Pallas kernels, call(): pl.pallas_call(kernel, out_shape=out_shape, in_specs=in_specs, out_specs=...  20.7 us
    ppermute x4, starting transfers between devices, diagonal(): lax.ppermute(v, ('seq', 'tensor'), [(i, i ^ flip) for i in range(seq * te...  6.23 us
    pallas_call x1, Pallas kernels, on_device(): pl.pallas_call(functools.partial(cache_kernel, counts=back_counts, accept...  4.46 us
    ppermute x4, waiting for transfers between devices, diagonal(): lax.ppermute(v, ('seq', 'tensor'), [(i, i ^ flip) for i in range(seq * te...  4.02 us
    unnamed x19, local copies, waits for them, and re-layouts  2.71 us
  transfers between devices with their start and end apart: 41, of which 18 were waited for; matrix products, arithmetic and copies ran while one was open for 3% of the time, Pallas kernels for 8%

profile of v4, /device:TPU:0, one launch (start us, length us, event | category | flops | bytes accessed | tf_op | source)
XLA Modules:
  0.0 108.5 jit_solution(11006795198317163422)
XLA Ops:
  0.6 3.0 %collective-permute-start.3 = (bf16[1,64,512]{2,1,0:T(8,128)(2,1)}, bf16[1,64,512]{2,1,0:T(8,128)(2,1)S(1)}, u32[]{:S(2)}, u32[]{:S(2)}) collective-permute-start(bf16[1,64,512]{2,1,0:T(8,128)(2,1)} %bitcast.9), channel_id=1, source_target_pairs={{0,4},{4,0},{8,12},{12,8},{16,20},{20,16},{24,28},{28,24},{1,5},{5... | collective-permute-start | bytes 196616 | tf_op jit(solution)/shard_map/ppermute | solution.py:472
  3.6 3.6 %collective-permute-start.2 = (bf16[1,64,512]{2,1,0:T(8,128)(2,1)}, bf16[1,64,512]{2,1,0:T(8,128)(2,1)S(1)}, u32[]{:S(2)}, u32[]{:S(2)}) collective-permute-start(bf16[1,64,512]{2,1,0:T(8,128)(2,1)} %bitcast.10), channel_id=1, source_target_pairs={{0,24},{4,28},{8,16},{12,20},{16,8},{20,12},{24,0},{28,4},{1,25},{... | collective-permute-start | bytes 196616 | tf_op jit(solution)/shard_map/ppermute | solution.py:472
  7.3 0.8 collective-permute-start
  8.0 0.8 select_reduce_fusion
  8.8 1.9 %collective-permute-done.2.refs_3_ = bf16[1,64,512]{2,1,0:T(8,128)(2,1)S(1)} collective-permute-done((bf16[1,64,512]{2,1,0:T(8,128)(2,1)}, bf16[1,64,512]{2,1,0:T(8,128)(2,1)S(1)}, u32[]{:S(2)}, u32[]{:S(2)}) %collective-permute-start.2) | collective-permute-done | bytes 65568 | tf_op jit(solution)/shard_map/ppermute | solution.py:472
  10.8 2.0 %collective-permute-done.1.refs_2_ = bf16[1,64,512]{2,1,0:T(8,128)(2,1)S(1)} collective-permute-done((bf16[1,64,512]{2,1,0:T(8,128)(2,1)}, bf16[1,64,512]{2,1,0:T(8,128)(2,1)S(1)}, u32[]{:S(2)}, u32[]{:S(2)}) %collective-permute-start.1) | collective-permute-done | bytes 65568 | tf_op jit(solution)/shard_map/ppermute | solution.py:472
  13.4 1.5 %collective-permute-start.4 = (bf16[1,64,512]{2,1,0:T(8,128)(2,1)S(1)}, bf16[1,64,512]{2,1,0:T(8,128)(2,1)S(1)}, u32[]{:S(2)}, u32[]{:S(2)}) collective-permute-start(bf16[1,64,512]{2,1,0:T(8,128)(2,1)S(1)} %collective-permute-done.refs_1_), channel_id=1, source_target_pairs={{0,4},{4,0},{8,12},{12,8},{16,20},{20,16},{24,28},{28,24},{1,5},{5... | collective-permute-start | bytes 196616 | tf_op jit(solution)/shard_map/ppermute | solution.py:472
  17.6 2.1 %near.1 = (f32[64,512]{1,0:T(8,128)S(1)}, f32[64,512]{1,0:T(8,128)S(1)}, f32[64,256]{1,0:T(8,128)S(1)}, bf16[12,128,512]{2,1,0:T(8,128)(2,1)S(1)}, bf16[12,128,512]{2,1,0:T(8,128)(2,1)S(1)}) custom-call(bf16[64,512]{1,0:T(8,128)(2,1)} %q_hbm.1, bf16[64,512]{1,0:T(8,128)(2,1)} %k_hbm.1, bf16[64,512]{1,0:T(8,128)(2,1)} %v_hbm.1, s32[1,64,64]{2,1,0:T(8,128)} %mask_hbm.1, ...), custom_call_target="tpu_custom_call" | custom-call | bytes 6000000 | tf_op jit(solution)/shard_map/near/pallas_call | solution.py:48
  19.8 3.9 %far.1 = (bf16[1,64,768]{2,1,0:T(8,128)(2,1)S(1)}, bf16[1,64,768]{2,1,0:T(8,128)(2,1)S(1)}, bf16[1,64,768]{2,1,0:T(8,128)(2,1)S(1)}, bf16[1,64,768]{2,1,0:T(8,12...) custom-call(s32[12]{0:T(128)S(1)} %get-tuple-element.93.pos_ref, ...), custom_call_target="tpu_custom_call" | custom-call | bytes 15000000 | tf_op jit(solution)/shard_map/far/pallas_call | solution.py:48
  23.7 3.1 %collective-permute-start.8 = (bf16[1,64,768]{2,1,0:T(8,128)(2,1)S(1)}, bf16[1,64,768]{2,1,0:T(8,128)(2,1)S(1)}, u32[]{:S(2)}, u32[]{:S(2)}) collective-permute-start(bf16[1,64,768]{2,1,0:T(8,128)(2,1)S(1)} %get-tuple-element.51), channel_id=1, source_target_pairs={{0,16},{4,20},{8,24},{12,28},{16,0},{20,4},{24,8},{28,12},{1,17},{... | collective-permute-start | bytes 294920 | tf_op jit(solution)/shard_map/ppermute | solution.py:472
  26.8 1.3 %collective-permute-start.9 = (bf16[1,64,768]{2,1,0:T(8,128)(2,1)}, bf16[1,64,768]{2,1,0:T(8,128)(2,1)S(1)}, u32[]{:S(2)}, u32[]{:S(2)}) collective-permute-start(bf16[1,64,768]{2,1,0:T(8,128)(2,1)} %get-tuple-element.52), channel_id=1, source_target_pairs={{0,24},{4,28},{8,16},{12,20},{16,8},{20,12},{24,0},{28,4},{1,25},{... | collective-permute-start | bytes 294920 | tf_op jit(solution)/shard_map/ppermute | solution.py:472
  28.8 4.2 %collective-permute-start.12 = (bf16[1,64,768]{2,1,0:T(8,128)(2,1)}, bf16[1,64,768]{2,1,0:T(8,128)(2,1)S(1)}, u32[]{:S(2)}, u32[]{:S(2)}) collective-permute-start(bf16[1,64,768]{2,1,0:T(8,128)(2,1)} %get-tuple-element.55), channel_id=1, source_target_pairs={{0,20},{4,16},{8,28},{12,24},{16,4},{20,0},{24,12},{28,8},{1,21},{... | collective-permute-start | bytes 294920 | tf_op jit(solution)/shard_map/ppermute | solution.py:472
  33.1 2.2 %collective-permute-done.8.refs_2_ = bf16[1,64,768]{2,1,0:T(8,128)(2,1)S(1)} collective-permute-done((bf16[1,64,768]{2,1,0:T(8,128)(2,1)S(1)}, bf16[1,64,768]{2,1,0:T(8,128)(2,1)S(1)}, u32[]{:S(2)}, u32[]{:S(2)}) %collective-permute-start.8) | collective-permute-done | bytes 98336 | tf_op jit(solution)/shard_map/ppermute | solution.py:472
  35.3 2.1 %collective-permute-start.13 = (bf16[1,64,768]{2,1,0:T(8,128)(2,1)S(1)}, bf16[1,64,768]{2,1,0:T(8,128)(2,1)S(1)}, u32[]{:S(2)}, u32[]{:S(2)}) collective-permute-start(bf16[1,64,768]{2,1,0:T(8,128)(2,1)S(1)} %get-tuple-element.56), channel_id=1, source_target_pairs={{0,28},{4,24},{8,20},{12,16},{16,12},{20,8},{24,4},{28,0},{1,29},{... | collective-permute-start | bytes 294920 | tf_op jit(solution)/shard_map/ppermute | solution.py:472
  37.4 3.4 %collective-permute-done.12.refs_6_ = bf16[1,64,768]{2,1,0:T(8,128)(2,1)S(1)} collective-permute-done((bf16[1,64,768]{2,1,0:T(8,128)(2,1)}, bf16[1,64,768]{2,1,0:T(8,128)(2,1)S(1)}, u32[]{:S(2)}, u32[]{:S(2)}) %collective-permute-start.12) | collective-permute-done | bytes 98336 | tf_op jit(solution)/shard_map/ppermute | solution.py:472
  40.8 1.8 %collective-permute-done.13.refs_7_ = bf16[1,64,768]{2,1,0:T(8,128)(2,1)S(1)} collective-permute-done((bf16[1,64,768]{2,1,0:T(8,128)(2,1)S(1)}, bf16[1,64,768]{2,1,0:T(8,128)(2,1)S(1)}, u32[]{:S(2)}, u32[]{:S(2)}) %collective-permute-start.13) | collective-permute-done | bytes 98336 | tf_op jit(solution)/shard_map/ppermute | solution.py:472
  42.7 1.9 %merge.1 = (f32[64,4]{1,0:T(8,128)S(1)}, f32[64,512]{1,0:T(8,128)S(1)}, bf16[64,512]{1,0:T(8,128)(2,1)S(1)}, bf16[64,512]{1,0:T(8,128)(2,1)S(1)}, bf16[64,512]{1,0:T(8,128)(2,1)S(1)}) custom-call(s32[1]{0:T(128)} %bitcast.t_ref, f32[64,512]{1,0:T(8,128)S(1)} %get-tuple-element.44.near_ref, f32[64,512]{1,0:T(8,128)S(1)} %get-tuple-element.45.lse_ref, ...), custom_call_target="tpu_custom_call" | custom-call | bytes 12000000 | tf_op jit(solution)/shard_map/merge/pallas_call | solution.py:48
  44.7 1.6 %collective-permute-start.15 = (bf16[64,512]{1,0:T(8,128)(2,1)S(1)}, bf16[64,512]{1,0:T(8,128)(2,1)S(1)}, u32[]{:S(2)}, u32[]{:S(2)}) collective-permute-start(bf16[64,512]{1,0:T(8,128)(2,1)S(1)} %get-tuple-element.59), channel_id=1, source_target_pairs={{0,2},{1,3},{2,0},{3,1},{4,6},{5,7},{6,4},{7,5},{8,10},{9,11},{10,... | collective-permute-start | bytes 196616 | tf_op jit(solution)/shard_map/ppermute | solution.py:472
  46.5 0.9 slots.1
  47.4 1.8 %collective-permute-done.15.b_ref = bf16[64,512]{1,0:T(8,128)(2,1)S(1)} collective-permute-done((bf16[64,512]{1,0:T(8,128)(2,1)S(1)}, bf16[64,512]{1,0:T(8,128)(2,1)S(1)}, u32[]{:S(2)}, u32[]{:S(2)}) %collective-permute-start.15) | collective-permute-done | bytes 65568 | tf_op jit(solution)/shard_map/ppermute | solution.py:472
  49.2 1.1 %collective-permute-done.16.c_ref = bf16[64,512]{1,0:T(8,128)(2,1)S(1)} collective-permute-done((bf16[64,512]{1,0:T(8,128)(2,1)S(1)}, bf16[64,512]{1,0:T(8,128)(2,1)S(1)}, u32[]{:S(2)}, u32[]{:S(2)}) %collective-permute-start.16) | collective-permute-done | bytes 65568 | tf_op jit(solution)/shard_map/ppermute | solution.py:472
  50.3 1.5 %collective-permute-start.22 = (bf16[1,64,512]{2,1,0:T(8,128)(2,1)S(1)}, bf16[1,64,512]{2,1,0:T(8,128)(2,1)S(1)}, u32[]{:S(2)}, u32[]{:S(2)}) collective-permute-start(bf16[1,64,512]{2,1,0:T(8,128)(2,1)S(1)} %get-tuple-element.65.refs_0_), channel_id=1, source_target_pairs={{0,24},{4,28},{8,16},{12,20},{16,8},{20,12},{24,0},{28,4},{1,25},{... | collective-permute-start | bytes 196616 | tf_op jit(solution)/shard_map/ppermute | solution.py:472
  51.8 0.9 collective-permute-start.21
  52.7 2.1 %collective-permute-start.20 = (bf16[1,64,512]{2,1,0:T(8,128)(2,1)S(1)}, bf16[1,64,512]{2,1,0:T(8,128)(2,1)S(1)}, u32[]{:S(2)}, u32[]{:S(2)}) collective-permute-start(bf16[1,64,512]{2,1,0:T(8,128)(2,1)S(1)} %get-tuple-element.65.refs_0_), channel_id=1, source_target_pairs={{0,8},{4,12},{8,0},{12,4},{16,24},{20,28},{24,16},{28,20},{1,9},{5... | collective-permute-start | bytes 196616 | tf_op jit(solution)/shard_map/ppermute | solution.py:472
  54.8 1.5 %collective-permute-start.19 = (bf16[1,64,512]{2,1,0:T(8,128)(2,1)S(1)}, bf16[1,64,512]{2,1,0:T(8,128)(2,1)S(1)}, u32[]{:S(2)}, u32[]{:S(2)}) collective-permute-start(bf16[1,64,512]{2,1,0:T(8,128)(2,1)S(1)} %get-tuple-element.65.refs_0_), channel_id=1, source_target_pairs={{0,6},{1,7},{2,4},{3,5},{4,2},{5,3},{6,0},{7,1},{8,14},{9,15},{10,... | collective-permute-start | bytes 196616 | tf_op jit(solution)/shard_map/ppermute | solution.py:480
  57.2 1.1 %collective-permute-start.17 = (bf16[1,64,512]{2,1,0:T(8,128)(2,1)S(1)}, bf16[1,64,512]{2,1,0:T(8,128)(2,1)S(1)}, u32[]{:S(2)}, u32[]{:S(2)}) collective-permute-start(bf16[1,64,512]{2,1,0:T(8,128)(2,1)S(1)} %get-tuple-element.65.refs_0_), channel_id=1, source_target_pairs={{0,4},{4,0},{8,12},{12,8},{16,20},{20,16},{24,28},{28,24},{1,5},{5... | collective-permute-start | bytes 196616 | tf_op jit(solution)/shard_map/ppermute | solution.py:472
  58.3 0.9 collective-permute-done.21.refs_1_
  59.2 2.3 %collective-permute-start.25 = (bf16[3,64,512]{2,1,0:T(8,128)(2,1)S(1)}, bf16[3,64,512]{2,1,0:T(8,128)(2,1)S(1)}, u32[]{:S(2)}, u32[]{:S(2)}) collective-permute-start(bf16[3,64,512]{2,1,0:T(8,128)(2,1)S(1)} %stack.18.refs_4_), channel_id=1, source_target_pairs={{0,6},{1,7},{2,4},{3,5},{4,2},{5,3},{6,0},{7,1},{8,14},{9,15},{10,... | collective-permute-start | bytes 589832 | tf_op jit(solution)/shard_map/ppermute | solution.py:480
  62.8 0.7 pad_maximum_fusion
  64.0 4.0 %collective-permute-done.25.refs_7_ = bf16[3,64,512]{2,1,0:T(8,128)(2,1)S(1)} collective-permute-done((bf16[3,64,512]{2,1,0:T(8,128)(2,1)S(1)}, bf16[3,64,512]{2,1,0:T(8,128)(2,1)S(1)}, u32[]{:S(2)}, u32[]{:S(2)}) %collective-permute-start.25) | collective-permute-done | bytes 196640 | tf_op jit(solution)/shard_map/ppermute | solution.py:480
  68.0 3.2 %collective-permute-done.24.refs_6_ = bf16[3,64,512]{2,1,0:T(8,128)(2,1)S(1)} collective-permute-done((bf16[3,64,512]{2,1,0:T(8,128)(2,1)S(1)}, bf16[3,64,512]{2,1,0:T(8,128)(2,1)S(1)}, u32[]{:S(2)}, u32[]{:S(2)}) %collective-permute-start.24) | collective-permute-done | bytes 196640 | tf_op jit(solution)/shard_map/ppermute | solution.py:472
  71.8 1.0 collective-permute-done.29.refs_11_
  73.0 10.4 %experts.1 = (bf16[8,128,256]{2,1,0:T(8,128)(2,1)S(1)}, bf16[2,8,64,512]{3,2,1,0:T(8,128)(2,1)S(1)}, bf16[2,8,256,512]{3,2,1,0:T(8,128)(2,1)S(1)}) custom-call(s32[1]{0:T(128)} %bitcast.t_ref, s32[4]{0:T(128)S(1)} %pad_add_fusion.cols_ref, f32[1,2048]{1,0:T(1,128)S(1)} %bitcast.14, bf16[8,128,64]{2,1,0:T(8,128)(2,1)S(1)} %get-tuple-element.61.after_ref.g_ref, ...), custom_call_target="tpu_custom_call" | custom-call | bytes 27000000 | tf_op jit(solution)/shard_map/experts/pallas_call | solution.py:48
  83.8 1.3 %down.1.own_ref = f32[2,8,64,512]{3,2,1,0:T(8,128)S(1)} custom-call(bf16[8,128,256]{2,1,0:T(8,128)(2,1)S(1)} %get-tuple-element.66.active_ref, bf16[8,64,128]{2,1,0:T(8,128)(2,1)S(1)} %get-tuple-element.64.c_ref, bf16[2,8,256,512]{3,2,1,0:T(8,128)(2,1)S(1)} %get-tuple-element.67.down_ref), custom_call_target="tpu_custom_call" | custom-call | bytes 6000000 | tf_op jit(solution)/shard_map/down/pallas_call | solution.py:48
  85.1 1.2 %collective-permute-done.31.add_ref = bf16[2,8,64,512]{3,2,1,0:T(8,128)(2,1)S(1)} collective-permute-done((bf16[2,8,64,512]{3,2,1,0:T(8,128)(2,1)S(1)}, bf16[2,8,64,512]{3,2,1,0:T(8,128)(2,1)S(1)}, u32[]{:S(2)}, u32[]{:S(2)}) %collective-permute-start.31) | collective-permute-done | bytes 1048608 | tf_op jit(solution)/shard_map/ppermute | solution.py:472
  86.4 0.9 collective-permute-start.32
  87.3 1.4 %collective-permute-start.33 = (bf16[3,64,512]{2,1,0:T(8,128)(2,1)S(1)}, bf16[3,64,512]{2,1,0:T(8,128)(2,1)S(1)}, u32[]{:S(2)}, u32[]{:S(2)}) collective-permute-start(bf16[3,64,512]{2,1,0:T(8,128)(2,1)S(1)} %get-tuple-element.72), channel_id=1, source_target_pairs={{0,2},{1,3},{2,0},{3,1},{4,6},{5,7},{6,4},{7,5},{8,10},{9,11},{10,... | collective-permute-start | bytes 589832 | tf_op jit(solution)/shard_map/ppermute | solution.py:472
  88.8 1.2 %collective-permute-start.34 = (bf16[3,64,512]{2,1,0:T(8,128)(2,1)S(1)}, bf16[3,64,512]{2,1,0:T(8,128)(2,1)S(1)}, u32[]{:S(2)}, u32[]{:S(2)}) collective-permute-start(bf16[3,64,512]{2,1,0:T(8,128)(2,1)S(1)} %get-tuple-element.73), channel_id=1, source_target_pairs={{0,6},{1,7},{2,4},{3,5},{4,2},{5,3},{6,0},{7,1},{8,14},{9,15},{10,... | collective-permute-start | bytes 589832 | tf_op jit(solution)/shard_map/ppermute | solution.py:480
  89.9 0.9 collective-permute-start.38
  90.8 1.4 %collective-permute-start.39 = (bf16[64,512]{1,0:T(8,128)(2,1)S(1)}, bf16[64,512]{1,0:T(8,128)(2,1)S(1)}, u32[]{:S(2)}, u32[]{:S(2)}) collective-permute-start(bf16[64,512]{1,0:T(8,128)(2,1)S(1)} %get-tuple-element.79), channel_id=1, source_target_pairs={{0,2},{1,3},{2,0},{3,1},{4,6},{5,7},{6,4},{7,5},{8,10},{9,11},{10,... | collective-permute-start | bytes 196616 | tf_op jit(solution)/shard_map/ppermute | solution.py:472
  92.3 4.5 %cache.1 = (bf16[12,128,512]{2,1,0:T(8,128)(2,1)}, bf16[12,128,512]{2,1,0:T(8,128)(2,1)}, f32[8,128]{1,0:T(8,128)S(1)}) custom-call(s32[12]{0:T(128)S(1)} %get-tuple-element.93.pos_ref, s32[12]{0:T(128)S(1)} %get-tuple-element.92.live_ref, bf16[12,128,512]{2,1,0:T(8,128)(2,1)} %key_ref.1, bf16[12,128,512]{2,1,0:T(8,128)(2,1)} %value_ref.1, ...), custom_call_target="tpu_custom_call" | custom-call | bytes 12000000 | tf_op jit(solution)/shard_map/cache/pallas_call | solution.py:696
  96.7 1.2 %collective-permute-start.40 = (bf16[64,512]{1,0:T(8,128)(2,1)S(1)}, bf16[64,512]{1,0:T(8,128)(2,1)S(1)}, u32[]{:S(2)}, u32[]{:S(2)}) collective-permute-start(bf16[64,512]{1,0:T(8,128)(2,1)S(1)} %get-tuple-element.80), channel_id=1, source_target_pairs={{0,6},{1,7},{2,4},{3,5},{4,2},{5,3},{6,0},{7,1},{8,14},{9,15},{10,... | collective-permute-start | bytes 196616 | tf_op jit(solution)/shard_map/ppermute | solution.py:480
  98.0 1.0 collective-permute-done.33.y_ref
  99.3 2.4 %collective-permute-start.36 = (bf16[64,512]{1,0:T(8,128)(2,1)S(1)}, bf16[64,512]{1,0:T(8,128)(2,1)S(1)}, u32[]{:S(2)}, u32[]{:S(2)}) collective-permute-start(bf16[64,512]{1,0:T(8,128)(2,1)S(1)} %get-tuple-element.76), channel_id=1, source_target_pairs={{0,16},{4,20},{8,24},{12,28},{16,0},{20,4},{24,8},{28,12},{1,17},{... | collective-permute-start | bytes 196616 | tf_op jit(solution)/shard_map/ppermute | solution.py:472
  101.8 1.8 %collective-permute-start.37 = (bf16[64,512]{1,0:T(8,128)(2,1)S(1)}, bf16[64,512]{1,0:T(8,128)(2,1)S(1)}, u32[]{:S(2)}, u32[]{:S(2)}) collective-permute-start(bf16[64,512]{1,0:T(8,128)(2,1)S(1)} %get-tuple-element.77), channel_id=1, source_target_pairs={{0,24},{4,28},{8,16},{12,20},{16,8},{20,12},{24,0},{28,4},{1,25},{... | collective-permute-start | bytes 196616 | tf_op jit(solution)/shard_map/ppermute | solution.py:472
  104.3 1.7 %collective-permute-done.36 = bf16[64,512]{1,0:T(8,128)(2,1)S(1)} collective-permute-done((bf16[64,512]{1,0:T(8,128)(2,1)S(1)}, bf16[64,512]{1,0:T(8,128)(2,1)S(1)}, u32[]{:S(2)}, u32[]{:S(2)}) %collective-permute-start.36) | collective-permute-done | bytes 65568 | tf_op jit(solution)/shard_map/ppermute | solution.py:472
  106.0 1.9 %collective-permute-done.37 = bf16[64,512]{1,0:T(8,128)(2,1)S(1)} collective-permute-done((bf16[64,512]{1,0:T(8,128)(2,1)S(1)}, bf16[64,512]{1,0:T(8,128)(2,1)S(1)}, u32[]{:S(2)}, u32[]{:S(2)}) %collective-permute-start.37) | collective-permute-done | bytes 65568 | tf_op jit(solution)/shard_map/ppermute | solution.py:472
  107.8 0.7 add_convert_fusion
  (69 shorter events, 9.6 us)
Async XLA Ops:
  0.6 19.1 %copy-start.1 = (bf16[64,512]{1,0:T(8,128)(2,1)S(1)}, bf16[64,512]{1,0:T(8,128)(2,1)}, u32[]{:S(2)}) copy-start(bf16[64,512]{1,0:T(8,128)(2,1)} %q_hbm.1) | copy-start | bytes 196612
  0.6 19.1 %collective-permute-start.3 = (bf16[1,64,512]{2,1,0:T(8,128)(2,1)}, bf16[1,64,512]{2,1,0:T(8,128)(2,1)S(1)}, u32[]{:S(2)}, u32[]{:S(2)}) collective-permute-start(bf16[1,64,512]{2,1,0:T(8,128)(2,1)} %bitcast.9), channel_id=1, source_target_pairs={{0,4},{4,0},{8,12},{12,8},{16,20},{20,16},{24,28},{28,24},{1,5},{5... | collective-permute-start | bytes 196616 | tf_op jit(solution)/shard_map/ppermute | solution.py:472
  3.6 7.1 %collective-permute-start.2 = (bf16[1,64,512]{2,1,0:T(8,128)(2,1)}, bf16[1,64,512]{2,1,0:T(8,128)(2,1)S(1)}, u32[]{:S(2)}, u32[]{:S(2)}) collective-permute-start(bf16[1,64,512]{2,1,0:T(8,128)(2,1)} %bitcast.10), channel_id=1, source_target_pairs={{0,24},{4,28},{8,16},{12,20},{16,8},{20,12},{24,0},{28,4},{1,25},{... | collective-permute-start | bytes 196616 | tf_op jit(solution)/shard_map/ppermute | solution.py:472
  7.2 5.6 %collective-permute-start.1 = (bf16[1,64,512]{2,1,0:T(8,128)(2,1)}, bf16[1,64,512]{2,1,0:T(8,128)(2,1)S(1)}, u32[]{:S(2)}, u32[]{:S(2)}) collective-permute-start(bf16[1,64,512]{2,1,0:T(8,128)(2,1)} %bitcast.11), channel_id=1, source_target_pairs={{0,16},{4,20},{8,24},{12,28},{16,0},{20,4},{24,8},{28,12},{1,17},{... | collective-permute-start | bytes 196616 | tf_op jit(solution)/shard_map/ppermute | solution.py:472
  7.3 6.2 %collective-permute-start = (bf16[1,64,512]{2,1,0:T(8,128)(2,1)}, bf16[1,64,512]{2,1,0:T(8,128)(2,1)S(1)}, u32[]{:S(2)}, u32[]{:S(2)}) collective-permute-start(bf16[1,64,512]{2,1,0:T(8,128)(2,1)} %bitcast.12), channel_id=1, source_target_pairs={{0,8},{4,12},{8,0},{12,4},{16,24},{20,28},{24,16},{28,20},{1,9},{5... | collective-permute-start | bytes 196616 | tf_op jit(solution)/shard_map/ppermute | solution.py:472
  10.7 9.0 %collective-permute-start.6 = (bf16[1,64,512]{2,1,0:T(8,128)(2,1)S(1)}, bf16[1,64,512]{2,1,0:T(8,128)(2,1)S(1)}, u32[]{:S(2)}, u32[]{:S(2)}) collective-permute-start(bf16[1,64,512]{2,1,0:T(8,128)(2,1)S(1)} %collective-permute-done.2.refs_3_), channel_id=1, source_target_pairs={{0,4},{4,0},{8,12},{12,8},{16,20},{20,16},{24,28},{28,24},{1,5},{5... | collective-permute-start | bytes 196616 | tf_op jit(solution)/shard_map/ppermute | solution.py:472
  12.9 6.9 %collective-permute-start.5 = (bf16[1,64,512]{2,1,0:T(8,128)(2,1)S(1)}, bf16[1,64,512]{2,1,0:T(8,128)(2,1)S(1)}, u32[]{:S(2)}, u32[]{:S(2)}) collective-permute-start(bf16[1,64,512]{2,1,0:T(8,128)(2,1)S(1)} %collective-permute-done.1.refs_2_), channel_id=1, source_target_pairs={{0,4},{4,0},{8,12},{12,8},{16,20},{20,16},{24,28},{28,24},{1,5},{5... | collective-permute-start | bytes 196616 | tf_op jit(solution)/shard_map/ppermute | solution.py:472
  13.4 6.3 %collective-permute-start.4 = (bf16[1,64,512]{2,1,0:T(8,128)(2,1)S(1)}, bf16[1,64,512]{2,1,0:T(8,128)(2,1)S(1)}, u32[]{:S(2)}, u32[]{:S(2)}) collective-permute-start(bf16[1,64,512]{2,1,0:T(8,128)(2,1)S(1)} %collective-permute-done.refs_1_), channel_id=1, source_target_pairs={{0,4},{4,0},{8,12},{12,8},{16,20},{20,16},{24,28},{28,24},{1,5},{5... | collective-permute-start | bytes 196616 | tf_op jit(solution)/shard_map/ppermute | solution.py:472
  15.6 0.7 copy-start.6
  19.7 23.0 %copy-start = (bf16[512,2048]{1,0:T(8,128)(2,1)S(1)}, bf16[512,2048]{1,0:T(8,128)(2,1)}, u32[]{:S(2)}) copy-start(bf16[512,2048]{1,0:T(8,128)(2,1)} %w_ref.1) | copy-start | bytes 6291460
  19.7 23.0 %copy-start.2 = (bf16[64,2048]{1,0:T(8,128)(2,1)S(1)}, bf16[64,2048]{1,0:T(8,128)(2,1)}, u32[]{:S(2)}) copy-start(bf16[64,2048]{1,0:T(8,128)(2,1)} %hidden_ref.1) | copy-start | bytes 786436
  23.7 5.2 %collective-permute-start.7 = (bf16[1,64,768]{2,1,0:T(8,128)(2,1)S(1)}, bf16[1,64,768]{2,1,0:T(8,128)(2,1)S(1)}, u32[]{:S(2)}, u32[]{:S(2)}) collective-permute-start(bf16[1,64,768]{2,1,0:T(8,128)(2,1)S(1)} %get-tuple-element.50), channel_id=1, source_target_pairs={{0,8},{4,12},{8,0},{12,4},{16,24},{20,28},{24,16},{28,20},{1,9},{5... | collective-permute-start | bytes 294920 | tf_op jit(solution)/shard_map/ppermute | solution.py:472
  23.7 11.6 %collective-permute-start.8 = (bf16[1,64,768]{2,1,0:T(8,128)(2,1)S(1)}, bf16[1,64,768]{2,1,0:T(8,128)(2,1)S(1)}, u32[]{:S(2)}, u32[]{:S(2)}) collective-permute-start(bf16[1,64,768]{2,1,0:T(8,128)(2,1)S(1)} %get-tuple-element.51), channel_id=1, source_target_pairs={{0,16},{4,20},{8,24},{12,28},{16,0},{20,4},{24,8},{28,12},{1,17},{... | collective-permute-start | bytes 294920 | tf_op jit(solution)/shard_map/ppermute | solution.py:472
  26.8 10.6 %collective-permute-start.9 = (bf16[1,64,768]{2,1,0:T(8,128)(2,1)}, bf16[1,64,768]{2,1,0:T(8,128)(2,1)S(1)}, u32[]{:S(2)}, u32[]{:S(2)}) collective-permute-start(bf16[1,64,768]{2,1,0:T(8,128)(2,1)} %get-tuple-element.52), channel_id=1, source_target_pairs={{0,24},{4,28},{8,16},{12,20},{16,8},{20,12},{24,0},{28,4},{1,25},{... | collective-permute-start | bytes 294920 | tf_op jit(solution)/shard_map/ppermute | solution.py:472
  28.1 9.4 %collective-permute-start.10 = (bf16[1,64,768]{2,1,0:T(8,128)(2,1)}, bf16[1,64,768]{2,1,0:T(8,128)(2,1)S(1)}, u32[]{:S(2)}, u32[]{:S(2)}) collective-permute-start(bf16[1,64,768]{2,1,0:T(8,128)(2,1)} %get-tuple-element.53), channel_id=1, source_target_pairs={{0,4},{4,0},{8,12},{12,8},{16,20},{20,16},{24,28},{28,24},{1,5},{5... | collective-permute-start | bytes 294920 | tf_op jit(solution)/shard_map/ppermute | solution.py:472
  28.6 8.8 %collective-permute-start.11 = (bf16[1,64,768]{2,1,0:T(8,128)(2,1)}, bf16[1,64,768]{2,1,0:T(8,128)(2,1)S(1)}, u32[]{:S(2)}, u32[]{:S(2)}) collective-permute-start(bf16[1,64,768]{2,1,0:T(8,128)(2,1)} %get-tuple-element.54), channel_id=1, source_target_pairs={{0,12},{4,8},{8,4},{12,0},{16,28},{20,24},{24,20},{28,16},{1,13},{... | collective-permute-start | bytes 294920 | tf_op jit(solution)/shard_map/ppermute | solution.py:472
  28.8 12.0 %collective-permute-start.12 = (bf16[1,64,768]{2,1,0:T(8,128)(2,1)}, bf16[1,64,768]{2,1,0:T(8,128)(2,1)S(1)}, u32[]{:S(2)}, u32[]{:S(2)}) collective-permute-start(bf16[1,64,768]{2,1,0:T(8,128)(2,1)} %get-tuple-element.55), channel_id=1, source_target_pairs={{0,20},{4,16},{8,28},{12,24},{16,4},{20,0},{24,12},{28,8},{1,21},{... | collective-permute-start | bytes 294920 | tf_op jit(solution)/shard_map/ppermute | solution.py:472
  35.3 7.4 %collective-permute-start.13 = (bf16[1,64,768]{2,1,0:T(8,128)(2,1)S(1)}, bf16[1,64,768]{2,1,0:T(8,128)(2,1)S(1)}, u32[]{:S(2)}, u32[]{:S(2)}) collective-permute-start(bf16[1,64,768]{2,1,0:T(8,128)(2,1)S(1)} %get-tuple-element.56), channel_id=1, source_target_pairs={{0,28},{4,24},{8,20},{12,16},{16,12},{20,8},{24,4},{28,0},{1,29},{... | collective-permute-start | bytes 294920 | tf_op jit(solution)/shard_map/ppermute | solution.py:472
  42.7 30.3 %copy-start.5 = (f32[2048]{0:T(1024)S(1)}, f32[2048]{0:T(1024)}, u32[]{:S(2)}) copy-start(f32[2048]{0:T(1024)} %param.30) | copy-start | bytes 24580
  44.6 2.8 %collective-permute-start.14 = (bf16[64,512]{1,0:T(8,128)(2,1)S(1)}, bf16[64,512]{1,0:T(8,128)(2,1)S(1)}, u32[]{:S(2)}, u32[]{:S(2)}) collective-permute-start(bf16[64,512]{1,0:T(8,128)(2,1)S(1)} %get-tuple-element.58), channel_id=1, source_target_pairs={{0,1},{1,0},{2,3},{3,2},{4,5},{5,4},{6,7},{7,6},{8,9},{9,8},{10,11... | collective-permute-start | bytes 196616 | tf_op jit(solution)/shard_map/ppermute | solution.py:472
  44.7 4.5 %collective-permute-start.15 = (bf16[64,512]{1,0:T(8,128)(2,1)S(1)}, bf16[64,512]{1,0:T(8,128)(2,1)S(1)}, u32[]{:S(2)}, u32[]{:S(2)}) collective-permute-start(bf16[64,512]{1,0:T(8,128)(2,1)S(1)} %get-tuple-element.59), channel_id=1, source_target_pairs={{0,2},{1,3},{2,0},{3,1},{4,6},{5,7},{6,4},{7,5},{8,10},{9,11},{10,... | collective-permute-start | bytes 196616 | tf_op jit(solution)/shard_map/ppermute | solution.py:472
  46.2 4.0 %collective-permute-start.16 = (bf16[64,512]{1,0:T(8,128)(2,1)S(1)}, bf16[64,512]{1,0:T(8,128)(2,1)S(1)}, u32[]{:S(2)}, u32[]{:S(2)}) collective-permute-start(bf16[64,512]{1,0:T(8,128)(2,1)S(1)} %get-tuple-element.60), channel_id=1, source_target_pairs={{0,3},{1,2},{2,1},{3,0},{4,7},{5,6},{6,5},{7,4},{8,11},{9,10},{10,... | collective-permute-start | bytes 196616 | tf_op jit(solution)/shard_map/ppermute | solution.py:472
  50.3 20.9 %copy-start.3 = (f32[64,512]{1,0:T(8,128)}, f32[64,512]{1,0:T(8,128)S(1)}, u32[]{:S(2)}) copy-start(f32[64,512]{1,0:T(8,128)S(1)} %get-tuple-element.62) | copy-start | bytes 393220
  50.3 6.8 %collective-permute-start.22 = (bf16[1,64,512]{2,1,0:T(8,128)(2,1)S(1)}, bf16[1,64,512]{2,1,0:T(8,128)(2,1)S(1)}, u32[]{:S(2)}, u32[]{:S(2)}) collective-permute-start(bf16[1,64,512]{2,1,0:T(8,128)(2,1)S(1)} %get-tuple-element.65.refs_0_), channel_id=1, source_target_pairs={{0,24},{4,28},{8,16},{12,20},{16,8},{20,12},{24,0},{28,4},{1,25},{... | collective-permute-start | bytes 196616 | tf_op jit(solution)/shard_map/ppermute | solution.py:472
  51.8 7.4 %collective-permute-start.21 = (bf16[1,64,512]{2,1,0:T(8,128)(2,1)S(1)}, bf16[1,64,512]{2,1,0:T(8,128)(2,1)S(1)}, u32[]{:S(2)}, u32[]{:S(2)}) collective-permute-start(bf16[1,64,512]{2,1,0:T(8,128)(2,1)S(1)} %get-tuple-element.65.refs_0_), channel_id=1, source_target_pairs={{0,16},{4,20},{8,24},{12,28},{16,0},{20,4},{24,8},{28,12},{1,17},{... | collective-permute-start | bytes 196616 | tf_op jit(solution)/shard_map/ppermute | solution.py:472
  52.7 6.5 %collective-permute-start.20 = (bf16[1,64,512]{2,1,0:T(8,128)(2,1)S(1)}, bf16[1,64,512]{2,1,0:T(8,128)(2,1)S(1)}, u32[]{:S(2)}, u32[]{:S(2)}) collective-permute-start(bf16[1,64,512]{2,1,0:T(8,128)(2,1)S(1)} %get-tuple-element.65.refs_0_), channel_id=1, source_target_pairs={{0,8},{4,12},{8,0},{12,4},{16,24},{20,28},{24,16},{28,20},{1,9},{5... | collective-permute-start | bytes 196616 | tf_op jit(solution)/shard_map/ppermute | solution.py:472
  54.8 7.4 %collective-permute-start.19 = (bf16[1,64,512]{2,1,0:T(8,128)(2,1)S(1)}, bf16[1,64,512]{2,1,0:T(8,128)(2,1)S(1)}, u32[]{:S(2)}, u32[]{:S(2)}) collective-permute-start(bf16[1,64,512]{2,1,0:T(8,128)(2,1)S(1)} %get-tuple-element.65.refs_0_), channel_id=1, source_target_pairs={{0,6},{1,7},{2,4},{3,5},{4,2},{5,3},{6,0},{7,1},{8,14},{9,15},{10,... | collective-permute-start | bytes 196616 | tf_op jit(solution)/shard_map/ppermute | solution.py:480
  56.3 6.5 %collective-permute-start.18 = (bf16[1,64,512]{2,1,0:T(8,128)(2,1)S(1)}, bf16[1,64,512]{2,1,0:T(8,128)(2,1)S(1)}, u32[]{:S(2)}, u32[]{:S(2)}) collective-permute-start(bf16[1,64,512]{2,1,0:T(8,128)(2,1)S(1)} %get-tuple-element.65.refs_0_), channel_id=1, source_target_pairs={{0,2},{1,3},{2,0},{3,1},{4,6},{5,7},{6,4},{7,5},{8,10},{9,11},{10,... | collective-permute-start | bytes 196616 | tf_op jit(solution)/shard_map/ppermute | solution.py:472
  57.2 5.6 %collective-permute-start.17 = (bf16[1,64,512]{2,1,0:T(8,128)(2,1)S(1)}, bf16[1,64,512]{2,1,0:T(8,128)(2,1)S(1)}, u32[]{:S(2)}, u32[]{:S(2)}) collective-permute-start(bf16[1,64,512]{2,1,0:T(8,128)(2,1)S(1)} %get-tuple-element.65.refs_0_), channel_id=1, source_target_pairs={{0,4},{4,0},{8,12},{12,8},{16,20},{20,16},{24,28},{28,24},{1,5},{5... | collective-permute-start | bytes 196616 | tf_op jit(solution)/shard_map/ppermute | solution.py:472
  59.2 8.8 %collective-permute-start.25 = (bf16[3,64,512]{2,1,0:T(8,128)(2,1)S(1)}, bf16[3,64,512]{2,1,0:T(8,128)(2,1)S(1)}, u32[]{:S(2)}, u32[]{:S(2)}) collective-permute-start(bf16[3,64,512]{2,1,0:T(8,128)(2,1)S(1)} %stack.18.refs_4_), channel_id=1, source_target_pairs={{0,6},{1,7},{2,4},{3,5},{4,2},{5,3},{6,0},{7,1},{8,14},{9,15},{10,... | collective-permute-start | bytes 589832 | tf_op jit(solution)/shard_map/ppermute | solution.py:480
  61.5 9.7 %collective-permute-start.24 = (bf16[3,64,512]{2,1,0:T(8,128)(2,1)S(1)}, bf16[3,64,512]{2,1,0:T(8,128)(2,1)S(1)}, u32[]{:S(2)}, u32[]{:S(2)}) collective-permute-start(bf16[3,64,512]{2,1,0:T(8,128)(2,1)S(1)} %stack.18.refs_4_), channel_id=1, source_target_pairs={{0,2},{1,3},{2,0},{3,1},{4,6},{5,7},{6,4},{7,5},{8,10},{9,11},{10,... | collective-permute-start | bytes 589832 | tf_op jit(solution)/shard_map/ppermute | solution.py:472
  62.1 9.1 %collective-permute-start.23 = (bf16[3,64,512]{2,1,0:T(8,128)(2,1)S(1)}, bf16[3,64,512]{2,1,0:T(8,128)(2,1)S(1)}, u32[]{:S(2)}, u32[]{:S(2)}) collective-permute-start(bf16[3,64,512]{2,1,0:T(8,128)(2,1)S(1)} %stack.18.refs_4_), channel_id=1, source_target_pairs={{0,4},{4,0},{8,12},{12,8},{16,20},{20,16},{24,28},{28,24},{1,5},{5... | collective-permute-start | bytes 589832 | tf_op jit(solution)/shard_map/ppermute | solution.py:472
  63.5 8.3 %collective-permute-start.26 = (bf16[4,64,512]{2,1,0:T(8,128)(2,1)}, bf16[4,64,512]{2,1,0:T(8,128)(2,1)S(1)}, u32[]{:S(2)}, u32[]{:S(2)}) collective-permute-start(bf16[4,64,512]{2,1,0:T(8,128)(2,1)} %pad_maximum_fusion), channel_id=1, source_target_pairs={{0,1},{1,0},{2,3},{3,2},{4,5},{5,4},{6,7},{7,6},{8,9},{9,8},{10,11... | collective-permute-start | bytes 786440 | tf_op jit(solution)/shard_map/ppermute | solution.py:472
  63.5 8.3 %collective-permute-start.27 = (bf16[3,64,512]{2,1,0:T(8,128)(2,1)S(1)}, bf16[3,64,512]{2,1,0:T(8,128)(2,1)S(1)}, u32[]{:S(2)}, u32[]{:S(2)}) collective-permute-start(bf16[3,64,512]{2,1,0:T(8,128)(2,1)S(1)} %stack.18.refs_4_), channel_id=1, source_target_pairs={{0,1},{1,0},{2,3},{3,2},{4,5},{5,4},{6,7},{7,6},{8,9},{9,8},{10,11... | collective-permute-start | bytes 589832 | tf_op jit(solution)/shard_map/ppermute | solution.py:472
  68.0 3.8 %collective-permute-start.30 = (bf16[3,64,512]{2,1,0:T(8,128)(2,1)S(1)}, bf16[3,64,512]{2,1,0:T(8,128)(2,1)S(1)}, u32[]{:S(2)}, u32[]{:S(2)}) collective-permute-start(bf16[3,64,512]{2,1,0:T(8,128)(2,1)S(1)} %collective-permute-done.25.refs_7_), channel_id=1, source_target_pairs={{0,1},{1,0},{2,3},{3,2},{4,5},{5,4},{6,7},{7,6},{8,9},{9,8},{10,11... | collective-permute-start | bytes 589832 | tf_op jit(solution)/shard_map/ppermute | solution.py:472
  71.2 1.6 %collective-permute-start.29 = (bf16[3,64,512]{2,1,0:T(8,128)(2,1)S(1)}, bf16[3,64,512]{2,1,0:T(8,128)(2,1)}, u32[]{:S(2)}, u32[]{:S(2)}) collective-permute-start(bf16[3,64,512]{2,1,0:T(8,128)(2,1)S(1)} %collective-permute-done.24.refs_6_), channel_id=1, source_target_pairs={{0,1},{1,0},{2,3},{3,2},{4,5},{5,4},{6,7},{7,6},{8,9},{9,8},{10,11... | collective-permute-start | bytes 589832 | tf_op jit(solution)/shard_map/ppermute | solution.py:472
  71.2 1.8 %collective-permute-start.28 = (bf16[3,64,512]{2,1,0:T(8,128)(2,1)S(1)}, bf16[3,64,512]{2,1,0:T(8,128)(2,1)}, u32[]{:S(2)}, u32[]{:S(2)}) collective-permute-start(bf16[3,64,512]{2,1,0:T(8,128)(2,1)S(1)} %collective-permute-done.23.refs_5_), channel_id=1, source_target_pairs={{0,1},{1,0},{2,3},{3,2},{4,5},{5,4},{6,7},{7,6},{8,9},{9,8},{10,11... | collective-permute-start | bytes 589832 | tf_op jit(solution)/shard_map/ppermute | solution.py:472
  83.5 2.7 %collective-permute-start.31 = (bf16[2,8,64,512]{3,2,1,0:T(8,128)(2,1)S(1)}, bf16[2,8,64,512]{3,2,1,0:T(8,128)(2,1)S(1)}, u32[]{:S(2)}, u32[]{:S(2)}) collective-permute-start(bf16[2,8,64,512]{3,2,1,0:T(8,128)(2,1)S(1)} %get-tuple-element.68), channel_id=1, source_target_pairs={{0,1},{1,0},{2,3},{3,2},{4,5},{5,4},{6,7},{7,6},{8,9},{9,8},{10,11... | collective-permute-start | bytes 3145736 | tf_op jit(solution)/shard_map/ppermute | solution.py:472
  86.4 10.3 %collective-permute-start.32 = (bf16[3,64,512]{2,1,0:T(8,128)(2,1)S(1)}, bf16[3,64,512]{2,1,0:T(8,128)(2,1)S(1)}, u32[]{:S(2)}, u32[]{:S(2)}) collective-permute-start(bf16[3,64,512]{2,1,0:T(8,128)(2,1)S(1)} %get-tuple-element.71), channel_id=1, source_target_pairs={{0,4},{4,0},{8,12},{12,8},{16,20},{20,16},{24,28},{28,24},{1,5},{5... | collective-permute-start | bytes 589832 | tf_op jit(solution)/shard_map/ppermute | solution.py:472
  87.3 11.6 %collective-permute-start.33 = (bf16[3,64,512]{2,1,0:T(8,128)(2,1)S(1)}, bf16[3,64,512]{2,1,0:T(8,128)(2,1)S(1)}, u32[]{:S(2)}, u32[]{:S(2)}) collective-permute-start(bf16[3,64,512]{2,1,0:T(8,128)(2,1)S(1)} %get-tuple-element.72), channel_id=1, source_target_pairs={{0,2},{1,3},{2,0},{3,1},{4,6},{5,7},{6,4},{7,5},{8,10},{9,11},{10,... | collective-permute-start | bytes 589832 | tf_op jit(solution)/shard_map/ppermute | solution.py:472
  88.8 10.3 %collective-permute-start.34 = (bf16[3,64,512]{2,1,0:T(8,128)(2,1)S(1)}, bf16[3,64,512]{2,1,0:T(8,128)(2,1)S(1)}, u32[]{:S(2)}, u32[]{:S(2)}) collective-permute-start(bf16[3,64,512]{2,1,0:T(8,128)(2,1)S(1)} %get-tuple-element.73), channel_id=1, source_target_pairs={{0,6},{1,7},{2,4},{3,5},{4,2},{5,3},{6,0},{7,1},{8,14},{9,15},{10,... | collective-permute-start | bytes 589832 | tf_op jit(solution)/shard_map/ppermute | solution.py:480
  89.9 11.8 %collective-permute-start.38 = (bf16[64,512]{1,0:T(8,128)(2,1)S(1)}, bf16[64,512]{1,0:T(8,128)(2,1)S(1)}, u32[]{:S(2)}, u32[]{:S(2)}) collective-permute-start(bf16[64,512]{1,0:T(8,128)(2,1)S(1)} %get-tuple-element.78), channel_id=1, source_target_pairs={{0,4},{4,0},{8,12},{12,8},{16,20},{20,16},{24,28},{28,24},{1,5},{5... | collective-permute-start | bytes 196616 | tf_op jit(solution)/shard_map/ppermute | solution.py:472
  90.8 13.4 %collective-permute-start.39 = (bf16[64,512]{1,0:T(8,128)(2,1)S(1)}, bf16[64,512]{1,0:T(8,128)(2,1)S(1)}, u32[]{:S(2)}, u32[]{:S(2)}) collective-permute-start(bf16[64,512]{1,0:T(8,128)(2,1)S(1)} %get-tuple-element.79), channel_id=1, source_target_pairs={{0,2},{1,3},{2,0},{3,1},{4,6},{5,7},{6,4},{7,5},{8,10},{9,11},{10,... | collective-permute-start | bytes 196616 | tf_op jit(solution)/shard_map/ppermute | solution.py:472
  92.3 15.6 %copy-start.4 = (f32[64,512]{1,0:T(8,128)S(1)}, f32[64,512]{1,0:T(8,128)}, u32[]{:S(2)}) copy-start(f32[64,512]{1,0:T(8,128)} %copy-done.3) | copy-start | bytes 393220
  96.7 7.5 %collective-permute-start.40 = (bf16[64,512]{1,0:T(8,128)(2,1)S(1)}, bf16[64,512]{1,0:T(8,128)(2,1)S(1)}, u32[]{:S(2)}, u32[]{:S(2)}) collective-permute-start(bf16[64,512]{1,0:T(8,128)(2,1)S(1)} %get-tuple-element.80), channel_id=1, source_target_pairs={{0,6},{1,7},{2,4},{3,5},{4,2},{5,3},{6,0},{7,1},{8,14},{9,15},{10,... | collective-permute-start | bytes 196616 | tf_op jit(solution)/shard_map/ppermute | solution.py:480
  99.1 5.1 %collective-permute-start.35 = (bf16[64,512]{1,0:T(8,128)(2,1)S(1)}, bf16[64,512]{1,0:T(8,128)(2,1)S(1)}, u32[]{:S(2)}, u32[]{:S(2)}) collective-permute-start(bf16[64,512]{1,0:T(8,128)(2,1)S(1)} %get-tuple-element.75), channel_id=1, source_target_pairs={{0,8},{4,12},{8,0},{12,4},{16,24},{20,28},{24,16},{28,20},{1,9},{5... | collective-permute-start | bytes 196616 | tf_op jit(solution)/shard_map/ppermute | solution.py:472
  99.3 6.6 %collective-permute-start.36 = (bf16[64,512]{1,0:T(8,128)(2,1)S(1)}, bf16[64,512]{1,0:T(8,128)(2,1)S(1)}, u32[]{:S(2)}, u32[]{:S(2)}) collective-permute-start(bf16[64,512]{1,0:T(8,128)(2,1)S(1)} %get-tuple-element.76), channel_id=1, source_target_pairs={{0,16},{4,20},{8,24},{12,28},{16,0},{20,4},{24,8},{28,12},{1,17},{... | collective-permute-start | bytes 196616 | tf_op jit(solution)/shard_map/ppermute | solution.py:472
  101.8 6.1 %collective-permute-start.37 = (bf16[64,512]{1,0:T(8,128)(2,1)S(1)}, bf16[64,512]{1,0:T(8,128)(2,1)S(1)}, u32[]{:S(2)}, u32[]{:S(2)}) collective-permute-start(bf16[64,512]{1,0:T(8,128)(2,1)S(1)} %get-tuple-element.77), channel_id=1, source_target_pairs={{0,24},{4,28},{8,16},{12,20},{16,8},{20,12},{24,0},{28,4},{1,25},{... | collective-permute-start | bytes 196616 | tf_op jit(solution)/shard_map/ppermute | solution.py:472
  (2 other events, 1.3 us)
